TPU v7x, 32 devices: a whole 2x2x4 slice. The times are simulated.
32 devices in a mesh: dp: 2 (over y), row: 4 (over x, core), col: 4 (over z).
Axes of the slice: x: 2, y: 2, z: 4, core: 2. Of those that a mesh axis runs over, the one named last changes fastest.
Arguments:
- block_input: bfloat16 [2, 4096, 1088], P('dp', 'col', 'row'), may hold values from -6 to 6
- cotangent: bfloat16 [2, 4096, 1088], P('dp', 'col', 'row'), may hold values from -6 to 6
- prefix_len: int32 [2], P('dp'), may hold values from 409 to 2048
- first_gain: float32 [1088], P('row'), may hold values from 0.5 to 1.5
- first_shift: float32 [1088], P('row'), may hold values from -1 to 1
- qkv_weight: bfloat16 [1088, 3264], P('row', 'col'), may hold values from -0.1875 to 0.1875
- qkv_bias: bfloat16 [3264], P('col'), may hold values from -1.5 to 1.5
- out_weight: bfloat16 [1088, 1088], P('col', 'row'), may hold values from -6 to 6
- out_bias: float32 [1088], P('row'), may hold values from -1.5 to 1.5
- second_gain: float32 [1088], P('row'), may hold values from 0.5 to 1.5
- second_shift: float32 [1088], P('row'), may hold values from -1 to 1
- up_weight: bfloat16 [1088, 4352], P('row', 'col'), may hold values from -0.1875 to 0.1875
- up_bias: bfloat16 [4352], P('col'), may hold values from -1.5 to 1.5
- down_weight: bfloat16 [4352, 1088], P('col', 'row'), may hold values from -0.09375 to 0.09375
- down_bias: float32 [1088], P('row'), may hold values from -1.5 to 1.5
Outputs:
- block_output: bfloat16 [2, 4096, 1088], P('dp', 'col', 'row')
- input_grad: float32 [2, 4096, 1088], P('dp', 'col', 'row')
- first_gain_grad: float32 [1088], P('row')
- first_shift_grad: float32 [1088], P('row')
- qkv_weight_grad: float32 [1088, 3264], P('row', 'col')
- qkv_bias_grad: float32 [3264], P('col')
- out_weight_grad: float32 [1088, 1088], P('col', 'row')
- out_bias_grad: float32 [1088], P('row')
- second_gain_grad: float32 [1088], P('row')
- second_shift_grad: float32 [1088], P('row')
- up_weight_grad: float32 [1088, 4352], P('row', 'col')
- up_bias_grad: float32 [4352], P('col')
- down_weight_grad: float32 [4352, 1088], P('col', 'row')
- down_bias_grad: float32 [1088], P('row')
All inputs are finite; a program needn't handle non-finite values.
Results may differ from a plain program's by a relative error of at most 0.029.
Values may be sent and summed in bfloat16 or wider, within the bound.
No kernel may reach another device: no remote copies, remote signals or barrier semaphores. Data moves between devices by JAX's collectives and lax.ppermute only.
A program may use at most 192 MiB of HBM per device.

v0:
```python
from functools import partial

import jax
import jax.numpy as jnp
from jax import lax
from jax.sharding import PartitionSpec as P

HEADS = 17
HDIM = 64
D = 1088


def positions(first_row, piece_len, tok_b, tok_a, col_total):
    flat_rows = first_row + jnp.arange(piece_len, dtype=jnp.int32)
    shard_no = flat_rows // tok_b
    return shard_no % col_total * tok_a + shard_no // col_total * tok_b + flat_rows % tok_b


def over_blocks(folded, pieces, step_fn):
    piece_len = pieces[0].shape[0]
    block_len = 512

    def one_block(block_no, running):
        offset = block_no * block_len
        sliced = tuple(
            (lax.dynamic_slice_in_dim(member, offset, block_len, 0) for member in pieces)
        )
        return step_fn(running, sliced, offset)

    return lax.fori_loop(0, piece_len // block_len, one_block, folded)


def head_scores(left, right, scale_factor):
    return (
        jnp.einsum("qhd,khd->hqk", left, right, preferred_element_type=jnp.float32) * scale_factor
    )


def normalize(values, norm_gain, norm_shift):
    width_all = values.shape[1] * lax.axis_size("row")
    row_sums = lax.psum((jnp.sum(values, 1), jnp.sum(values * values, 1)), "row")
    row_mean = row_sums[0] / width_all
    variance = row_sums[1] / width_all - row_mean * row_mean
    inv_std = lax.rsqrt(variance + 1e-05)
    centred = (values - row_mean[:, None]) * inv_std[:, None]
    return (centred * norm_gain + norm_shift, centred, inv_std)


def norm_back(d_normed, centred, inv_std, norm_gain):
    width_all = d_normed.shape[1] * lax.axis_size("row")
    scaled = d_normed * norm_gain
    row_sums = lax.psum((jnp.sum(scaled, 1), jnp.sum(scaled * centred, 1)), "row")
    d_values = inv_std[:, None] * (
        scaled - row_sums[0][:, None] / width_all - centred * row_sums[1][:, None] / width_all
    )
    return (d_values, jnp.sum(d_normed * centred, 0), jnp.sum(d_normed, 0))


def row_partials(term_fn, tok_b):
    return lax.psum_scatter(
        term_fn(jnp.int32(0), tok_b * lax.axis_size("row")).astype(jnp.bfloat16),
        "row",
        scatter_dimension=0,
        tiled=True,
    ).astype(jnp.float32)


def rows_gather(values):
    return lax.all_gather(values, "row", axis=0, tiled=True)


def row_product(normed_low, weight, tok_b):

    def term_fn(first_row, row_count):
        return jnp.dot(normed_low, weight, preferred_element_type=jnp.float32)

    return row_partials(term_fn, tok_b)


def back_product(grad_low, weight, tok_b):

    def term_fn(first_row, row_count):
        return lax.dot_general(
            grad_low, weight, (((1,), (1,)), ((), ())), preferred_element_type=jnp.float32
        )

    return row_partials(term_fn, tok_b)


def fold_back(grad_rows, normed_low, weight_full):
    piece = lax.all_gather(grad_rows, "row", axis=0, tiled=True)
    contrib = lax.dot_general(
        piece, weight_full, (((1,), (1,)), ((), ())), preferred_element_type=jnp.float32
    )
    d_weight = lax.dot_general(
        normed_low, piece, (((0,), (0,)), ((), ())), preferred_element_type=jnp.float32
    )
    return (contrib, d_weight, jnp.sum(piece.astype(jnp.float32), 0))


def scatter_columns(gradients):
    return (
        lax.psum_scatter(
            gradients[0].astype(jnp.bfloat16), "col", scatter_dimension=1, tiled=True
        ).astype(jnp.float32),
        lax.psum_scatter(
            gradients[1].astype(jnp.bfloat16), "col", scatter_dimension=0, tiled=True
        ).astype(jnp.float32),
        lax.psum_scatter(
            gradients[2].astype(jnp.bfloat16), "col", scatter_dimension=0, tiled=True
        ).astype(jnp.float32),
        lax.psum_scatter(
            gradients[3].astype(jnp.bfloat16), "col", scatter_dimension=1, tiled=True
        ).astype(jnp.float32),
        lax.psum_scatter(
            gradients[4].astype(jnp.bfloat16), "col", scatter_dimension=0, tiled=True
        ).astype(jnp.float32),
        lax.psum_scatter(
            gradients[5].astype(jnp.bfloat16), "col", scatter_dimension=0, tiled=True
        ).astype(jnp.float32),
    )


def sum_over_data(gradients):
    return (
        lax.psum(gradients[0].astype(jnp.bfloat16), "dp").astype(jnp.float32),
        lax.psum(gradients[1].astype(jnp.bfloat16), "dp").astype(jnp.float32),
        lax.psum(gradients[2].astype(jnp.bfloat16), "dp").astype(jnp.float32),
        lax.psum(gradients[3].astype(jnp.bfloat16), "dp").astype(jnp.float32),
        lax.psum(gradients[4].astype(jnp.bfloat16), "dp").astype(jnp.float32),
        lax.psum(gradients[5].astype(jnp.bfloat16), "dp").astype(jnp.float32),
    )


def shards(
    block_input,
    cotangent,
    prefix_len,
    first_gain,
    first_shift,
    qkv_weight,
    qkv_bias,
    out_weight,
    out_bias,
    second_gain,
    second_shift,
    up_weight,
    up_bias,
    down_weight,
    down_bias,
):
    row_total = lax.axis_size("row")
    col_total = lax.axis_size("col")
    tok_a = block_input.shape[1]
    tok_b = tok_a // row_total
    scale_factor = HDIM ** (-0.5)
    gathered = (
        lax.all_gather(qkv_weight, "col", axis=1, tiled=True),
        lax.all_gather(qkv_bias, "col", axis=0, tiled=True),
        lax.all_gather(out_weight, "col", axis=0, tiled=True),
        lax.all_gather(up_weight, "col", axis=1, tiled=True),
        lax.all_gather(up_bias, "col", axis=0, tiled=True),
        lax.all_gather(down_weight, "col", axis=0, tiled=True),
    )
    qkv_full, qkv_bias_full, out_full, up_full, up_bias_full, down_full = gathered
    residual = block_input[0].astype(jnp.float32)
    prefix_end = prefix_len[0]
    own_pos = (
        lax.axis_index("col") * tok_a
        + lax.axis_index("row") * tok_b
        + jnp.arange(tok_b, dtype=jnp.int32)
    )

    def visible(key_pos, query_pos):
        return (key_pos[None, :] < prefix_end) | (key_pos[None, :] <= query_pos[:, None])

    def piece_pos(first_row, piece_len):
        return positions(first_row, piece_len, tok_b, tok_a, col_total)

    normed_one, centred_one, inv_one = normalize(residual, first_gain, first_shift)
    normed_one_low = normed_one.astype(jnp.bfloat16)
    mixed_qkv = (
        row_product(normed_one_low, qkv_full, tok_b) + qkv_bias_full.astype(jnp.float32)
    ).astype(jnp.bfloat16)
    query_rows = mixed_qkv[:, :D]
    key_rows = mixed_qkv[:, D : 2 * D]
    value_rows = mixed_qkv[:, 2 * D :]
    own_query = query_rows.reshape(tok_b, HEADS, HDIM)
    own_key = key_rows.reshape(tok_b, HEADS, HDIM)
    own_value = value_rows.reshape(tok_b, HEADS, HDIM)

    def max_step(running, sliced, first_row):
        key_block = sliced[0]
        allowed = visible(piece_pos(first_row, key_block.shape[0]), own_pos)
        scores = jnp.where(
            allowed[None],
            head_scores(own_query, key_block.reshape(-1, HEADS, HDIM), scale_factor),
            -1e30,
        )
        new_max = jnp.maximum(running[0], jnp.max(scores, 2))
        new_total = running[1] * jnp.exp(running[0] - new_max) + jnp.sum(
            jnp.where(allowed[None], jnp.exp(scores - new_max[:, :, None]), 0.0), 2
        )
        return (new_max, new_total)

    start_max = (
        jnp.full((HEADS, tok_b), -1e30, jnp.float32),
        jnp.zeros((HEADS, tok_b), jnp.float32),
    )
    run_max, run_total = over_blocks(
        start_max, (lax.all_gather(key_rows, ("row", "col"), axis=0, tiled=True),), max_step
    )
    log_total = run_max + jnp.log(run_total)

    def value_step(running, sliced, first_row):
        key_block, value_block = sliced
        allowed = visible(piece_pos(first_row, key_block.shape[0]), own_pos)
        scores = head_scores(own_query, key_block.reshape(-1, HEADS, HDIM), scale_factor)
        attn_probs = jnp.where(allowed[None], jnp.exp(scores - log_total[:, :, None]), 0.0).astype(
            jnp.bfloat16
        )
        return running + jnp.einsum(
            "hqk,khd->qhd",
            attn_probs,
            value_block.reshape(-1, HEADS, HDIM),
            preferred_element_type=jnp.float32,
        )

    attn_acc = over_blocks(
        jnp.zeros((tok_b, HEADS, HDIM), jnp.float32),
        (
            lax.all_gather(key_rows, ("row", "col"), axis=0, tiled=True),
            lax.all_gather(value_rows, ("row", "col"), axis=0, tiled=True),
        ),
        value_step,
    )
    attn_float = attn_acc.reshape(tok_b, D)
    attn_all = rows_gather(attn_float.astype(jnp.bfloat16))
    residual_two = (
        residual + jnp.dot(attn_all, out_full, preferred_element_type=jnp.float32) + out_bias
    )
    normed_two, centred_two, inv_two = normalize(residual_two, second_gain, second_shift)
    normed_two_low = normed_two.astype(jnp.bfloat16)
    hidden = row_product(normed_two_low, up_full, tok_b) + up_bias_full.astype(jnp.float32)
    active_all = rows_gather(jax.nn.gelu(hidden, approximate=False).astype(jnp.bfloat16))
    block_output = (
        residual_two
        + jnp.dot(active_all, down_full, preferred_element_type=jnp.float32)
        + down_bias
    ).astype(jnp.bfloat16)
    cot_low = cotangent[0]
    cot_float = cot_low.astype(jnp.float32)
    down_grad = lax.dot_general(
        active_all, cot_low, (((0,), (0,)), ((), ())), preferred_element_type=jnp.float32
    )
    down_bias_grad = jnp.sum(cot_float, 0)
    d_active = back_product(cot_low, down_full, tok_b)
    gelu_back = jax.vjp(partial(jax.nn.gelu, approximate=False), hidden)[1]
    d_hidden_low = gelu_back(d_active)[0].astype(jnp.bfloat16)
    d_norm_two, up_grad, up_bias_grad = fold_back(d_hidden_low, normed_two_low, up_full)
    d_part_two, second_gain_grad, second_shift_grad = norm_back(
        d_norm_two, centred_two, inv_two, second_gain
    )
    d_residual = cot_float + d_part_two
    branch_low = d_residual.astype(jnp.bfloat16)
    out_grad = lax.dot_general(
        attn_all, branch_low, (((0,), (0,)), ((), ())), preferred_element_type=jnp.float32
    )
    out_bias_grad = jnp.sum(branch_low.astype(jnp.float32), 0)
    d_attn_low = back_product(branch_low, out_full, tok_b).astype(jnp.bfloat16)
    delta_rows = jnp.sum(
        (d_attn_low.astype(jnp.float32) * attn_float).reshape(tok_b, HEADS, HDIM), 2
    )
    lse_rows = log_total.T
    all_lse, all_delta = (
        lax.all_gather(lse_rows, ("row", "col"), axis=0, tiled=True),
        lax.all_gather(delta_rows, ("row", "col"), axis=0, tiled=True),
    )
    own_grad = d_attn_low.reshape(tok_b, HEADS, HDIM)

    def back_step(running, sliced, first_row):
        query_p, key_p, value_p, grad_p = sliced
        piece_len = query_p.shape[0]
        pos_piece = piece_pos(first_row, piece_len)
        lse_piece = lax.dynamic_slice_in_dim(all_lse, first_row, piece_len, 0)
        delta_piece = lax.dynamic_slice_in_dim(all_delta, first_row, piece_len, 0)
        query_p3 = query_p.reshape(piece_len, HEADS, HDIM)
        key_p3 = key_p.reshape(piece_len, HEADS, HDIM)
        value_p3 = value_p.reshape(piece_len, HEADS, HDIM)
        grad_p3 = grad_p.reshape(piece_len, HEADS, HDIM)
        allowed_own = visible(pos_piece, own_pos)
        allowed_far = visible(own_pos, pos_piece)
        scores = head_scores(own_query, key_p3, scale_factor)
        attn_probs = jnp.where(allowed_own[None], jnp.exp(scores - log_total[:, :, None]), 0.0)
        d_probs = jnp.einsum("qhd,khd->hqk", own_grad, value_p3, preferred_element_type=jnp.float32)
        d_scores = (attn_probs * (d_probs - delta_rows.T[:, :, None])).astype(jnp.bfloat16)
        new_query = (
            running[0]
            + jnp.einsum("hqk,khd->qhd", d_scores, key_p3, preferred_element_type=jnp.float32)
            * scale_factor
        )
        scores = head_scores(query_p3, own_key, scale_factor)
        attn_probs = jnp.where(allowed_far[None], jnp.exp(scores - lse_piece.T[:, :, None]), 0.0)
        d_value = running[2] + jnp.einsum(
            "hqk,qhd->khd",
            attn_probs.astype(jnp.bfloat16),
            grad_p3,
            preferred_element_type=jnp.float32,
        )
        d_probs = jnp.einsum("qhd,khd->hqk", grad_p3, own_value, preferred_element_type=jnp.float32)
        d_scores = (attn_probs * (d_probs - delta_piece.T[:, :, None])).astype(jnp.bfloat16)
        d_key = (
            running[1]
            + jnp.einsum("hqk,qhd->khd", d_scores, query_p3, preferred_element_type=jnp.float32)
            * scale_factor
        )
        return (new_query, d_key, d_value)

    zero_heads = jnp.zeros((tok_b, HEADS, HDIM), jnp.float32)
    d_query, d_key, d_value = over_blocks(
        (zero_heads, zero_heads, zero_heads),
        (
            lax.all_gather(query_rows, ("row", "col"), axis=0, tiled=True),
            lax.all_gather(key_rows, ("row", "col"), axis=0, tiled=True),
            lax.all_gather(value_rows, ("row", "col"), axis=0, tiled=True),
            lax.all_gather(d_attn_low, ("row", "col"), axis=0, tiled=True),
        ),
        back_step,
    )
    d_mixed_low = jnp.concatenate(
        [d_query.reshape(tok_b, D), d_key.reshape(tok_b, D), d_value.reshape(tok_b, D)], 1
    ).astype(jnp.bfloat16)
    d_norm_one, qkv_grad, qkv_bias_grad = fold_back(d_mixed_low, normed_one_low, qkv_full)
    d_part_one, first_gain_grad, first_shift_grad = norm_back(
        d_norm_one, centred_one, inv_one, first_gain
    )
    input_grad = d_residual + d_part_one
    col_ready = (qkv_grad, qkv_bias_grad, out_grad, up_grad, up_bias_grad, down_grad)
    reduced = scatter_columns(sum_over_data(col_ready))
    small = lax.psum(
        (
            first_gain_grad,
            first_shift_grad,
            out_bias_grad,
            second_gain_grad,
            second_shift_grad,
            down_bias_grad,
        ),
        ("dp", "col"),
    )
    return (
        block_output[None],
        input_grad[None],
        small[0],
        small[1],
        reduced[0],
        reduced[1],
        reduced[2],
        small[2],
        small[3],
        small[4],
        reduced[3],
        reduced[4],
        reduced[5],
        small[5],
    )


def solution(mesh):
    in_specs = (
        P("dp", "col", "row"),
        P("dp", "col", "row"),
        P("dp"),
        P("row"),
        P("row"),
        P("row", "col"),
        P("col"),
        P("col", "row"),
        P("row"),
        P("row"),
        P("row"),
        P("row", "col"),
        P("col"),
        P("col", "row"),
        P("row"),
    )
    out_specs = (
        P("dp", "col", "row"),
        P("dp", "col", "row"),
        P("row"),
        P("row"),
        P("row", "col"),
        P("col"),
        P("col", "row"),
        P("row"),
        P("row"),
        P("row"),
        P("row", "col"),
        P("col"),
        P("col", "row"),
        P("row"),
    )
    return jax.shard_map(shards, mesh=mesh, in_specs=in_specs, out_specs=out_specs, check_vma=False)
```

profile of v0, /device:TPU:0, one launch (start us, length us, event | category | flops | bytes accessed | tf_op | source)
XLA Modules:
  0.0 1603.0 jit_solution(11520335814510918020)
XLA Ops:
  10.3 8.5 all-reduce.8
  18.8 36.8 %all-gather.31.cloned.1.call-done = bf16[4,816,272]{1,2,0:T(8,128)(2,1)} async-done(((bf16[1,816,272]{1,2,0:T(8,128)(2,1)}), bf16[4,816,272]{1,2,0:T(8,128)(2,1)}) %all-gather.31.cloned.1.call-update) | async-done | bytes 1775632 | tf_op jit(solution)/shard_map/all_gather | solution.py:158
  60.3 7.4 convolution_convert_fusion.2
  70.8 16.9 %all-reduce.10 = (bf16[3264]{0:T(1024)(128)(2,1)S(1)}, bf16[4352]{0:T(1024)(128)(2,1)S(1)}) all-reduce(bf16[3264]{0:T(1024)(128)(2,1)S(1)} %dynamic-update-slice, bf16[4352]{0:T(1024)(128)(2,1)S(1)} %dynamic-update-slice.1), channel_id=1, replica_groups=mesh['dp'=2,'row'=4,'col'=4] {'col'}, use_global_device_ids=true, to_apply=%add | all-reduce | flops 7616 | bytes 30464
  87.7 40.0 %reduce-scatter.15.cloned.1.call-done = bf16[256,3264]{0,1:T(8,128)(2,1)} async-done(((bf16[1024,3264]{0,1:T(8,128)(2,1)}), bf16[256,3264]{0,1:T(8,128)(2,1)}) %reduce-scatter.15.cloned.1.call-update) | async-done | bytes 1671184 | tf_op jit(solution)/shard_map/reduce_scatter | solution.py:60
  132.7 79.4 %all-gather.17.cloned.1.call-done = bf16[4096,1088]{0,1:T(8,128)(2,1)} async-done(((bf16[256,1088]{0,1:T(8,128)(2,1)}), bf16[4096,1088]{0,1:T(8,128)(2,1)}) %all-gather.17.cloned.1.call-update) | async-done | bytes 8912912 | tf_op jit(solution)/shard_map/all_gather | solution.py:232
  212.1 48.2 %while.57 = (s32[]{:T(128)}, f32[17,256]{1,0:T(8,128)S(1)}, f32[17,256]{1,0:T(8,128)S(1)}, s32[]{:T(128)}, bf16[4096,1088]{0,1:T(8,128)(2,1)}, /*index=5*/bf16[2...) while((s32[]{:T(128)}, f32[17,256]{1,0:T(8,128)S(1)}, ...), condition=%wide.region_8.9_spmd.clone, body=%wide.region_5.8_spmd.clone.sunk | while | flops 303367168 | bytes 22352064 | solution.py:30
  260.4 33.9 %all-gather.15.cloned.1.call-done = bf16[4096,1088]{0,1:T(8,128)(2,1)} async-done(((bf16[256,1088]{0,1:T(8,128)(2,1)}), bf16[4096,1088]{0,1:T(8,128)(2,1)}) %all-gather.15.cloned.1.call-update) | async-done | bytes 8912912 | tf_op jit(solution)/shard_map/all_gather | solution.py:233
  294.2 59.3 %while.58 = (s32[]{:T(128)}, f32[256,17,64]{0,2,1:T(8,128)}, bf16[4096,1088]{0,1:T(8,128)(2,1)}, s32[]{:T(128)}, bf16[4096,1088]{0,1:T(8,128)(2,1)}, /*index=5*/...) while((s32[]{:T(128)}, f32[256,17,64]{0,2,1:T(8,128)}, ...), condition=%wide.region_10.11_spmd.clone, body=%wide.region_9.10_spmd.clone.sunk | while | flops 580202240 | bytes 9756873 | solution.py:30
  362.0 10.2 convolution_convert_fusion
  373.0 31.8 %all_gather.56 = bf16[1088,272]{1,0:T(8,128)(2,1)} all-gather(bf16[272,272]{1,0:T(8,128)(2,1)S(1)} %copy-done.19), channel_id=1, replica_groups=mesh['dp'=2,'row'=4,'col'=4] {'col'}, dimensions={0}, use_global_device_ids=true | all-gather | bytes 739840 | tf_op jit(solution)/shard_map/all_gather | solution.py:160
  404.8 8.5 all-gather.33.cloned.1.call-done
  419.0 19.0 %all-gather.19.cloned.1.call-done = bf16[1024,1088]{0,1:T(8,128)(2,1)} async-done(((bf16[256,1088]{0,1:T(8,128)(2,1)}), bf16[1024,1088]{0,1:T(8,128)(2,1)}) %all-gather.19.cloned.1.call-update) | async-done | bytes 2228240 | tf_op jit(solution)/shard_map/all_gather | solution.py:69
  441.8 6.4 all-reduce.7
  448.3 9.3 convolution_convert_fusion.1
  457.6 58.2 %reduce-scatter.19.cloned.1.call-done = bf16[256,4352]{1,0:T(8,128)(2,1)} async-done(((bf16[1024,4352]{1,0:T(8,128)(2,1)}), bf16[256,4352]{1,0:T(8,128)(2,1)}) %reduce-scatter.19.cloned.1.call-update) | async-done | bytes 2228240 | tf_op jit(solution)/shard_map/reduce_scatter | solution.py:60
  515.8 77.9 %reduce-scatter.17.cloned.1.call-done = bf16[256,4352]{1,0:T(8,128)(2,1)} async-done(((bf16[1024,4352]{1,0:T(8,128)(2,1)}), bf16[256,4352]{1,0:T(8,128)(2,1)}) %reduce-scatter.17.cloned.1.call-update) | async-done | bytes 2228240 | tf_op jit(solution)/shard_map/reduce_scatter | solution.py:60
  593.7 13.2 fusion.89
  607.0 61.4 %all-gather.23.cloned.1.call-done = bf16[1024,4352]{1,0:T(8,128)(2,1)} async-done(((bf16[256,4352]{1,0:T(8,128)(2,1)}), bf16[1024,4352]{1,0:T(8,128)(2,1)}) %all-gather.23.cloned.1.call-update) | async-done | bytes 8912912 | tf_op jit(solution)/shard_map/all_gather | solution.py:91
  668.4 7.9 multiply_reduce_fusion
  676.3 6.1 all-reduce.6
  689.5 32.8 %reduce-scatter.21.cloned.1.call-done = bf16[256,1088]{0,1:T(8,128)(2,1)} async-done(((bf16[1024,1088]{0,1:T(8,128)(2,1)}), bf16[256,1088]{0,1:T(8,128)(2,1)}) %reduce-scatter.21.cloned.1.call-update) | async-done | bytes 557072 | tf_op jit(solution)/shard_map/reduce_scatter | solution.py:60
  722.4 41.3 %all_gather.63 = f32[4096,17]{0,1:T(8,128)} all-gather(f32[256,17]{0,1:T(8,128)S(1)} %bitcast.279), channel_id=1, replica_groups=mesh['dp'=2,'row'=4,'col'=4] {'row','col'}, dimensions={0}, use_global_device_ids=true | all-gather | bytes 295936 | tf_op jit(solution)/shard_map/all_gather | solution.py:276
  763.8 5.0 multiply_convert_fusion.8
  772.0 48.0 %all_gather.65 = f32[4096,17]{0,1:T(8,128)} all-gather(f32[256,17]{0,1:T(8,128)} %reduce_sum.182), channel_id=1, replica_groups=mesh['dp'=2,'row'=4,'col'=4] {'row','col'}, dimensions={0}, use_global_device_ids=true | all-gather | bytes 295936 | tf_op jit(solution)/shard_map/all_gather | solution.py:277
  820.0 76.7 %all-gather.27.cloned.1.call-done = bf16[4096,1088]{0,1:T(8,128)(2,1)} async-done(((bf16[256,1088]{0,1:T(8,128)(2,1)}), bf16[4096,1088]{0,1:T(8,128)(2,1)}) %all-gather.27.cloned.1.call-update) | async-done | bytes 8912912 | tf_op jit(solution)/shard_map/all_gather | solution.py:326
  896.8 344.6 %while.59 = (s32[]{:T(128)}, f32[256,17,64]{0,2,1:T(8,128)}, f32[256,17,64]{0,2,1:T(8,128)}, f32[256,17,64]{0,2,1:T(8,128)}, bf16[4096,1088]{0,1:T(8,128)(2,1)},...) while((s32[]{:T(128)}, f32[256,17,64]{0,2,1:T(8,128)}, ...), condition=%wide.region_24.25_spmd.clone, body=%wide.region_23.24_spmd.clone.sunk | while | flops 2034938112 | bytes 75590472 | solution.py:30
  911.5 9.1 fusion.227
  920.7 6.2 fusion.228
  931.6 8.1 fusion.225
  953.8 9.5 fusion.227
  963.3 6.4 fusion.228
  974.4 8.4 fusion.225
  996.9 9.4 fusion.227
  1006.4 6.4 fusion.228
  1017.5 8.4 fusion.225
  1040.0 9.4 fusion.227
  1049.4 6.4 fusion.228
  1060.6 8.4 fusion.225
  1083.1 9.4 fusion.227
  1092.5 6.4 fusion.228
  1103.7 8.4 fusion.225
  1126.2 9.4 fusion.227
  1135.6 6.4 fusion.228
  1146.8 8.4 fusion.225
  1169.3 9.4 fusion.227
  1178.7 6.4 fusion.228
  1189.9 8.4 fusion.225
  1212.4 9.4 fusion.227
  1221.8 6.4 fusion.228
  1233.0 8.4 fusion.225
  1245.9 6.8 convolution_convert_fusion.4
  1255.8 6.5 convolution_convert_fusion.3
  1265.4 28.9 %all-gather.29.cloned.1.call-done = bf16[1024,3264]{0,1:T(8,128)(2,1)} async-done(((bf16[256,3264]{0,1:T(8,128)(2,1)}), bf16[1024,3264]{0,1:T(8,128)(2,1)}) %all-gather.29.cloned.1.call-update) | async-done | bytes 6684688 | tf_op jit(solution)/shard_map/all_gather | solution.py:91
  1294.3 5.1 convolution_convert_fusion.5
  1313.9 45.9 %reduce-scatter.27.cloned.1.call-done = bf16[1088,272]{1,0:T(8,128)(2,1)} async-done(((bf16[4352,272]{1,0:T(8,128)(2,1)}), bf16[1088,272]{1,0:T(8,128)(2,1)}) %reduce-scatter.27.cloned.1.call-update) | async-done | bytes 591888
  1362.1 63.5 %reduce-scatter.29.cloned.1.call-done = bf16[1088,272]{1,0:T(8,128)(2,1)} async-done(((bf16[4352,272]{1,0:T(8,128)(2,1)}), bf16[1088,272]{1,0:T(8,128)(2,1)}) %reduce-scatter.29.cloned.1.call-update) | async-done | bytes 591888
  1427.9 50.6 %reduce-scatter.25.cloned.1.call-done = bf16[816,272]{1,0:T(8,128)(2,1)} async-done(((bf16[3264,272]{1,0:T(8,128)(2,1)}), bf16[816,272]{1,0:T(8,128)(2,1)}) %reduce-scatter.25.cloned.1.call-update) | async-done | bytes 443920
  1480.5 24.6 %reduce-scatter.23.cloned.1.call-done = bf16[272,272]{1,0:T(8,128)(2,1)} async-done(((bf16[1088,272]{1,0:T(8,128)(2,1)}), bf16[272,272]{1,0:T(8,128)(2,1)}) %reduce-scatter.23.cloned.1.call-update) | async-done | bytes 147984 | tf_op jit(solution)/shard_map/reduce_scatter | solution.py:109
  1505.2 7.7 fusion.109
  1516.9 17.7 %all-reduce.9 = (bf16[3264]{0:T(1024)(128)(2,1)S(1)}, bf16[4352]{0:T(1024)(128)(2,1)S(1)}) all-reduce(bf16[3264]{0:T(1024)(128)(2,1)S(1)} %reduce_sum.187, bf16[4352]{0:T(1024)(128)(2,1)S(1)} %reduce_sum.191), channel_id=7, replica_groups=mesh['dp'=2,'row'=4,'col'=4] {'col'}, use_global_device_ids=true, to_apply=%region_37.38.clone | all-reduce | flops 7616 | bytes 30464
  1541.0 6.4 fusion.123
  1547.4 34.0 %all-reduce.4 = (f32[272]{0:T(512)}, f32[272]{0:T(512)}, f32[272]{0:T(512)}, f32[272]{0:T(512)}, f32[272]{0:T(512)}, /*index=5*/f32[272]{0:T(512)}) all-reduce(f32[272]{0:T(512)S(1)} %get-tuple-element.1124, f32[272]{0:T(512)S(1)} %get-tuple-element.1129, ...), channel_id=1, replica_groups=mesh['dp'=2,'row'=4,'col'=4] {'dp','col'}, use_global_device_ids=true, to_apply=%region_30.31 | all-reduce | flops 1632 | bytes 13056 | tf_op jit(solution)/shard_map/psum | solution.py:340
  1581.4 5.7 all-reduce.5
  (415 shorter events, 351.0 us)
Async XLA Ops:
  7.2 48.4 %all-gather.31.cloned.1.call-start = ((), (), s32[]{:S(2)}) async-start(), calls=%async_computation.21 | async-start | bytes 2437120 | tf_op jit(solution)/shard_map/all_gather | solution.py:158
  7.9 119.8 %reduce-scatter.15.cloned.1.call-start = ((), (), s32[]{:S(2)}) async-start(), calls=%async_computation.8 | async-start | bytes 8355840 | tf_op jit(solution)/shard_map/reduce_scatter | solution.py:60
  18.8 41.4 %copy-start.20 = (f32[1024]{0:T(1024)}, f32[1024]{0:T(1024)S(1)}, u32[]{:S(2)}) copy-start(f32[1024]{0:T(1024)S(1)} %get-tuple-element.1242) | copy-start | bytes 12292
  18.8 41.4 %copy-start.22 = (f32[1024]{0:T(1024)}, f32[1024]{0:T(1024)S(1)}, u32[]{:S(2)}) copy-start(f32[1024]{0:T(1024)S(1)} %get-tuple-element.1243) | copy-start | bytes 12292
  57.9 2.4 copy-start.5
  57.9 2.4 copy-start.27
  57.9 2.3 copy-start.39
  67.7 2.6 copy-start.33
  67.7 2.8 copy-start.26
  67.7 144.4 %all-gather.17.cloned.1.call-start = ((), (), s32[]{:S(2)}) async-start(), calls=%async_computation.10 | async-start | bytes 9469952 | tf_op jit(solution)/shard_map/all_gather | solution.py:232
  130.7 163.5 %all-gather.15.cloned.1.call-start = ((), (), s32[]{:S(2)}) async-start(), calls=%async_computation.9 | async-start | bytes 9469952 | tf_op jit(solution)/shard_map/all_gather | solution.py:233
  131.3 225.0 %all-gather.35.cloned.1.call-start = ((), (), s32[]{:S(2)}) async-start(), calls=%async_computation.23 | async-start | bytes 3133440 | tf_op jit(solution)/shard_map/all_gather | solution.py:163
  131.9 281.4 %all-gather.33.cloned.1.call-start = ((), (), s32[]{:S(2)}) async-start(), calls=%async_computation.22 | async-start | bytes 3133440 | tf_op jit(solution)/shard_map/all_gather | solution.py:161
  132.5 305.5 %all-gather.19.cloned.1.call-start = ((), (), s32[]{:S(2)}) async-start(), calls=%async_computation.11 | async-start | bytes 2785280 | tf_op jit(solution)/shard_map/all_gather | solution.py:69
  353.6 5.4 copy-start
  356.0 159.8 %reduce-scatter.19.cloned.1.call-start = ((), (), s32[]{:S(2)}) async-start(), calls=%async_computation.14 | async-start | bytes 11141120 | tf_op jit(solution)/shard_map/reduce_scatter | solution.py:60
  372.1 221.6 %reduce-scatter.17.cloned.1.call-start = ((), (), s32[]{:S(2)}) async-start(), calls=%async_computation.12 | async-start | bytes 11141120 | tf_op jit(solution)/shard_map/reduce_scatter | solution.py:60
  416.0 22.0 %copy-start.6 = (bf16[1,1024,272]{1,2,0:T(8,128)(2,1)S(1)}, bf16[1,1024,272]{1,2,0:T(8,128)(2,1)}, u32[]{:S(2)}) copy-start(bf16[1,1024,272]{1,2,0:T(8,128)(2,1)} %param.21) | copy-start | bytes 1671172
  416.0 22.0 %copy-start.36 = (f32[272]{0:T(512)S(1)}, f32[272]{0:T(512)}, u32[]{:S(2)}) copy-start(f32[272]{0:T(512)} %param.29) | copy-start | bytes 3268
  418.9 29.3 %copy-start.11 = (bf16[4352,272]{0,1:T(8,128)(2,1)S(1)}, bf16[4352,272]{0,1:T(8,128)(2,1)}, u32[]{:S(2)}) copy-start(bf16[4352,272]{0,1:T(8,128)(2,1)} %reshape.587) | copy-start | bytes 7102468
  419.0 29.3 %copy-start.29 = (f32[272]{0:T(512)S(1)}, f32[272]{0:T(512)}, u32[]{:S(2)}) copy-start(f32[272]{0:T(512)} %param.30) | copy-start | bytes 3268
  419.0 29.3 %copy-start.37 = (f32[272]{0:T(512)S(1)}, f32[272]{0:T(512)}, u32[]{:S(2)}) copy-start(f32[272]{0:T(512)} %param.31) | copy-start | bytes 3268
  457.5 210.9 %all-gather.23.cloned.1.call-start = ((), (), s32[]{:S(2)}) async-start(), calls=%async_computation.15 | async-start | bytes 11141120 | tf_op jit(solution)/shard_map/all_gather | solution.py:91
  607.0 61.5 %copy-start.13 = (f32[1024,272]{0,1:T(8,128)S(1)}, f32[1024,272]{0,1:T(8,128)}, u32[]{:S(2)}) copy-start(f32[1024,272]{0,1:T(8,128)} %get-tuple-element.1246) | copy-start | bytes 3342340
  607.0 61.5 %copy-start.30 = (f32[272]{0:T(512)S(1)}, f32[272]{0:T(512)}, u32[]{:S(2)}) copy-start(f32[272]{0:T(512)} %param.30) | copy-start | bytes 3268
  607.0 115.3 %reduce-scatter.21.cloned.1.call-start = ((), (), s32[]{:S(2)}) async-start(), calls=%async_computation.16 | async-start | bytes 2785280 | tf_op jit(solution)/shard_map/reduce_scatter | solution.py:60
  676.3 9.9 copy-start.16
  688.8 74.9 %copy-start.4 = (bf16[256,4352]{1,0:T(8,128)(2,1)S(1)}, bf16[256,4352]{1,0:T(8,128)(2,1)}, u32[]{:S(2)}) copy-start(bf16[256,4352]{1,0:T(8,128)(2,1)} %reduce-scatter.17.cloned.1.call-done) | copy-start | bytes 6684676
  688.9 131.1 %all-gather.25.cloned.1.call-start = ((), (), s32[]{:S(2)}) async-start(), calls=%async_computation.17 | async-start | bytes 9469952 | tf_op jit(solution)/shard_map/all_gather | solution.py:323
  689.4 207.3 %all-gather.27.cloned.1.call-start = ((), (), s32[]{:S(2)}) async-start(), calls=%async_computation.18 | async-start | bytes 9469952 | tf_op jit(solution)/shard_map/all_gather | solution.py:326
  722.4 533.4 %all-gather.21.cloned.1.call-start = ((), (), s32[]{:S(2)}) async-start(), calls=%async_computation.13 | async-start | bytes 11141120 | tf_op jit(solution)/shard_map/all_gather | solution.py:69
  768.8 127.9 %copy-start.1 = (bf16[256,17,64]{0,2,1:T(8,128)(2,1)S(1)}, bf16[256,17,64]{0,2,1:T(8,128)(2,1)}, u32[]{:S(2)}) copy-start(bf16[256,17,64]{0,2,1:T(8,128)(2,1)} %copy-done) | copy-start | bytes 1671172
  768.8 127.9 %copy-start.3 = (bf16[256,1088]{0,1:T(8,128)(2,1)S(1)}, bf16[256,1088]{0,1:T(8,128)(2,1)}, u32[]{:S(2)}) copy-start(bf16[256,1088]{0,1:T(8,128)(2,1)} %get-tuple-element.1237) | copy-start | bytes 1671172
  768.8 525.5 %all-gather.29.cloned.1.call-start = ((), (), s32[]{:S(2)}) async-start(), calls=%async_computation.19 | async-start | bytes 8355840 | tf_op jit(solution)/shard_map/all_gather | solution.py:91
  926.8 4.7 copy-start.2
  969.7 4.7 copy-start.2
  1012.8 4.7 copy-start.2
  1055.9 4.7 copy-start.2
  1098.9 4.7 copy-start.2
  1142.0 4.7 copy-start.2
  1185.1 4.7 copy-start.2
  1228.2 4.7 copy-start.2
  1241.4 2.7 copy-start.15
  1244.2 1.7 copy-start.14
  1244.2 1.7 copy-start.31
  1244.2 1.7 copy-start.38
  1245.6 114.3 %reduce-scatter.27.cloned.1.call-start = ((), (), s32[]{:S(2)}) async-start(), calls=%async_computation.25 | async-start | bytes 4177920
  1255.7 169.9 %reduce-scatter.29.cloned.1.call-start = ((), (), s32[]{:S(2)}) async-start(), calls=%async_computation.26 | async-start | bytes 4177920
  1265.3 29.0 %copy-start.7 = (bf16[1,1024,272]{1,2,0:T(8,128)(2,1)S(1)}, bf16[1,1024,272]{1,2,0:T(8,128)(2,1)}, u32[]{:S(2)}) copy-start(bf16[1,1024,272]{1,2,0:T(8,128)(2,1)} %param.21) | copy-start | bytes 1671172
  1265.3 29.0 %copy-start.21 = (f32[1024]{0:T(1024)S(1)}, f32[1024]{0:T(1024)}, u32[]{:S(2)}) copy-start(f32[1024]{0:T(1024)} %copy-done.20) | copy-start | bytes 12292
  1265.3 29.0 %copy-start.23 = (f32[1024]{0:T(1024)S(1)}, f32[1024]{0:T(1024)}, u32[]{:S(2)}) copy-start(f32[1024]{0:T(1024)} %copy-done.22) | copy-start | bytes 12292
  1265.3 29.0 %copy-start.28 = (f32[272]{0:T(512)S(1)}, f32[272]{0:T(512)}, u32[]{:S(2)}) copy-start(f32[272]{0:T(512)} %param.24) | copy-start | bytes 3268
  1265.3 29.0 %copy-start.40 = (f32[272]{0:T(512)S(1)}, f32[272]{0:T(512)}, u32[]{:S(2)}) copy-start(f32[272]{0:T(512)} %param.25) | copy-start | bytes 3268
  1265.4 213.1 %reduce-scatter.25.cloned.1.call-start = ((), (), s32[]{:S(2)}) async-start(), calls=%async_computation.24 | async-start | bytes 3133440
  1302.0 203.1 %reduce-scatter.23.cloned.1.call-start = ((), (), s32[]{:S(2)}) async-start(), calls=%async_computation.20 | async-start | bytes 1044480 | tf_op jit(solution)/shard_map/reduce_scatter | solution.py:109
  1307.4 282.4 %all-reduce.15.cloned.1.call-start = ((), (), s32[]{:S(2)}) async-start(), calls=%async_computation.27 | async-start | bytes 3899392 | tf_op jit(solution)/shard_map/psum | solution.py:126
  1362.1 143.1 %copy-start.41 = (f32[272]{0:T(512)S(1)}, f32[272]{0:T(512)}, u32[]{:S(2)}) copy-start(f32[272]{0:T(512)} %param.35) | copy-start | bytes 3268
  1512.8 28.1 %copy-start.12 = (bf16[3264,272]{0,1:T(8,128)(2,1)S(1)}, bf16[3264,272]{0,1:T(8,128)(2,1)}, u32[]{:S(2)}) copy-start(bf16[3264,272]{0,1:T(8,128)(2,1)} %reshape.585) | copy-start | bytes 5326852
  1541.0 6.4 copy-start.24
  1541.0 6.4 copy-start.25
  1541.0 6.4 copy-start.34
  1541.0 6.4 copy-start.35
  1589.8 3.9 copy-start.18
  1589.8 5.0 copy-start.17
  (5 other events, 5.4 us)
Sparse Core Ops, SparseCore 0:
  9.6 45.9 all-gather.30
  67.8 59.8 reduce-scatter.14
  130.9 81.2 all-gather.16
  214.8 79.3 all-gather.14
  295.7 51.0 all-gather.34
  348.4 64.9 all-gather.32
  415.5 22.4 all-gather.18
  440.7 75.0 reduce-scatter.18
  518.6 75.0 reduce-scatter.16
  607.1 61.2 all-gather.22
  689.0 33.2 reduce-scatter.20
  724.3 91.4 all-gather.24
  817.9 78.8 all-gather.26
  898.2 59.4 all-gather.20
  1245.7 48.5 all-gather.28
  1296.5 63.3 reduce-scatter.26
  1362.1 63.4 reduce-scatter.28
  1427.8 50.6 reduce-scatter.24
  1481.4 23.6 reduce-scatter.22
  1508.1 59.9 all-reduce.14
where the time goes:
time: 1610 us; the launch traced here: 1600 us
  waiting for transfers between devices  741 us (46%)
  matrix products  397 us (25%)
  blocking collectives  222 us (14%)
  local copies, waits for them, and re-layouts  120 us (7%)
  other arithmetic  103 us (6%)
  between operations  17.7 us (1%)
    reduce_scatter x4, waiting for transfers between devices, row_partials(): lax.psum_scatter(term_fn(jnp.int32(0), tok_b * lax.axis_size('row')).asty...  209 us
    unnamed x23, waiting for transfers between devices  163 us
    all_gather x2, waiting for transfers between devices, fold_back(): piece = lax.all_gather(grad_rows, 'row', axis=0, tiled=True)  90.2 us
    dot_general x24, matrix products, head_scores(): jnp.einsum('qhd,khd->hqk', left, right, preferred_element_type=jnp.float32)  88.4 us
    all_gather x1, waiting for transfers between devices, shards(): lax.all_gather(key_rows, ('row', 'col'), axis=0, tiled=True)  79.4 us
    all_gather x1, waiting for transfers between devices, shards(): lax.all_gather(d_attn_low, ('row', 'col'), axis=0, tiled=True)  76.7 us
    dot_general x8, matrix products, back_step(): jnp.einsum('hqk,qhd->khd', d_scores, query_p3, preferred_element_type=jnp...  75.3 us
    dynamic_slice x32, local copies, waits for them, and re-layouts, one_block(): lax.dynamic_slice_in_dim(member, offset, block_len, 0)  69.6 us
  transfers between devices with their start and end apart: 20, of which 16 were waited for; matrix products, arithmetic and copies ran while one was open for 35% of the time, Pallas kernels for 0%

commit v1 on v0

--- a/solution.py
+++ b/solution.py
@@ -2,7 +2,10 @@
 
 import jax
 import jax.numpy as jnp
+import numpy as np
 from jax import lax
+from jax.experimental import pallas as pl
+from jax.experimental.pallas import tpu as pltpu
 from jax.sharding import PartitionSpec as P
 
 HEADS = 17
@@ -366,6 +369,668 @@
     )
 
 
+LOG2E = 1.4426950408889634
+LN2 = 0.6931471805599453
+PAD = 16
+VMEM_LIMIT = 56 * 1024 * 1024
+
+
+def swap(value, step):
+    size = lax.axis_size("row")
+    return lax.ppermute(value, "row", [(i, i ^ step) for i in range(size)])
+
+
+def pick(stacked, index, axis=0):
+    return lax.dynamic_index_in_dim(stacked, index, axis, keepdims=False)
+
+
+def row_gather(own):
+    far = swap(own, 2)
+    return [own, swap(own, 1), far, swap(far, 1)]
+
+
+def row_exchange(parts):
+    return [parts[0], swap(parts[1], 1), swap(parts[2], 2), swap(parts[3], 3)]
+
+
+def row_reduce(parts):
+    low = [p.astype(jnp.bfloat16) for p in parts]
+    beyond = swap(low[3], 1)
+    near = swap(low[1], 1)
+    pair = (parts[2].astype(jnp.float32) + beyond.astype(jnp.float32)).astype(jnp.bfloat16)
+    far = swap(pair, 2)
+    return parts[0].astype(jnp.float32) + near.astype(jnp.float32) + far.astype(jnp.float32)
+
+
+def in_order(parts, me):
+    stacked = jnp.stack(parts)
+    return [pick(stacked, me ^ i) for i in range(len(parts))]
+
+
+def layer_norm(values, gain, shift):
+    mean = jnp.mean(values, 1, keepdims=True)
+    variance = jnp.mean(values * values, 1, keepdims=True) - mean * mean
+    inv_std = lax.rsqrt(variance + 1e-05)
+    centred = (values - mean) * inv_std
+    return (centred * gain + shift, centred, inv_std)
+
+
+def layer_norm_back(d_normed, centred, inv_std, gain):
+    scaled = d_normed * gain
+    return inv_std * (
+        scaled
+        - jnp.mean(scaled, 1, keepdims=True)
+        - centred * jnp.mean(scaled * centred, 1, keepdims=True)
+    )
+
+
+def load_pieces(info, pieces, slot, transposed, plain, tok_b, block):
+    cols = pieces[0].shape[-1] // tok_b
+    per_block = block // tok_b
+    rows = len(pieces)
+    for s, piece in enumerate(pieces):
+        source = info[0] ^ s
+        for c in range(cols):
+            part = piece[slot, :, c * tok_b : (c + 1) * tok_b]
+            number = (info[3] ^ c) * rows + source
+            where = number // per_block
+            offset = pl.multiple_of((number % per_block) * tok_b, tok_b)
+            if transposed is not None:
+                transposed[where, :, pl.ds(offset, tok_b)] = part
+            if plain is not None:
+                plain[where, pl.ds(offset, tok_b), :] = part.T
+
+
+def allowed_mask(key_start, query_start, shape, prefix):
+    key_pos = key_start + lax.broadcasted_iota(jnp.int32, shape, 0)
+    query_pos = query_start + lax.broadcasted_iota(jnp.int32, shape, 1)
+    return (key_pos < prefix) | (key_pos <= query_pos)
+
+
+def forward_kernel(n_pieces, own_query, tok_b, block, info, *refs):
+    prefix, first = info[1], info[2]
+    pieces = refs[:n_pieces]
+    refs = refs[n_pieces:]
+    if own_query:
+        query_ref, refs = refs[0], refs[1:]
+        q_len = query_ref.shape[1]
+        n_query = 1
+    else:
+        q_len = block
+        n_query = n_pieces * pieces[0].shape[-1] // block
+    out_ref, full_ref, lse_ref, q_t, k_n, v_t, acc = refs
+    key_slot = 0 if own_query else 1
+    if not own_query:
+        load_pieces(info, pieces, 0, q_t, None, tok_b, block)
+    load_pieces(info, pieces, key_slot, None, k_n, tok_b, block)
+    load_pieces(info, pieces, key_slot + 1, v_t, None, tok_b, block)
+    edge = prefix // block
+    out_len = out_ref.shape[-1]
+
+    def one_query(n, carry):
+        start = first + n * q_len
+        query = query_ref[...] if own_query else q_t[n]
+        last = jnp.maximum(start // block, edge)
+        acc[...] = jnp.zeros_like(acc)
+
+        def step(kb, carry, masked):
+            top, total = carry
+            scores = jnp.dot(k_n[kb], query, preferred_element_type=jnp.float32)
+            if masked:
+                keep = allowed_mask(kb * block, start, scores.shape, prefix)
+                scores = jnp.where(keep, scores, -1e30)
+            new_top = jnp.maximum(top, jnp.max(scores, 0, keepdims=True))
+            probs = jnp.exp2(scores - new_top)
+            if masked:
+                probs = jnp.where(keep, probs, 0.0)
+            fade = jnp.exp2(top - new_top)
+            total = total * fade + jnp.sum(probs, 0, keepdims=True)
+            acc[...] = acc[...] * fade + jnp.dot(
+                v_t[kb], probs.astype(jnp.bfloat16), preferred_element_type=jnp.float32
+            )
+            return (new_top, total)
+
+        start_carry = (
+            jnp.full((1, q_len), -1e30, jnp.float32),
+            jnp.zeros((1, q_len), jnp.float32),
+        )
+        carry = lax.fori_loop(0, last, partial(step, masked=False), start_carry)
+        top, total = step(last, carry, True)
+        result = acc[...] / total
+        for i in range(q_len // out_len):
+            full_ref[n * (q_len // out_len) + i] = result[:, i * out_len : (i + 1) * out_len]
+            out_ref[n * (q_len // out_len) + i] = result[
+                :, i * out_len : (i + 1) * out_len
+            ].astype(jnp.bfloat16)
+        lse_ref[n] = top + jnp.log2(total)
+        return 0
+
+    lax.fori_loop(0, n_query, one_query, 0)
+
+
+def attend(info, pieces, query, tok_b, block):
+    total = len(pieces) * pieces[0].shape[-1]
+    own = query is not None
+    q_len = query.shape[1] if own else block
+    n_query = 1 if own else total // block
+    n_out = n_query * q_len // tok_b
+    vmem = pl.BlockSpec(memory_space=pltpu.VMEM)
+    return pl.pallas_call(
+        partial(forward_kernel, len(pieces), own, tok_b, block),
+        out_shape=(
+            jax.ShapeDtypeStruct((n_out, HDIM, tok_b), jnp.bfloat16),
+            jax.ShapeDtypeStruct((n_out, HDIM, tok_b), jnp.float32),
+            jax.ShapeDtypeStruct((n_query, 1, q_len), jnp.float32),
+        ),
+        in_specs=[pl.BlockSpec(memory_space=pltpu.SMEM)] + [vmem] * (len(pieces) + own),
+        out_specs=(vmem, vmem, vmem),
+        scratch_shapes=[
+            pltpu.VMEM((total // block, HDIM, block), jnp.bfloat16),
+            pltpu.VMEM((total // block, block, HDIM), jnp.bfloat16),
+            pltpu.VMEM((total // block, HDIM, block), jnp.bfloat16),
+            pltpu.VMEM((HDIM, q_len), jnp.float32),
+        ],
+        compiler_params=pltpu.CompilerParams(vmem_limit_bytes=VMEM_LIMIT),
+        cost_estimate=pl.CostEstimate(
+            flops=n_query * q_len * total * HDIM * 8, bytes_accessed=4 << 20, transcendentals=0
+        ),
+    )(info, *pieces, *([query] if own else []))
+
+
+def backward_kernel(n_pieces, own_query, tok_b, block, info, *refs):
+    prefix, first = info[1], info[2]
+    pieces = refs[:n_pieces]
+    refs = refs[n_pieces:]
+    if own_query:
+        query_ref, refs = refs[0], refs[1:]
+    full_ref, lse_ref, grad_ref = refs[:3]
+    refs = refs[3:]
+    total = n_pieces * pieces[0].shape[-1]
+    q_len = lse_ref.shape[-1]
+    n_query = lse_ref.shape[0]
+    outs = refs[:n_pieces]
+    refs = refs[n_pieces:]
+    if own_query:
+        dq_ref, refs = refs[0], refs[1:]
+    q_t, q_n, k_t, k_n, v_n, g_t, g_n, delta, dq_t, dk, dv = refs
+    key_slot = 0 if own_query else 1
+    if own_query:
+        q_t[0] = query_ref[...]
+        q_n[0] = query_ref[...].T
+    else:
+        load_pieces(info, pieces, 0, q_t, q_n, tok_b, block)
+    load_pieces(info, pieces, key_slot, k_t, k_n, tok_b, block)
+    load_pieces(info, pieces, key_slot + 1, None, v_n, tok_b, block)
+    per_query = q_len // tok_b
+    for n in range(n_query):
+        for i in range(per_query):
+            number = n * per_query + i
+            span = slice(i * tok_b, (i + 1) * tok_b)
+            grad = grad_ref[number]
+            g_t[n, :, span] = grad
+            g_n[n, span, :] = grad.T
+            delta[n, :, span] = jnp.sum(
+                grad.astype(jnp.float32) * full_ref[number], 0, keepdims=True
+            )
+    dk[...] = jnp.zeros_like(dk)
+    dv[...] = jnp.zeros_like(dv)
+    dq_t[...] = jnp.zeros_like(dq_t)
+    edge = prefix // block
+
+    def one_query(n, carry):
+        start = first + n * q_len
+        last = jnp.maximum(start // block, edge)
+
+        def step(kb, carry, masked):
+            scores = jnp.dot(k_n[kb], q_t[n], preferred_element_type=jnp.float32)
+            probs = jnp.exp2(scores - lse_ref[n])
+            if masked:
+                keep = allowed_mask(kb * block, start, scores.shape, prefix)
+                probs = jnp.where(keep, probs, 0.0)
+            d_probs = jnp.dot(v_n[kb], g_t[n], preferred_element_type=jnp.float32)
+            d_scores = (probs * (d_probs - delta[n])).astype(jnp.bfloat16)
+            dv[kb] += jnp.dot(
+                probs.astype(jnp.bfloat16), g_n[n], preferred_element_type=jnp.float32
+            )
+            dk[kb] += jnp.dot(d_scores, q_n[n], preferred_element_type=jnp.float32)
+            dq_t[n] += jnp.dot(k_t[kb], d_scores, preferred_element_type=jnp.float32)
+            return carry
+
+        lax.fori_loop(0, last, partial(step, masked=False), 0)
+        step(last, 0, True)
+        return 0
+
+    lax.fori_loop(0, n_query, one_query, 0)
+    rows = n_pieces
+    per_block = block // tok_b
+    for s, out in enumerate(outs):
+        source = info[0] ^ s
+        for c in range(total // rows // tok_b):
+            number = (info[3] ^ c) * rows + source
+            where = number // per_block
+            offset = pl.multiple_of((number % per_block) * tok_b, tok_b)
+            span = slice(c * tok_b, (c + 1) * tok_b)
+            if not own_query:
+                out[0, :, span] = (
+                    dq_t[where, :, pl.ds(offset, tok_b)] * HDIM ** (-0.5)
+                ).astype(jnp.bfloat16)
+            out[key_slot, :, span] = (
+                (dk[where, pl.ds(offset, tok_b), :] * LN2).astype(jnp.bfloat16).T
+            )
+            out[key_slot + 1, :, span] = (
+                dv[where, pl.ds(offset, tok_b), :].astype(jnp.bfloat16).T
+            )
+    if own_query:
+        dq_ref[...] = (dq_t[0] * HDIM ** (-0.5)).astype(jnp.bfloat16)
+
+
+def attend_back(info, pieces, query, full, lse, grad, tok_b, block):
+    total = len(pieces) * pieces[0].shape[-1]
+    own = query is not None
+    n_query, _, q_len = lse.shape
+    vmem = pl.BlockSpec(memory_space=pltpu.VMEM)
+    n_key = total // block
+    out_shape = tuple(jax.ShapeDtypeStruct(p.shape, jnp.bfloat16) for p in pieces)
+    if own:
+        out_shape += (jax.ShapeDtypeStruct(query.shape, jnp.bfloat16),)
+    return pl.pallas_call(
+        partial(backward_kernel, len(pieces), own, tok_b, block),
+        out_shape=out_shape,
+        in_specs=[pl.BlockSpec(memory_space=pltpu.SMEM)] + [vmem] * (len(pieces) + own + 3),
+        out_specs=(vmem,) * len(out_shape),
+        scratch_shapes=[
+            pltpu.VMEM((n_query, HDIM, q_len), jnp.bfloat16),
+            pltpu.VMEM((n_query, q_len, HDIM), jnp.bfloat16),
+            pltpu.VMEM((n_key, HDIM, block), jnp.bfloat16),
+            pltpu.VMEM((n_key, block, HDIM), jnp.bfloat16),
+            pltpu.VMEM((n_key, block, HDIM), jnp.bfloat16),
+            pltpu.VMEM((n_query, HDIM, q_len), jnp.bfloat16),
+            pltpu.VMEM((n_query, q_len, HDIM), jnp.bfloat16),
+            pltpu.VMEM((n_query, 1, q_len), jnp.float32),
+            pltpu.VMEM((n_query, HDIM, q_len), jnp.float32),
+            pltpu.VMEM((n_key, block, HDIM), jnp.float32),
+            pltpu.VMEM((n_key, block, HDIM), jnp.float32),
+        ],
+        compiler_params=pltpu.CompilerParams(vmem_limit_bytes=VMEM_LIMIT),
+        cost_estimate=pl.CostEstimate(
+            flops=n_query * q_len * total * HDIM * 20, bytes_accessed=4 << 20, transcendentals=0
+        ),
+    )(info, *pieces, *([query] if own else []), full, lse, grad)
+
+
+def dot(left, right, left_dim, right_dim):
+    return lax.dot_general(
+        left,
+        right,
+        (((left_dim,), (right_dim,)), ((), ())),
+        preferred_element_type=jnp.float32,
+    )
+
+
+def dp_swap(value):
+    return lax.ppermute(value, "dp", [(0, 1), (1, 0)])
+
+
+def col_send(value, pairs):
+    return lax.ppermute(value, "col", pairs)
+
+
+NEAR = [(0, 1), (1, 0), (2, 3), (3, 2)]
+MIDDLE = [(1, 2), (2, 1)]
+
+
+def line_gather(own, col):
+    near = col_send(own, NEAR)
+    mid = col_send(own, MIDDLE)
+    first = col == 1
+    left = col_send(jnp.where(first, mid, near), [(1, 0), (2, 1)])
+    right = col_send(jnp.where(first, near, mid), [(1, 2), (2, 3)])
+    two = jnp.where(col < 2, left, right)
+    ends = col_send(two, [(1, 0), (2, 3)])
+    three = jnp.where(first | (col == 2), mid, ends)
+    return [own, near, two, three]
+
+
+def add_low(left, right):
+    return (left.astype(jnp.float32) + right.astype(jnp.float32)).astype(jnp.bfloat16)
+
+
+def line_reduce(parts, col):
+    first = col == 1
+    ends = col_send(parts[3], [(0, 1), (3, 2)])
+    second = add_low(parts[2], ends)
+    right = col_send(second, [(0, 1), (1, 2)])
+    left = col_send(second, [(3, 2), (2, 1)])
+    near = col_send(add_low(parts[1], jnp.where(first, left, right)), NEAR)
+    mid = col_send(add_low(parts[3], jnp.where(first, right, left)), MIDDLE)
+    return parts[0].astype(jnp.float32) + near.astype(jnp.float32) + mid.astype(jnp.float32)
+
+
+def col_exchange(parts):
+    return [parts[0]] + [
+        col_send(parts[s], [(i, i ^ s) for i in range(len(parts))]) for s in range(1, len(parts))
+    ]
+
+
+def sum_everywhere(values):
+    for axis in ("row", "col"):
+        for step in (1, 2):
+            values = values + lax.ppermute(values, axis, [(i, i ^ step) for i in range(4)])
+    return values + dp_swap(values)
+
+
+def dp_scatter(values, dp, axis):
+    half = values.shape[axis] // 2
+    values = values.astype(jnp.bfloat16)
+    own = lax.dynamic_slice_in_dim(values, dp * half, half, axis)
+    other = lax.dynamic_slice_in_dim(values, (1 - dp) * half, half, axis)
+    return add_low(own, dp_swap(other))
+
+
+def dp_gather(half, dp, axis):
+    other = dp_swap(half)
+    return jnp.concatenate(
+        [jnp.where(dp == 0, half, other), jnp.where(dp == 0, other, half)], axis
+    )
+
+
+def after(value, *earlier):
+    return lax.optimization_barrier((value,) + earlier)[0]
+
+
+def with_bias_rows(weight, bias):
+    return jnp.concatenate(
+        [weight, bias[None], jnp.zeros((PAD - 1, weight.shape[1]), weight.dtype)], 0
+    )
+
+
+def strip_tables(cols, wide):
+    native = 3 * D // cols
+    slots = wide + HDIM
+    from_native = np.full((cols, cols, slots), -1, np.int32)
+    to_strip = np.full((cols, cols, slots), -1, np.int32)
+    for c in range(cols):
+        for s in range(cols):
+            for block, group, table in ((c, c ^ s, 0), (c ^ s, c, 1)):
+                count = 0
+                for i in range(3):
+                    for place in range(wide + HDIM):
+                        last = place >= wide
+                        column = i * D + (D - HDIM + place - wide if last else group * wide + place)
+                        if column // native != block:
+                            continue
+                        slot = wide + place - wide if last else count
+                        count += not last
+                        if table == 0:
+                            from_native[c, s, slot] = column - block * native
+                        else:
+                            to_strip[c, s, slot] = (
+                                3 * wide + i * HDIM + place - wide if last else i * wide + place
+                            )
+    return from_native.reshape(cols, -1), to_strip.reshape(cols, -1)
+
+
+def one_hot(table, col, size):
+    slots = pick(jnp.asarray(table), col)
+    return (lax.broadcasted_iota(jnp.int32, (size, table.shape[1]), 0) == slots[None]).astype(
+        jnp.bfloat16
+    )
+
+
+def head_shards(
+    block_input,
+    cotangent,
+    prefix_len,
+    first_gain,
+    first_shift,
+    qkv_weight,
+    qkv_bias,
+    out_weight,
+    out_bias,
+    second_gain,
+    second_shift,
+    up_weight,
+    up_bias,
+    down_weight,
+    down_bias,
+):
+    rows = lax.axis_size("row")
+    cols = lax.axis_size("col")
+    row = lax.axis_index("row")
+    col = lax.axis_index("col")
+    dp = lax.axis_index("dp")
+    tok_a = block_input.shape[1]
+    tok_b = tok_a // rows
+    feat = block_input.shape[2]
+    block = 2 * tok_b
+    wide = rows * HDIM
+    slots = wide + HDIM
+    hidden_len = up_weight.shape[1]
+    from_native, to_strip = strip_tables(cols, wide)
+
+    narrow = jnp.stack(
+        [first_gain, first_shift, out_bias, second_gain, second_shift, down_bias]
+        + [jnp.zeros_like(first_gain)] * 2
+    )
+    narrow_all = jnp.concatenate(in_order(row_gather(narrow), row), 1)
+
+    def to_tokens(values):
+        tiles = values.reshape(rows, tok_b, feat)
+        got = row_exchange([pick(tiles, row ^ s) for s in range(rows)])
+        return jnp.concatenate(in_order(got, row), 1)
+
+    def to_features(values):
+        tiles = [
+            lax.dynamic_slice_in_dim(values, (row ^ s) * feat, feat, 1) for s in range(rows)
+        ]
+        return jnp.concatenate(in_order(row_exchange(tiles), row), 0)
+
+    x_tok = to_tokens(block_input[0]).astype(jnp.float32)
+    normed_one, centred_one, inv_one = layer_norm(x_tok, narrow_all[0], narrow_all[1])
+    normed_one = normed_one.astype(jnp.bfloat16)
+    normed_parts = line_gather(normed_one, col)
+
+    spread = one_hot(from_native, col, qkv_weight.shape[1])
+    sent = dot(with_bias_rows(qkv_weight, qkv_bias), spread, 1, 0).astype(jnp.bfloat16)
+    got = col_exchange([sent[:, s * slots : (s + 1) * slots] for s in range(cols)])
+    placed = one_hot(to_strip, col, 3 * slots)
+    strip = sum(
+        dot(g, placed[:, s * slots : (s + 1) * slots], 1, 1) for s, g in enumerate(got)
+    ).astype(jnp.bfloat16)
+    strip_rows = in_order(row_gather(strip), row)
+    qkv_strip = jnp.concatenate([s[:feat] for s in strip_rows], 0)
+    strip_bias = strip[feat].astype(jnp.float32)
+
+    out_cols = lax.all_gather(out_weight.T, "col")
+    out_rows = out_cols.transpose(1, 0, 2).reshape(feat, -1)
+    out_full = jnp.concatenate(in_order(row_gather(out_rows), row), 0)
+
+    query_scale = LOG2E * HDIM ** (-0.5)
+    scale = jnp.concatenate(
+        [
+            jnp.full((wide,), query_scale, jnp.float32),
+            jnp.ones((2 * wide,), jnp.float32),
+            jnp.full((HDIM,), query_scale, jnp.float32),
+            jnp.ones((2 * HDIM,), jnp.float32),
+        ]
+    )
+    normed_set = jnp.concatenate(normed_parts, 0)
+    mixed = (
+        (dot(qkv_strip, normed_set, 0, 1) + strip_bias[:, None]) * scale[:, None]
+    ).astype(jnp.bfloat16)
+    by_head = mixed[: 3 * wide].reshape(3, rows, HDIM, tok_a)
+    pieces = row_exchange([pick(by_head, row ^ s, 1) for s in range(rows)])
+    last_query = mixed[3 * wide : 3 * wide + HDIM, :tok_b]
+    last_pieces = row_gather(after(mixed[3 * wide + HDIM :], pieces[3]).reshape(2, HDIM, tok_a))
+
+    def hidden_slice(native, earlier):
+        half = native.shape[0] // 2
+        mine = after(lax.dynamic_slice_in_dim(native, dp * half, half, 0), earlier)
+        blocks = lax.all_gather(mine, "col")
+        got = row_exchange([pick(blocks, row ^ s) for s in range(rows)])
+        got = jnp.stack(in_order(got, row))
+        return blocks, dp_gather(got, dp, 1)
+
+    up_blocks, up_got = hidden_slice(with_bias_rows(up_weight, up_bias), normed_parts[3])
+    up_slice = up_got[:, :feat].reshape(rows * feat, hidden_len)
+    up_slice_bias = up_got[0, feat].astype(jnp.float32)
+    _, down_got = hidden_slice(down_weight.T, up_blocks)
+    down_slice = down_got.reshape(rows * feat, hidden_len)
+
+    cot_tok = to_tokens(after(cotangent[0], x_tok))
+    cot_all = jnp.concatenate(row_gather(cot_tok), 0)
+
+    zero = jnp.int32(0)
+    info = jnp.stack([row, prefix_len[0], zero, col])
+    last_info = jnp.stack([row, prefix_len[0], col * tok_a + row * tok_b, col])
+    heads_out, heads_full, heads_lse = attend(info, pieces, None, tok_b, block)
+    last_out, last_full, last_lse = attend(last_info, last_pieces, last_query, tok_b, block)
+    attended = jnp.concatenate(
+        [
+            lax.all_to_all(heads_out, ("col", "row"), 0, 0, tiled=True).reshape(-1, tok_b),
+            last_out[0],
+        ],
+        0,
+    )
+    residual = x_tok + dot(attended, out_full, 0, 1) + narrow_all[2]
+    normed_two, centred_two, inv_two = layer_norm(residual, narrow_all[3], narrow_all[4])
+    normed_two = jnp.concatenate(row_gather(normed_two.astype(jnp.bfloat16)), 0)
+    hidden = dot(normed_two, up_slice, 1, 0) + up_slice_bias
+    active, gelu_back = jax.vjp(partial(jax.nn.gelu, approximate=False), hidden)
+    active = active.astype(jnp.bfloat16)
+    d_active = dot(cot_all, down_slice, 1, 0)
+    d_hidden = gelu_back(d_active)[0].astype(jnp.bfloat16)
+
+    def token_parts(values):
+        return [values[s * tok_b : (s + 1) * tok_b] for s in range(rows)]
+
+    d_norm_two = row_reduce(token_parts(dot(d_hidden, up_slice, 1, 1)))
+    d_residual = cot_tok.astype(jnp.float32) + layer_norm_back(
+        d_norm_two, centred_two, inv_two, narrow_all[3]
+    )
+    branch = d_residual.astype(jnp.bfloat16)
+    d_attended = dot(out_full, branch, 0, 1).astype(jnp.bfloat16)
+    d_heads = lax.all_to_all(
+        d_attended[: D - HDIM].reshape(rows * cols, HDIM, tok_b), ("col", "row"), 0, 0, tiled=True
+    )
+    *last_grads, d_last_query = attend_back(
+        last_info,
+        last_pieces,
+        last_query,
+        last_full,
+        last_lse,
+        d_attended[D - HDIM :][None],
+        tok_b,
+        block,
+    )
+    head_grads = attend_back(info, pieces, None, heads_full, heads_lse, d_heads, tok_b, block)
+    d_last_keys = row_reduce([after(g, d_heads) for g in last_grads]).astype(jnp.bfloat16)
+
+    partial_out = dot(after(active, d_heads), down_slice, 1, 1)
+    block_output = to_features(
+        (row_reduce(token_parts(partial_out)) + residual + narrow_all[5]).astype(jnp.bfloat16)
+    )
+
+    def hidden_grad(left, right):
+        whole = dot(left, right, 0, 0).reshape(rows, feat, hidden_len)
+        half = dp_scatter(whole, dp, 1)
+        return jnp.stack(
+            in_order(row_exchange([pick(half, row ^ s) for s in range(rows)]), row)
+        )
+
+    up_half = lax.psum_scatter(
+        hidden_grad(normed_two, d_hidden), "col", scatter_dimension=0
+    )
+    up_grad = dp_gather(up_half, dp, 0).astype(jnp.float32)
+    out_part = dp_scatter(dot(branch, attended, 0, 1).reshape(rows, feat, -1), dp, 1)
+    out_sum = row_reduce([pick(out_part, row ^ s) for s in range(rows)]).astype(jnp.bfloat16)
+    out_got = out_sum.reshape(feat // 2, cols, -1).transpose(1, 0, 2)
+    down_out_half = lax.psum_scatter(
+        jnp.concatenate([hidden_grad(cot_all, active), out_got], 2), "col", scatter_dimension=0
+    )
+    down_out_grad = dp_gather(down_out_half, dp, 0).astype(jnp.float32)
+
+    got = jnp.stack(in_order(row_exchange(list(head_grads)), row), 1)
+    d_mixed = jnp.concatenate(
+        [
+            got.reshape(3 * wide, tok_a),
+            jnp.concatenate(
+                [d_last_query, jnp.zeros((HDIM, tok_a - tok_b), jnp.bfloat16)], 1
+            ),
+            d_last_keys.reshape(2 * HDIM, tok_a),
+        ],
+        0,
+    )
+    d_norm_one = line_reduce(
+        [
+            dot(d_mixed[:, s * tok_b : (s + 1) * tok_b], qkv_strip, 0, 1).astype(jnp.bfloat16)
+            for s in range(cols)
+        ],
+        col,
+    )
+    qkv_part = dp_scatter(dot(normed_set, d_mixed, 0, 1).reshape(rows, feat, -1), dp, 1)
+    qkv_sum = row_reduce([pick(qkv_part, row ^ s) for s in range(rows)]).astype(jnp.bfloat16)
+    got = col_exchange(
+        [
+            dot(qkv_sum, placed[:, s * slots : (s + 1) * slots], 1, 0).astype(jnp.bfloat16)
+            for s in range(cols)
+        ]
+    )
+    qkv_half = sum(
+        dot(g, spread[:, s * slots : (s + 1) * slots], 1, 1) for s, g in enumerate(got)
+    ).astype(jnp.bfloat16)
+    qkv_grad = dp_gather(qkv_half, dp, 0).astype(jnp.float32)
+    input_grad = d_residual + layer_norm_back(d_norm_one, centred_one, inv_one, narrow_all[0])
+    input_grad = to_features(input_grad.astype(jnp.bfloat16)).astype(jnp.float32)
+
+    at_row = (jnp.arange(rows) == row)[:, None]
+
+    def own_row(values):
+        return jnp.where(at_row, values[None], 0.0).reshape(-1)
+
+    bias_strip = jnp.sum(d_mixed.astype(jnp.float32), 1)
+    at_col = (jnp.arange(cols) == col)[None, :, None]
+    bias_heads = jnp.where(at_col, bias_strip[: 3 * wide].reshape(3, 1, wide), 0.0)
+    bias_all = jnp.concatenate(
+        [bias_heads.reshape(3, -1), bias_strip[3 * wide :].reshape(3, HDIM)], 1
+    ).reshape(-1)
+    early = [
+        own_row(jnp.sum(cotangent[0].astype(jnp.float32), 0)),
+        jnp.sum(branch.astype(jnp.float32), 0),
+        jnp.sum(d_norm_two * centred_two, 0),
+        jnp.sum(d_norm_two, 0),
+        own_row(jnp.sum(d_hidden.astype(jnp.float32), 0)),
+        bias_all,
+        jnp.sum(d_norm_one * centred_one, 0),
+        jnp.sum(d_norm_one, 0),
+    ]
+    total = sum_everywhere(jnp.concatenate(early).reshape(8, -1)).reshape(-1)
+
+    def own_part(start, size, index):
+        return lax.dynamic_slice_in_dim(total, start + index * size, size, 0)
+
+    width = rows * feat
+    up_at = 4 * width
+    qkv_at = up_at + rows * hidden_len
+    first_at = qkv_at + 3 * width
+    return (
+        block_output[None],
+        input_grad[None],
+        own_part(first_at, feat, row),
+        own_part(first_at + width, feat, row),
+        qkv_grad,
+        own_part(qkv_at, 3 * width // cols, col),
+        down_out_grad[:, hidden_len:].T,
+        own_part(width, feat, row),
+        own_part(2 * width, feat, row),
+        own_part(3 * width, feat, row),
+        up_grad,
+        own_part(up_at, hidden_len, col),
+        down_out_grad[:, :hidden_len].T,
+        own_part(0, feat, row),
+    )
+
+
 def solution(mesh):
     in_specs = (
         P("dp", "col", "row"),
@@ -400,4 +1065,6 @@
         P("col", "row"),
         P("row"),
     )
-    return jax.shard_map(shards, mesh=mesh, in_specs=in_specs, out_specs=out_specs, check_vma=False)
+    one_head_each = mesh.shape["row"] == 4 and mesh.shape["col"] == 4 and mesh.shape["dp"] == 2
+    body = head_shards if one_head_each else shards
+    return jax.shard_map(body, mesh=mesh, in_specs=in_specs, out_specs=out_specs, check_vma=False)

time: 1610 us -> 655 us (0.41)
  waiting for transfers between devices: 741 us -> 204 us
  matrix products: 397 us -> 93.7 us
  blocking collectives: 222 us -> 18.9 us
  starting transfers between devices: 1.44 us -> 110 us
  Pallas kernels: 0 us -> 67.4 us
  other arithmetic: 103 us -> 60.3 us
  local copies, waits for them, and re-layouts: 120 us -> 77.8 us
    all_gather x11 -> x2, waiting for transfers between devices: 345 us -> 0.01 us  [hidden_slice(): blocks = lax.all_gather(mine, 'col')]
    dot_general x68 -> x27, matrix products: 397 us -> 93.7 us  [dot(): lax.dot_general(left, right, (((left_dim,), (right_dim,)), ((), ())), pre...]
    reduce_scatter x5 -> x0, waiting for transfers between devices: 234 us -> none  [the longest x4 209 us: row_partials(): lax.psum_scatter(term_fn(jnp.int32(0), tok_b * lax.axis_size('row')).asty...]
    ppermute x0 -> x93, waiting for transfers between devices: none -> 204 us  [the longest x63 113 us: swap(): return lax.ppermute(value, 'row', [(i, i ^ step) for i in range(size)])]
    unnamed x23 -> x6, waiting for transfers between devices: 163 us -> 0.09 us
    all_gather x3 -> x1, blocking collectives: 121 us -> 18.9 us  [head_shards(): out_cols = lax.all_gather(out_weight.T, 'col')]
    ppermute x0 -> x93, starting transfers between devices: none -> 97.7 us  [the longest x63 42.3 us: swap(): return lax.ppermute(value, 'row', [(i, i ^ step) for i in range(size)])]
    pallas_call x0 -> x4, Pallas kernels: none -> 67.4 us  [the longest x2 37.8 us: attend_back(): pl.pallas_call(partial(backward_kernel, len(pieces), own, tok_b, block),...]
  transfers between devices with their start and end apart: 20 -> 99, of which waited for: 16 -> 34; matrix products, arithmetic and copies ran while one was open for 35% -> 32% of each run, Pallas kernels for 0% -> 10%
where the time goes in v1:
time: 655 us; the launch traced here: 649 us
  waiting for transfers between devices  204 us (31%)
  starting transfers between devices  110 us (17%)
  matrix products  93.7 us (14%)
  local copies, waits for them, and re-layouts  77.8 us (12%)
  Pallas kernels  67.4 us (10%)
  other arithmetic  60.3 us (9%)
  blocking collectives  18.9 us (3%)
  between operations  17 us (3%)
    ppermute x63, waiting for transfers between devices, swap(): return lax.ppermute(value, 'row', [(i, i ^ step) for i in range(size)])  113 us
    dot_general x27, matrix products, dot(): lax.dot_general(left, right, (((left_dim,), (right_dim,)), ((), ())), pre...  93.7 us
    ppermute x16, waiting for transfers between devices, col_send(): return lax.ppermute(value, 'col', pairs)  45.4 us
    ppermute x63, starting transfers between devices, swap(): return lax.ppermute(value, 'row', [(i, i ^ step) for i in range(size)])  42.3 us
    pallas_call x2, Pallas kernels, attend_back(): pl.pallas_call(partial(backward_kernel, len(pieces), own, tok_b, block),...  37.8 us
    ppermute x10, waiting for transfers between devices, dp_swap(): return lax.ppermute(value, 'dp', [(0, 1), (1, 0)])  34 us
    ppermute x16, starting transfers between devices, col_send(): return lax.ppermute(value, 'col', pairs)  30.8 us
    pallas_call x2, Pallas kernels, attend(): pl.pallas_call(partial(forward_kernel, len(pieces), own, tok_b, block), o...  29.6 us
  transfers between devices with their start and end apart: 99, of which 34 were waited for; matrix products, arithmetic and copies ran while one was open for 32% of the time, Pallas kernels for 10%

profile of v1, /device:TPU:0, one launch (start us, length us, event | category | flops | bytes accessed | tf_op | source)
XLA Modules:
  0.0 648.6 jit_solution(17209907290979275734)
XLA Ops:
  11.4 3.0 collective-permute-start.10
  16.0 2.3 convolution_convert_fusion.4
  20.1 3.6 collective-permute-start.5
  28.9 2.7 fusion.45
  31.8 18.9 %all-gather = bf16[1088,272]{1,0:T(8,128)(2,1)S(1)} all-gather(bf16[272,272]{1,0:T(8,128)(2,1)S(1)} %bitcast.265), channel_id=2, replica_groups=mesh['dp'=2,'row'=4,'col'=4] {'col'}, dimensions={0}, use_global_device_ids=true | all-gather | bytes 739840 | tf_op jit(solution)/shard_map/all_gather | solution.py:844
  82.1 2.7 collective-permute-start.12
  88.0 9.4 %collective-permute-done.12 = bf16[256,1088]{0,1:T(8,128)(2,1)S(1)} collective-permute-done((bf16[256,1088]{0,1:T(8,128)(2,1)S(1)}, bf16[256,1088]{0,1:T(8,128)(2,1)S(1)}, u32[]{:S(2)}, u32[]{:S(2)}) %collective-permute-start.12) | collective-permute-done | bytes 557088 | tf_op jit(solution)/shard_map/ppermute | solution.py:675
  118.9 16.7 %collective-permute-done.16 = bf16[256,1088]{0,1:T(8,128)(2,1)S(1)} collective-permute-done((bf16[256,1088]{0,1:T(8,128)(2,1)S(1)}, bf16[256,1088]{0,1:T(8,128)(2,1)S(1)}, u32[]{:S(2)}, u32[]{:S(2)}) %collective-permute-start.16) | collective-permute-done | bytes 557088 | tf_op jit(solution)/shard_map/ppermute | solution.py:675
  135.8 2.8 multiply_convert_fusion.1
  147.1 4.7 collective-permute-done.19.refs_3_
  153.0 7.3 %collective-permute-done.18.refs_2_ = bf16[3,64,1024]{2,1,0:T(8,128)(2,1)} collective-permute-done((bf16[3,64,1024]{2,1,0:T(8,128)(2,1)}, bf16[3,64,1024]{2,1,0:T(8,128)(2,1)}, u32[]{:S(2)}, u32[]{:S(2)}) %collective-permute-start.18) | collective-permute-done | bytes 393248 | tf_op jit(solution)/shard_map/ppermute | solution.py:380
  160.3 26.6 %shard_map.272 = (bf16[16,64,256]{2,1,0:T(8,128)(2,1)}, f32[16,64,256]{2,1,0:T(8,128)}, f32[8,1,512]{2,1,0:T(1,128)}) custom-call(s32[4]{0:T(128)} %add_add_fusion.info, bf16[3,64,1024]{2,1,0:T(8,128)(2,1)} %get-tuple-element.180.refs_0_, bf16[3,64,1024]{2,1,0:T(8,128)(2,1)} %collective-permute-done.17.refs_1_, ...), custom_call_target="tpu_custom_call" | custom-call | flops 8589934592 | bytes 4194304 | tf_op jit(solution)/shard_map/pallas_call | solution.py:518
  186.9 3.6 all-to-all-start
  197.2 3.0 shard_map.273
  205.0 4.9 fusion.97
  209.9 3.1 collective-permute-done.31
  213.0 7.3 %collective-permute-done.30 = bf16[144,1088]{1,0:T(8,128)(2,1)} collective-permute-done((bf16[144,1088]{1,0:T(8,128)(2,1)}, bf16[144,1088]{1,0:T(8,128)(2,1)}, u32[]{:S(2)}, u32[]{:S(2)}) %collective-permute-start.30) | collective-permute-done | bytes 313376 | tf_op jit(solution)/shard_map/ppermute | solution.py:380
  223.1 6.6 %collective-permute-start.32 = (bf16[4,144,1088]{2,1,0:T(8,128)(2,1)}, bf16[4,144,1088]{2,1,0:T(8,128)(2,1)}, u32[]{:S(2)}, u32[]{:S(2)}) collective-permute-start(bf16[4,144,1088]{2,1,0:T(8,128)(2,1)} %pad_maximum_fusion.13), channel_id=1, source_target_pairs={{0,16},{16,0},{1,17},{17,1},{2,18},{18,2},{3,19},{19,3},{4,20},{20... | collective-permute-start | bytes 3760136 | tf_op jit(solution)/shard_map/ppermute | solution.py:671
  235.3 10.1 %collective-permute-done.27 = bf16[256,1088]{0,1:T(8,128)(2,1)} collective-permute-done((bf16[256,1088]{0,1:T(8,128)(2,1)}, bf16[256,1088]{0,1:T(8,128)(2,1)}, u32[]{:S(2)}, u32[]{:S(2)}) %collective-permute-start.27) | collective-permute-done | bytes 557088 | tf_op jit(solution)/shard_map/ppermute | solution.py:380
  245.4 13.7 %collective-permute-done.32 = bf16[4,144,1088]{2,1,0:T(8,128)(2,1)} collective-permute-done((bf16[4,144,1088]{2,1,0:T(8,128)(2,1)}, bf16[4,144,1088]{2,1,0:T(8,128)(2,1)}, u32[]{:S(2)}, u32[]{:S(2)}) %collective-permute-start.32) | collective-permute-done | bytes 1253408 | tf_op jit(solution)/shard_map/ppermute | solution.py:671
  262.0 16.8 %multiply_convert_fusion = (bf16[1024,1088]{0,1:T(8,128)(2,1)S(1)}, f32[1024,1088]{0,1:T(8,128)}, f32[1024,1088]{0,1:T(8,128)}) fusion(f32[1088]{0:T(1024)S(1)} %fusion.84, bf16[1088,1088]{1,0:T(8,128)(2,1)S(1)} %bitcast.249, bf16[256,1088]{0,1:T(8,128)(2,1)S(1)} %collective-permute-done.28, bf16[256,1088]{0,1:T(8,128)(2,1)} %collective-permute-done.27, ...), kind=kOutput, calls=%fused_computation.11 | convolution fusion | flops 2506752000 | bytes 15741184 | tf_op jit(solution)/shard_map/dot_general | solution.py:662
  278.9 5.2 convolution_convert_fusion.2
  293.4 6.7 %collective-permute-done.41 = bf16[136,1088]{1,0:T(8,128)(2,1)S(1)} collective-permute-done((bf16[136,1088]{1,0:T(8,128)(2,1)}, bf16[136,1088]{1,0:T(8,128)(2,1)S(1)}, u32[]{:S(2)}, u32[]{:S(2)}) %collective-permute-start.41) | collective-permute-done | bytes 295968 | tf_op jit(solution)/shard_map/ppermute | solution.py:380
  300.1 7.1 %collective-permute-done.40 = bf16[136,1088]{1,0:T(8,128)(2,1)S(1)} collective-permute-done((bf16[136,1088]{1,0:T(8,128)(2,1)S(1)}, bf16[136,1088]{1,0:T(8,128)(2,1)S(1)}, u32[]{:S(2)}, u32[]{:S(2)}) %collective-permute-start.40) | collective-permute-done | bytes 295968 | tf_op jit(solution)/shard_map/ppermute | solution.py:380
  309.1 8.5 %collective-permute-done.79 = bf16[4,136,1088]{2,1,0:T(8,128)(2,1)} collective-permute-done((bf16[4,136,1088]{2,1,0:T(8,128)(2,1)}, bf16[4,136,1088]{2,1,0:T(8,128)(2,1)}, u32[]{:S(2)}, u32[]{:S(2)}) %collective-permute-start.79) | collective-permute-done | bytes 1183776 | tf_op jit(solution)/shard_map/ppermute | solution.py:671
  323.1 5.7 collective-permute-done.82
  328.7 7.1 %collective-permute-done.81 = bf16[136,1088]{1,0:T(8,128)(2,1)S(1)} collective-permute-done((bf16[136,1088]{1,0:T(8,128)(2,1)S(1)}, bf16[136,1088]{1,0:T(8,128)(2,1)S(1)}, u32[]{:S(2)}, u32[]{:S(2)}) %collective-permute-start.81) | collective-permute-done | bytes 295968 | tf_op jit(solution)/shard_map/ppermute | solution.py:380
  337.2 5.3 collective-permute-done.42
  343.1 7.9 %convert_reduce_fusion = (f32[1088]{0:T(1024)S(1)}, bf16[1024,1088]{0,1:T(8,128)(2,1)S(1)}) fusion(f32[1024,1088]{0,1:T(8,128)S(1)} %bitcast.300, f32[1024,1088]{0,1:T(8,128)S(1)} %bitcast.302, bf16[1088,1088]{1,0:T(8,128)(2,1)S(1)} %bitcast.251, bf16[256,1088]{0,1:T(8,128)(2,1)} %collective-permute-done.38, bf16[256,1088]{0,1:T(8,128)(2,1)} %collective-permute-done.37, ...), kind=kOutput, calls=%fused_computation.9 | convolution fusion | flops 2457730048 | bytes 15741184 | tf_op jit(solution)/shard_map/dot_general | solution.py:662
  351.0 3.1 fusion.105
  356.2 5.8 convolution_convert_fusion.1
  365.0 2.4 constant_dynamic-slice_fusion.5
  368.9 8.4 %collective-permute-done.45 = bf16[256,1088]{0,1:T(8,128)(2,1)S(1)} collective-permute-done((bf16[256,1088]{0,1:T(8,128)(2,1)}, bf16[256,1088]{0,1:T(8,128)(2,1)S(1)}, u32[]{:S(2)}, u32[]{:S(2)}) %collective-permute-start.45) | collective-permute-done | bytes 557088 | tf_op jit(solution)/shard_map/ppermute | solution.py:380
  377.3 2.7 multiply_reduce_fusion.1
  383.4 7.9 %all-to-all-start.1 = ((bf16[16,64,256]{2,1,0:T(8,128)(2,1)}), bf16[16,64,256]{2,1,0:T(8,128)(2,1)}, u32[]{:S(2)}, u32[]{:S(2)}) async-start(bf16[16,64,256]{2,1,0:T(8,128)(2,1)} %bitcast.62), calls=%async_computation.1 | async-start | bytes 1048576 | tf_op jit(solution)/shard_map/all_to_all | solution.py:913
  393.5 2.9 collective-permute-done.88
  402.1 4.0 shard_map.275
  406.1 3.6 collective-permute-done.91
  409.6 6.1 collective-permute-done.90
  417.6 7.5 %fusion.106 = (bf16[1024,1088]{0,1:T(8,128)(2,1)S(1)}, f32[1024,1088]{0,1:T(8,128)}) fusion(bf16[1088,1088]{1,0:T(8,128)(2,1)} %bitcast.252, bf16[1024,1088]{0,1:T(8,128)(2,1)} %copy-done.110), kind=kOutput, calls=%fused_computation.347 | convolution fusion | flops 2425421824 | bytes 11280384 | tf_op jit(solution)/shard_map/dot_general | solution.py:662
  426.7 33.8 %shard_map.274 = (bf16[3,64,1024]{2,1,0:T(8,128)(2,1)}, bf16[3,64,1024]{2,1,0:T(8,128)(2,1)}, bf16[3,64,1024]{2,1,0:T(8,128)(2,1)}, bf16[3,64,1024]{2,1,0:T(8,128)(2,1)}) custom-call(s32[4]{0:T(128)} %add_add_fusion.info, bf16[3,64,1024]{2,1,0:T(8,128)(2,1)} %get-tuple-element.180.refs_0_, bf16[3,64,1024]{2,1,0:T(8,128)(2,1)} %collective-permute-done.17.refs_1_, ...), custom_call_target="tpu_custom_call" | custom-call | flops 21474836480 | bytes 4194304 | tf_op jit(solution)/shard_map/pallas_call | solution.py:636
  465.9 5.6 collective-permute-done.54
  472.6 8.0 %collective-permute-done.53 = bf16[3,64,1024]{2,1,0:T(8,128)(2,1)S(1)} collective-permute-done((bf16[3,64,1024]{2,1,0:T(8,128)(2,1)}, bf16[3,64,1024]{2,1,0:T(8,128)(2,1)S(1)}, u32[]{:S(2)}, u32[]{:S(2)}) %collective-permute-start.53) | collective-permute-done | bytes 393248 | tf_op jit(solution)/shard_map/ppermute | solution.py:380
  485.5 6.2 collective-permute-done.57
  493.8 4.8 collective-permute-start.58
  498.9 6.0 convolution_convert_fusion.3
  504.9 4.2 copy.61
  509.0 2.3 constant_dynamic-slice_fusion.13
  511.3 6.0 collective-permute-start.71
  517.3 2.3 fusion.47
  522.3 2.6 pad_maximum_fusion.11
  525.0 7.5 %collective-permute-done.48 = bf16[256,1088]{0,1:T(8,128)(2,1)} collective-permute-done((bf16[256,1088]{0,1:T(8,128)(2,1)}, bf16[256,1088]{0,1:T(8,128)(2,1)}, u32[]{:S(2)}, u32[]{:S(2)}) %collective-permute-start.48) | collective-permute-done | bytes 557088 | tf_op jit(solution)/shard_map/ppermute | solution.py:380
  546.7 18.0 %collective-permute-done.60 = bf16[256,1088]{0,1:T(8,128)(2,1)S(1)} collective-permute-done((bf16[256,1088]{0,1:T(8,128)(2,1)S(1)}, bf16[256,1088]{0,1:T(8,128)(2,1)S(1)}, u32[]{:S(2)}, u32[]{:S(2)}) %collective-permute-start.60) | collective-permute-done | bytes 557088 | tf_op jit(solution)/shard_map/ppermute | solution.py:675
  569.1 3.3 add_convert_fusion.7
  572.4 5.7 collective-permute-start.61
  581.9 5.3 collective-permute-done.74
  590.8 2.6 collective-permute-start.77
  593.4 2.6 fusion.22
  596.0 2.6 convolution_convert_fusion.12
  600.4 2.3 fusion.16
  604.9 3.4 multiply_reduce_fusion
  615.5 5.3 collective-permute-done.67
  627.0 3.8 collective-permute-done.69
  633.5 3.7 collective-permute-done.70
  (577 shorter events, 206.2 us)
Async XLA Ops:
  7.2 193.0 %all-gather.6.cloned.1.call-start = ((), (), s32[]{:S(2)}) async-start(), calls=%async_computation.4 | async-start | bytes 1658880 | tf_op jit(solution)/shard_map/all_gather | solution.py:869
  11.4 46.2 %collective-permute-start.10 = (f32[8,272]{1,0:T(8,128)S(1)}, f32[8,272]{1,0:T(8,128)}, u32[]{:S(2)}, u32[]{:S(2)}) collective-permute-start(f32[8,272]{1,0:T(8,128)S(1)} %stack.268), channel_id=1, source_target_pairs={{0,8},{4,12},{8,0},{12,4},{1,9},{5,13},{9,1},{13,5},{2,10},{6,14},... | collective-permute-start | bytes 26120 | tf_op jit(solution)/shard_map/ppermute | solution.py:380
  14.4 51.4 %collective-permute-start.9 = (f32[8,272]{1,0:T(8,128)S(1)}, f32[8,272]{1,0:T(8,128)}, u32[]{:S(2)}, u32[]{:S(2)}) collective-permute-start(f32[8,272]{1,0:T(8,128)S(1)} %stack.268), channel_id=1, source_target_pairs={{0,4},{4,0},{8,12},{12,8},{1,5},{5,1},{9,13},{13,9},{2,6},{6,2},{1... | collective-permute-start | bytes 26120 | tf_op jit(solution)/shard_map/ppermute | solution.py:380
  20.1 61.9 %collective-permute-start.5 = (bf16[288,320]{1,0:T(8,128)(2,1)}, bf16[288,320]{1,0:T(8,128)(2,1)}, u32[]{:S(2)}, u32[]{:S(2)}) collective-permute-start(bf16[288,320]{1,0:T(8,128)(2,1)} %get-tuple-element.222), channel_id=1, source_target_pairs={{0,3},{1,2},{2,1},{3,0},{4,7},{5,6},{6,5},{7,4},{8,11},{9,10},{10,... | collective-permute-start | bytes 552968 | tf_op jit(solution)/shard_map/ppermute | solution.py:675
  23.7 55.9 %collective-permute-start.3 = (bf16[288,320]{1,0:T(8,128)(2,1)}, bf16[288,320]{1,0:T(8,128)(2,1)}, u32[]{:S(2)}, u32[]{:S(2)}) collective-permute-start(bf16[288,320]{1,0:T(8,128)(2,1)} %get-tuple-element.223), channel_id=1, source_target_pairs={{0,1},{1,0},{2,3},{3,2},{4,5},{5,4},{6,7},{7,6},{8,9},{9,8},{10,11... | collective-permute-start | bytes 552968 | tf_op jit(solution)/shard_map/ppermute | solution.py:675
  26.8 42.3 %collective-permute-start.2 = (bf16[256,272]{0,1:T(8,128)(2,1)}, bf16[256,272]{0,1:T(8,128)(2,1)}, u32[]{:S(2)}, u32[]{:S(2)}) collective-permute-start(bf16[256,272]{0,1:T(8,128)(2,1)} %bitcast.236), channel_id=1, source_target_pairs={{0,12},{4,8},{8,4},{12,0},{1,13},{5,9},{9,5},{13,1},{2,14},{6,10},... | collective-permute-start | bytes 417800 | tf_op jit(solution)/shard_map/ppermute | solution.py:380
  69.0 17.4 %collective-permute-start.4 = (bf16[288,320]{1,0:T(8,128)(2,1)}, bf16[288,320]{1,0:T(8,128)(2,1)S(1)}, u32[]{:S(2)}, u32[]{:S(2)}) collective-permute-start(bf16[288,320]{1,0:T(8,128)(2,1)} %get-tuple-element.221), channel_id=1, source_target_pairs={{0,2},{1,3},{2,0},{3,1},{4,6},{5,7},{6,4},{7,5},{8,10},{9,11},{10,... | collective-permute-start | bytes 552968 | tf_op jit(solution)/shard_map/ppermute | solution.py:675
  71.9 28.0 %collective-permute-start.35 = (bf16[256,272]{0,1:T(8,128)(2,1)}, bf16[256,272]{0,1:T(8,128)(2,1)}, u32[]{:S(2)}, u32[]{:S(2)}) collective-permute-start(bf16[256,272]{0,1:T(8,128)(2,1)} %bitcast.233), channel_id=1, source_target_pairs={{0,12},{4,8},{8,4},{12,0},{1,13},{5,9},{9,5},{13,1},{2,14},{6,10},... | collective-permute-start | bytes 417800 | tf_op jit(solution)/shard_map/ppermute | solution.py:380
  73.9 31.6 %collective-permute-start.34 = (bf16[256,272]{0,1:T(8,128)(2,1)}, bf16[256,272]{0,1:T(8,128)(2,1)}, u32[]{:S(2)}, u32[]{:S(2)}) collective-permute-start(bf16[256,272]{0,1:T(8,128)(2,1)} %bitcast.289), channel_id=1, source_target_pairs={{0,8},{4,12},{8,0},{12,4},{1,9},{5,13},{9,1},{13,5},{2,10},{6,14},... | collective-permute-start | bytes 417800 | tf_op jit(solution)/shard_map/ppermute | solution.py:380
  82.1 15.3 %collective-permute-start.12 = (bf16[256,1088]{0,1:T(8,128)(2,1)S(1)}, bf16[256,1088]{0,1:T(8,128)(2,1)S(1)}, u32[]{:S(2)}, u32[]{:S(2)}) collective-permute-start(bf16[256,1088]{0,1:T(8,128)(2,1)S(1)} %add_convert_fusion.10), channel_id=1, source_target_pairs={{0,1},{1,0},{2,3},{3,2},{4,5},{5,4},{6,7},{7,6},{8,9},{9,8},{10,11... | collective-permute-start | bytes 1671176 | tf_op jit(solution)/shard_map/ppermute | solution.py:675
  86.4 21.3 %collective-permute-start.33 = (bf16[256,272]{0,1:T(8,128)(2,1)}, bf16[256,272]{0,1:T(8,128)(2,1)}, u32[]{:S(2)}, u32[]{:S(2)}) collective-permute-start(bf16[256,272]{0,1:T(8,128)(2,1)} %bitcast.235), channel_id=1, source_target_pairs={{0,4},{4,0},{8,12},{12,8},{1,5},{5,1},{9,13},{13,9},{2,6},{6,2},{1... | collective-permute-start | bytes 417800 | tf_op jit(solution)/shard_map/ppermute | solution.py:380
  87.1 25.9 %collective-permute-start.7 = (bf16[288,960]{1,0:T(8,128)(2,1)S(1)}, bf16[288,960]{1,0:T(8,128)(2,1)}, u32[]{:S(2)}, u32[]{:S(2)}) collective-permute-start(bf16[288,960]{1,0:T(8,128)(2,1)S(1)} %fusion.15), channel_id=1, source_target_pairs={{0,8},{4,12},{8,0},{12,4},{1,9},{5,13},{9,1},{13,5},{2,10},{6,14},... | collective-permute-start | bytes 1658888 | tf_op jit(solution)/shard_map/ppermute | solution.py:380
  98.6 16.2 %collective-permute-start.14 = (bf16[256,1088]{0,1:T(8,128)(2,1)}, bf16[256,1088]{0,1:T(8,128)(2,1)}, u32[]{:S(2)}, u32[]{:S(2)}) collective-permute-start(bf16[256,1088]{0,1:T(8,128)(2,1)} %get-tuple-element.218), channel_id=1, source_target_pairs={{1,0},{2,1},{5,4},{6,5},{9,8},{10,9},{13,12},{14,13},{17,16},{18,1... | collective-permute-start | bytes 1671176 | tf_op jit(solution)/shard_map/ppermute | solution.py:675
  99.9 14.9 %collective-permute-start.15 = (bf16[256,1088]{0,1:T(8,128)(2,1)}, bf16[256,1088]{0,1:T(8,128)(2,1)}, u32[]{:S(2)}, u32[]{:S(2)}) collective-permute-start(bf16[256,1088]{0,1:T(8,128)(2,1)} %get-tuple-element.217), channel_id=1, source_target_pairs={{1,2},{2,3},{5,6},{6,7},{9,10},{10,11},{13,14},{14,15},{17,18},{18... | collective-permute-start | bytes 1671176 | tf_op jit(solution)/shard_map/ppermute | solution.py:675
  105.5 40.5 %collective-permute-start.24 = (bf16[272,1088]{1,0:T(8,128)(2,1)}, bf16[272,1088]{1,0:T(8,128)(2,1)}, u32[]{:S(2)}, u32[]{:S(2)}) collective-permute-start(bf16[272,1088]{1,0:T(8,128)(2,1)} %reshape.246), channel_id=1, source_target_pairs={{0,8},{4,12},{8,0},{12,4},{1,9},{5,13},{9,1},{13,5},{2,10},{6,14},... | collective-permute-start | bytes 1775624 | tf_op jit(solution)/shard_map/ppermute | solution.py:380
  107.8 82.8 %collective-permute-start.23 = (bf16[272,1088]{1,0:T(8,128)(2,1)}, bf16[272,1088]{1,0:T(8,128)(2,1)}, u32[]{:S(2)}, u32[]{:S(2)}) collective-permute-start(bf16[272,1088]{1,0:T(8,128)(2,1)} %reshape.246), channel_id=1, source_target_pairs={{0,4},{4,0},{8,12},{12,8},{1,5},{5,1},{9,13},{13,9},{2,6},{6,2},{1... | collective-permute-start | bytes 1775624 | tf_op jit(solution)/shard_map/ppermute | solution.py:380
  115.9 19.7 %collective-permute-start.16 = (bf16[256,1088]{0,1:T(8,128)(2,1)S(1)}, bf16[256,1088]{0,1:T(8,128)(2,1)S(1)}, u32[]{:S(2)}, u32[]{:S(2)}) collective-permute-start(bf16[256,1088]{0,1:T(8,128)(2,1)S(1)} %broadcast_select_fusion.7), channel_id=1, source_target_pairs={{1,0},{2,3},{5,4},{6,7},{9,8},{10,11},{13,12},{14,15},{17,16},{18,... | collective-permute-start | bytes 1671176 | tf_op jit(solution)/shard_map/ppermute | solution.py:675
  141.2 19.1 %collective-permute-start.18 = (bf16[3,64,1024]{2,1,0:T(8,128)(2,1)}, bf16[3,64,1024]{2,1,0:T(8,128)(2,1)}, u32[]{:S(2)}, u32[]{:S(2)}) collective-permute-start(bf16[3,64,1024]{2,1,0:T(8,128)(2,1)} %get-tuple-element.177), channel_id=1, source_target_pairs={{0,8},{4,12},{8,0},{12,4},{1,9},{5,13},{9,1},{13,5},{2,10},{6,14},... | collective-permute-start | bytes 1179656 | tf_op jit(solution)/shard_map/ppermute | solution.py:380
  146.0 88.7 %collective-permute-start.37 = (bf16[256,1088]{0,1:T(8,128)(2,1)}, bf16[256,1088]{0,1:T(8,128)(2,1)}, u32[]{:S(2)}, u32[]{:S(2)}) collective-permute-start(bf16[256,1088]{0,1:T(8,128)(2,1)} %pad_maximum_fusion.24), channel_id=1, source_target_pairs={{0,8},{4,12},{8,0},{12,4},{1,9},{5,13},{9,1},{13,5},{2,10},{6,14},... | collective-permute-start | bytes 1671176 | tf_op jit(solution)/shard_map/ppermute | solution.py:380
  151.8 38.8 %collective-permute-start.25 = (bf16[272,1088]{1,0:T(8,128)(2,1)}, bf16[272,1088]{1,0:T(8,128)(2,1)S(1)}, u32[]{:S(2)}, u32[]{:S(2)}) collective-permute-start(bf16[272,1088]{1,0:T(8,128)(2,1)} %collective-permute-done.24), channel_id=1, source_target_pairs={{0,4},{4,0},{8,12},{12,8},{1,5},{5,1},{9,13},{13,9},{2,6},{6,2},{1... | collective-permute-start | bytes 1775624 | tf_op jit(solution)/shard_map/ppermute | solution.py:380
  152.0 40.7 %collective-permute-start.21 = (bf16[2,64,1024]{2,1,0:T(8,128)(2,1)}, bf16[2,64,1024]{2,1,0:T(8,128)(2,1)S(1)}, u32[]{:S(2)}, u32[]{:S(2)}) collective-permute-start(bf16[2,64,1024]{2,1,0:T(8,128)(2,1)} %bitcast.29.refs_0_), channel_id=1, source_target_pairs={{0,8},{4,12},{8,0},{12,4},{1,9},{5,13},{9,1},{13,5},{2,10},{6,14},... | collective-permute-start | bytes 786440 | tf_op jit(solution)/shard_map/ppermute | solution.py:380
  186.9 18.0 %all-to-all-start = ((bf16[16,64,256]{2,1,0:T(8,128)(2,1)}), bf16[16,64,256]{2,1,0:T(8,128)(2,1)S(1)}, u32[]{:S(2)}, u32[]{:S(2)}) async-start(bf16[16,64,256]{2,1,0:T(8,128)(2,1)} %get-tuple-element.38), calls=%async_computation | async-start | bytes 1048576 | tf_op jit(solution)/shard_map/all_to_all | solution.py:890
  190.5 98.0 %all-gather.8.cloned.1.call-start = ((), (), s32[]{:S(2)}) async-start(), calls=%async_computation.5 | async-start | bytes 1566720 | tf_op jit(solution)/shard_map/all_gather | solution.py:869
  204.5 15.8 %collective-permute-start.30 = (bf16[144,1088]{1,0:T(8,128)(2,1)}, bf16[144,1088]{1,0:T(8,128)(2,1)}, u32[]{:S(2)}, u32[]{:S(2)}) collective-permute-start(bf16[144,1088]{1,0:T(8,128)(2,1)} %get-tuple-element.187), channel_id=1, source_target_pairs={{0,8},{4,12},{8,0},{12,4},{1,9},{5,13},{9,1},{13,5},{2,10},{6,14},... | collective-permute-start | bytes 940040 | tf_op jit(solution)/shard_map/ppermute | solution.py:380
  204.8 15.5 %collective-permute-start.29 = (bf16[144,1088]{1,0:T(8,128)(2,1)}, bf16[144,1088]{1,0:T(8,128)(2,1)}, u32[]{:S(2)}, u32[]{:S(2)}) collective-permute-start(bf16[144,1088]{1,0:T(8,128)(2,1)} %get-tuple-element.188), channel_id=1, source_target_pairs={{0,4},{4,0},{8,12},{12,8},{1,5},{5,1},{9,13},{13,9},{2,6},{6,2},{1... | collective-permute-start | bytes 940040 | tf_op jit(solution)/shard_map/ppermute | solution.py:380
  223.1 36.0 %collective-permute-start.32 = (bf16[4,144,1088]{2,1,0:T(8,128)(2,1)}, bf16[4,144,1088]{2,1,0:T(8,128)(2,1)}, u32[]{:S(2)}, u32[]{:S(2)}) collective-permute-start(bf16[4,144,1088]{2,1,0:T(8,128)(2,1)} %pad_maximum_fusion.13), channel_id=1, source_target_pairs={{0,16},{16,0},{1,17},{17,1},{2,18},{18,2},{3,19},{19,3},{4,20},{20... | collective-permute-start | bytes 3760136 | tf_op jit(solution)/shard_map/ppermute | solution.py:671
  230.9 14.4 %collective-permute-start.27 = (bf16[256,1088]{0,1:T(8,128)(2,1)}, bf16[256,1088]{0,1:T(8,128)(2,1)}, u32[]{:S(2)}, u32[]{:S(2)}) collective-permute-start(bf16[256,1088]{0,1:T(8,128)(2,1)} %add_convert_fusion.9), channel_id=1, source_target_pairs={{0,8},{4,12},{8,0},{12,4},{1,9},{5,13},{9,1},{13,5},{2,10},{6,14},... | collective-permute-start | bytes 1671176 | tf_op jit(solution)/shard_map/ppermute | solution.py:380
  234.7 44.1 %collective-permute-start.36 = (bf16[256,1088]{0,1:T(8,128)(2,1)}, bf16[256,1088]{0,1:T(8,128)(2,1)}, u32[]{:S(2)}, u32[]{:S(2)}) collective-permute-start(bf16[256,1088]{0,1:T(8,128)(2,1)} %pad_maximum_fusion.24), channel_id=1, source_target_pairs={{0,4},{4,0},{8,12},{12,8},{1,5},{5,1},{9,13},{13,9},{2,6},{6,2},{1... | collective-permute-start | bytes 1671176 | tf_op jit(solution)/shard_map/ppermute | solution.py:380
  234.7 44.1 %collective-permute-start.38 = (bf16[256,1088]{0,1:T(8,128)(2,1)}, bf16[256,1088]{0,1:T(8,128)(2,1)}, u32[]{:S(2)}, u32[]{:S(2)}) collective-permute-start(bf16[256,1088]{0,1:T(8,128)(2,1)} %collective-permute-done.37), channel_id=1, source_target_pairs={{0,4},{4,0},{8,12},{12,8},{1,5},{5,1},{9,13},{13,9},{2,6},{6,2},{1... | collective-permute-start | bytes 1671176 | tf_op jit(solution)/shard_map/ppermute | solution.py:380
  235.2 25.8 %collective-permute-start.26 = (bf16[256,1088]{0,1:T(8,128)(2,1)}, bf16[256,1088]{0,1:T(8,128)(2,1)S(1)}, u32[]{:S(2)}, u32[]{:S(2)}) collective-permute-start(bf16[256,1088]{0,1:T(8,128)(2,1)} %add_convert_fusion.9), channel_id=1, source_target_pairs={{0,4},{4,0},{8,12},{12,8},{1,5},{5,1},{9,13},{13,9},{2,6},{6,2},{1... | collective-permute-start | bytes 1671176 | tf_op jit(solution)/shard_map/ppermute | solution.py:380
  245.4 15.7 %collective-permute-start.28 = (bf16[256,1088]{0,1:T(8,128)(2,1)}, bf16[256,1088]{0,1:T(8,128)(2,1)S(1)}, u32[]{:S(2)}, u32[]{:S(2)}) collective-permute-start(bf16[256,1088]{0,1:T(8,128)(2,1)} %collective-permute-done.27), channel_id=1, source_target_pairs={{0,4},{4,0},{8,12},{12,8},{1,5},{5,1},{9,13},{13,9},{2,6},{6,2},{1... | collective-permute-start | bytes 1671176 | tf_op jit(solution)/shard_map/ppermute | solution.py:380
  286.7 30.8 %collective-permute-start.79 = (bf16[4,136,1088]{2,1,0:T(8,128)(2,1)}, bf16[4,136,1088]{2,1,0:T(8,128)(2,1)}, u32[]{:S(2)}, u32[]{:S(2)}) collective-permute-start(bf16[4,136,1088]{2,1,0:T(8,128)(2,1)} %constant_dynamic-slice_fusion.12), channel_id=1, source_target_pairs={{0,16},{16,0},{1,17},{17,1},{2,18},{18,2},{3,19},{19,3},{4,20},{20... | collective-permute-start | bytes 3551240 | tf_op jit(solution)/shard_map/ppermute | solution.py:671
  290.7 16.5 %collective-permute-start.40 = (bf16[136,1088]{1,0:T(8,128)(2,1)S(1)}, bf16[136,1088]{1,0:T(8,128)(2,1)S(1)}, u32[]{:S(2)}, u32[]{:S(2)}) collective-permute-start(bf16[136,1088]{1,0:T(8,128)(2,1)S(1)} %get-tuple-element.213), channel_id=1, source_target_pairs={{0,8},{4,12},{8,0},{12,4},{1,9},{5,13},{9,1},{13,5},{2,10},{6,14},... | collective-permute-start | bytes 887816 | tf_op jit(solution)/shard_map/ppermute | solution.py:380
  292.5 14.7 %collective-permute-start.39 = (bf16[136,1088]{1,0:T(8,128)(2,1)S(1)}, bf16[136,1088]{1,0:T(8,128)(2,1)}, u32[]{:S(2)}, u32[]{:S(2)}) collective-permute-start(bf16[136,1088]{1,0:T(8,128)(2,1)S(1)} %get-tuple-element.214), channel_id=1, source_target_pairs={{0,4},{4,0},{8,12},{12,8},{1,5},{5,1},{9,13},{13,9},{2,6},{6,2},{1... | collective-permute-start | bytes 887816 | tf_op jit(solution)/shard_map/ppermute | solution.py:380
  308.7 33.7 %collective-permute-start.42 = (bf16[4,136,1088]{2,1,0:T(8,128)(2,1)S(1)}, bf16[4,136,1088]{2,1,0:T(8,128)(2,1)S(1)}, u32[]{:S(2)}, u32[]{:S(2)}) collective-permute-start(bf16[4,136,1088]{2,1,0:T(8,128)(2,1)S(1)} %pad_maximum_fusion.15), channel_id=1, source_target_pairs={{0,16},{16,0},{1,17},{17,1},{2,18},{18,2},{3,19},{19,3},{4,20},{20... | collective-permute-start | bytes 3551240 | tf_op jit(solution)/shard_map/ppermute | solution.py:671
  319.4 16.4 %collective-permute-start.81 = (bf16[136,1088]{1,0:T(8,128)(2,1)S(1)}, bf16[136,1088]{1,0:T(8,128)(2,1)S(1)}, u32[]{:S(2)}, u32[]{:S(2)}) collective-permute-start(bf16[136,1088]{1,0:T(8,128)(2,1)S(1)} %get-tuple-element.203), channel_id=1, source_target_pairs={{0,8},{4,12},{8,0},{12,4},{1,9},{5,13},{9,1},{13,5},{2,10},{6,14},... | collective-permute-start | bytes 887816 | tf_op jit(solution)/shard_map/ppermute | solution.py:380
  321.4 14.5 %collective-permute-start.80 = (bf16[136,1088]{1,0:T(8,128)(2,1)S(1)}, bf16[136,1088]{1,0:T(8,128)(2,1)S(1)}, u32[]{:S(2)}, u32[]{:S(2)}) collective-permute-start(bf16[136,1088]{1,0:T(8,128)(2,1)S(1)} %get-tuple-element.204), channel_id=1, source_target_pairs={{0,4},{4,0},{8,12},{12,8},{1,5},{5,1},{9,13},{13,9},{2,6},{6,2},{1... | collective-permute-start | bytes 887816 | tf_op jit(solution)/shard_map/ppermute | solution.py:380
  355.0 13.9 %collective-permute-start.43 = (bf16[256,1088]{0,1:T(8,128)(2,1)}, bf16[256,1088]{0,1:T(8,128)(2,1)S(1)}, u32[]{:S(2)}, u32[]{:S(2)}) collective-permute-start(bf16[256,1088]{0,1:T(8,128)(2,1)} %get-tuple-element.171), channel_id=1, source_target_pairs={{0,4},{4,0},{8,12},{12,8},{1,5},{5,1},{9,13},{13,9},{2,6},{6,2},{1... | collective-permute-start | bytes 1671176 | tf_op jit(solution)/shard_map/ppermute | solution.py:380
  362.9 14.3 %collective-permute-start.45 = (bf16[256,1088]{0,1:T(8,128)(2,1)}, bf16[256,1088]{0,1:T(8,128)(2,1)S(1)}, u32[]{:S(2)}, u32[]{:S(2)}) collective-permute-start(bf16[256,1088]{0,1:T(8,128)(2,1)} %fusion.52), channel_id=1, source_target_pairs={{0,8},{4,12},{8,0},{12,4},{1,9},{5,13},{9,1},{13,5},{2,10},{6,14},... | collective-permute-start | bytes 1671176 | tf_op jit(solution)/shard_map/ppermute | solution.py:380
  367.5 28.9 %collective-permute-start.88 = (bf16[4,136,1088]{2,1,0:T(8,128)(2,1)}, bf16[4,136,1088]{2,1,0:T(8,128)(2,1)}, u32[]{:S(2)}, u32[]{:S(2)}) collective-permute-start(bf16[4,136,1088]{2,1,0:T(8,128)(2,1)} %constant_dynamic-slice_fusion.5), channel_id=1, source_target_pairs={{0,16},{16,0},{1,17},{17,1},{2,18},{18,2},{3,19},{19,3},{4,20},{20... | collective-permute-start | bytes 3551240 | tf_op jit(solution)/shard_map/ppermute | solution.py:671
  383.4 34.2 %all-to-all-start.1 = ((bf16[16,64,256]{2,1,0:T(8,128)(2,1)}), bf16[16,64,256]{2,1,0:T(8,128)(2,1)}, u32[]{:S(2)}, u32[]{:S(2)}) async-start(bf16[16,64,256]{2,1,0:T(8,128)(2,1)} %bitcast.62), calls=%async_computation.1 | async-start | bytes 1048576 | tf_op jit(solution)/shard_map/all_to_all | solution.py:913
  391.3 177.4 %reduce-scatter.9.cloned.1.call-start = ((), (), s32[]{:S(2)}) async-start(), calls=%async_computation.7 | async-start | bytes 1566720
  398.9 16.9 %collective-permute-start.90 = (bf16[136,1088]{1,0:T(8,128)(2,1)S(1)}, bf16[136,1088]{1,0:T(8,128)(2,1)S(1)}, u32[]{:S(2)}, u32[]{:S(2)}) collective-permute-start(bf16[136,1088]{1,0:T(8,128)(2,1)S(1)} %get-tuple-element.195), channel_id=1, source_target_pairs={{0,8},{4,12},{8,0},{12,4},{1,9},{5,13},{9,1},{13,5},{2,10},{6,14},... | collective-permute-start | bytes 887816 | tf_op jit(solution)/shard_map/ppermute | solution.py:380
  399.2 16.5 %collective-permute-start.89 = (bf16[136,1088]{1,0:T(8,128)(2,1)S(1)}, bf16[136,1088]{1,0:T(8,128)(2,1)S(1)}, u32[]{:S(2)}, u32[]{:S(2)}) collective-permute-start(bf16[136,1088]{1,0:T(8,128)(2,1)S(1)} %get-tuple-element.196), channel_id=1, source_target_pairs={{0,4},{4,0},{8,12},{12,8},{1,5},{5,1},{9,13},{13,9},{2,6},{6,2},{1... | collective-permute-start | bytes 887816 | tf_op jit(solution)/shard_map/ppermute | solution.py:380
  400.7 62.0 %collective-permute-start.83 = (bf16[4,136,1088]{2,1,0:T(8,128)(2,1)}, bf16[4,136,1088]{2,1,0:T(8,128)(2,1)}, u32[]{:S(2)}, u32[]{:S(2)}) collective-permute-start(bf16[4,136,1088]{2,1,0:T(8,128)(2,1)} %constant_dynamic-slice_fusion.6), channel_id=1, source_target_pairs={{0,16},{16,0},{1,17},{17,1},{2,18},{18,2},{3,19},{19,3},{4,20},{20... | collective-permute-start | bytes 3551240 | tf_op jit(solution)/shard_map/ppermute | solution.py:671
  417.3 209.5 %reduce-scatter.7.cloned.1.call-start = ((), (), s32[]{:S(2)}) async-start(), calls=%async_computation.6 | async-start | bytes 1914880
  426.2 85.2 %collective-permute-start.47 = (bf16[256,1088]{0,1:T(8,128)(2,1)}, bf16[256,1088]{0,1:T(8,128)(2,1)}, u32[]{:S(2)}, u32[]{:S(2)}) collective-permute-start(bf16[256,1088]{0,1:T(8,128)(2,1)} %get-tuple-element.170), channel_id=1, source_target_pairs={{0,4},{4,0},{8,12},{12,8},{1,5},{5,1},{9,13},{13,9},{2,6},{6,2},{1... | collective-permute-start | bytes 1671176 | tf_op jit(solution)/shard_map/ppermute | solution.py:380
  426.7 38.6 %collective-permute-start.56 = (bf16[2,64,1024]{2,1,0:T(8,128)(2,1)S(1)}, bf16[2,64,1024]{2,1,0:T(8,128)(2,1)S(1)}, u32[]{:S(2)}, u32[]{:S(2)}) collective-permute-start(bf16[2,64,1024]{2,1,0:T(8,128)(2,1)S(1)} %copy-done.108), channel_id=1, source_target_pairs={{0,4},{4,0},{8,12},{12,8},{1,5},{5,1},{9,13},{13,9},{2,6},{6,2},{1... | collective-permute-start | bytes 786440 | tf_op jit(solution)/shard_map/ppermute | solution.py:380
  461.3 19.2 %collective-permute-start.53 = (bf16[3,64,1024]{2,1,0:T(8,128)(2,1)}, bf16[3,64,1024]{2,1,0:T(8,128)(2,1)S(1)}, u32[]{:S(2)}, u32[]{:S(2)}) collective-permute-start(bf16[3,64,1024]{2,1,0:T(8,128)(2,1)} %get-tuple-element.49), channel_id=1, source_target_pairs={{0,8},{4,12},{8,0},{12,4},{1,9},{5,13},{9,1},{13,5},{2,10},{6,14},... | collective-permute-start | bytes 1179656 | tf_op jit(solution)/shard_map/ppermute | solution.py:380
  462.7 17.9 %collective-permute-start.52 = (bf16[3,64,1024]{2,1,0:T(8,128)(2,1)}, bf16[3,64,1024]{2,1,0:T(8,128)(2,1)S(1)}, u32[]{:S(2)}, u32[]{:S(2)}) collective-permute-start(bf16[3,64,1024]{2,1,0:T(8,128)(2,1)} %get-tuple-element.48), channel_id=1, source_target_pairs={{0,4},{4,0},{8,12},{12,8},{1,5},{5,1},{9,13},{13,9},{2,6},{6,2},{1... | collective-permute-start | bytes 1179656 | tf_op jit(solution)/shard_map/ppermute | solution.py:380
  465.4 59.6 %collective-permute-start.46 = (bf16[256,1088]{0,1:T(8,128)(2,1)}, bf16[256,1088]{0,1:T(8,128)(2,1)}, u32[]{:S(2)}, u32[]{:S(2)}) collective-permute-start(bf16[256,1088]{0,1:T(8,128)(2,1)} %get-tuple-element.169), channel_id=1, source_target_pairs={{0,4},{4,0},{8,12},{12,8},{1,5},{5,1},{9,13},{13,9},{2,6},{6,2},{1... | collective-permute-start | bytes 1671176 | tf_op jit(solution)/shard_map/ppermute | solution.py:380
  471.5 13.0 %collective-permute-start.55 = (bf16[2,64,1024]{2,1,0:T(8,128)(2,1)S(1)}, bf16[2,64,1024]{2,1,0:T(8,128)(2,1)S(1)}, u32[]{:S(2)}, u32[]{:S(2)}) collective-permute-start(bf16[2,64,1024]{2,1,0:T(8,128)(2,1)S(1)} %copy-done.107), channel_id=1, source_target_pairs={{0,4},{4,0},{8,12},{12,8},{1,5},{5,1},{9,13},{13,9},{2,6},{6,2},{1... | collective-permute-start | bytes 786440 | tf_op jit(solution)/shard_map/ppermute | solution.py:380
  480.6 39.1 %collective-permute-start.84 = (bf16[136,1088]{1,0:T(8,128)(2,1)}, bf16[136,1088]{1,0:T(8,128)(2,1)}, u32[]{:S(2)}, u32[]{:S(2)}) collective-permute-start(bf16[136,1088]{1,0:T(8,128)(2,1)} %get-tuple-element.205), channel_id=1, source_target_pairs={{0,4},{4,0},{8,12},{12,8},{1,5},{5,1},{9,13},{13,9},{2,6},{6,2},{1... | collective-permute-start | bytes 887816 | tf_op jit(solution)/shard_map/ppermute | solution.py:380
  484.6 36.0 %collective-permute-start.86 = (bf16[136,1088]{1,0:T(8,128)(2,1)}, bf16[136,1088]{1,0:T(8,128)(2,1)}, u32[]{:S(2)}, u32[]{:S(2)}) collective-permute-start(bf16[136,1088]{1,0:T(8,128)(2,1)} %fusion.54), channel_id=1, source_target_pairs={{0,8},{4,12},{8,0},{12,4},{1,9},{5,13},{9,1},{13,5},{2,10},{6,14},... | collective-permute-start | bytes 887816 | tf_op jit(solution)/shard_map/ppermute | solution.py:380
  493.8 42.6 %collective-permute-start.58 = (bf16[256,1088]{0,1:T(8,128)(2,1)}, bf16[256,1088]{0,1:T(8,128)(2,1)}, u32[]{:S(2)}, u32[]{:S(2)}) collective-permute-start(bf16[256,1088]{0,1:T(8,128)(2,1)} %convolution_convert_fusion.5), channel_id=1, source_target_pairs={{0,1},{3,2},{4,5},{7,6},{8,9},{11,10},{12,13},{15,14},{16,17},{19,... | collective-permute-start | bytes 1671176 | tf_op jit(solution)/shard_map/ppermute | solution.py:675
  511.3 32.2 %collective-permute-start.71 = (bf16[4,136,960]{2,1,0:T(8,128)(2,1)}, bf16[4,136,960]{2,1,0:T(8,128)(2,1)}, u32[]{:S(2)}, u32[]{:S(2)}) collective-permute-start(bf16[4,136,960]{2,1,0:T(8,128)(2,1)} %constant_dynamic-slice_fusion.13), channel_id=1, source_target_pairs={{0,16},{16,0},{1,17},{17,1},{2,18},{18,2},{3,19},{19,3},{4,20},{20... | collective-permute-start | bytes 3133448 | tf_op jit(solution)/shard_map/ppermute | solution.py:671
  519.7 12.8 %collective-permute-start.48 = (bf16[256,1088]{0,1:T(8,128)(2,1)}, bf16[256,1088]{0,1:T(8,128)(2,1)}, u32[]{:S(2)}, u32[]{:S(2)}) collective-permute-start(bf16[256,1088]{0,1:T(8,128)(2,1)} %fusion.47), channel_id=1, source_target_pairs={{0,8},{4,12},{8,0},{12,4},{1,9},{5,13},{9,1},{13,5},{2,10},{6,14},... | collective-permute-start | bytes 1671176 | tf_op jit(solution)/shard_map/ppermute | solution.py:380
  538.5 26.2 %collective-permute-start.60 = (bf16[256,1088]{0,1:T(8,128)(2,1)S(1)}, bf16[256,1088]{0,1:T(8,128)(2,1)S(1)}, u32[]{:S(2)}, u32[]{:S(2)}) collective-permute-start(bf16[256,1088]{0,1:T(8,128)(2,1)S(1)} %add_convert_fusion.8), channel_id=1, source_target_pairs={{0,1},{1,2},{4,5},{5,6},{8,9},{9,10},{12,13},{13,14},{16,17},{17,1... | collective-permute-start | bytes 1671176 | tf_op jit(solution)/shard_map/ppermute | solution.py:675
  540.5 24.2 %collective-permute-start.59 = (bf16[256,1088]{0,1:T(8,128)(2,1)S(1)}, bf16[256,1088]{0,1:T(8,128)(2,1)S(1)}, u32[]{:S(2)}, u32[]{:S(2)}) collective-permute-start(bf16[256,1088]{0,1:T(8,128)(2,1)S(1)} %add_convert_fusion.8), channel_id=1, source_target_pairs={{3,2},{2,1},{7,6},{6,5},{11,10},{10,9},{15,14},{14,13},{19,18},{18... | collective-permute-start | bytes 1671176 | tf_op jit(solution)/shard_map/ppermute | solution.py:675
  546.0 32.1 %collective-permute-start.73 = (bf16[136,960]{1,0:T(8,128)(2,1)}, bf16[136,960]{1,0:T(8,128)(2,1)}, u32[]{:S(2)}, u32[]{:S(2)}) collective-permute-start(bf16[136,960]{1,0:T(8,128)(2,1)} %get-tuple-element.216), channel_id=1, source_target_pairs={{0,4},{4,0},{8,12},{12,8},{1,5},{5,1},{9,13},{13,9},{2,6},{6,2},{1... | collective-permute-start | bytes 783368 | tf_op jit(solution)/shard_map/ppermute | solution.py:380
  546.7 35.2 %collective-permute-start.72 = (bf16[136,960]{1,0:T(8,128)(2,1)}, bf16[136,960]{1,0:T(8,128)(2,1)}, u32[]{:S(2)}, u32[]{:S(2)}) collective-permute-start(bf16[136,960]{1,0:T(8,128)(2,1)} %get-tuple-element.215), channel_id=1, source_target_pairs={{0,4},{4,0},{8,12},{12,8},{1,5},{5,1},{9,13},{13,9},{2,6},{6,2},{1... | collective-permute-start | bytes 783368 | tf_op jit(solution)/shard_map/ppermute | solution.py:380
  567.0 37.8 %collective-permute-start.62 = (bf16[256,1088]{0,1:T(8,128)(2,1)S(1)}, bf16[256,1088]{0,1:T(8,128)(2,1)}, u32[]{:S(2)}, u32[]{:S(2)}) collective-permute-start(bf16[256,1088]{0,1:T(8,128)(2,1)S(1)} %add_convert_fusion.6), channel_id=1, source_target_pairs={{1,2},{2,1},{5,6},{6,5},{9,10},{10,9},{13,14},{14,13},{17,18},{18,... | collective-permute-start | bytes 1671176 | tf_op jit(solution)/shard_map/ppermute | solution.py:675
  572.4 32.4 %collective-permute-start.61 = (bf16[256,1088]{0,1:T(8,128)(2,1)}, bf16[256,1088]{0,1:T(8,128)(2,1)}, u32[]{:S(2)}, u32[]{:S(2)}) collective-permute-start(bf16[256,1088]{0,1:T(8,128)(2,1)} %add_convert_fusion.7), channel_id=1, source_target_pairs={{0,1},{1,0},{2,3},{3,2},{4,5},{5,4},{6,7},{7,6},{8,9},{9,8},{10,11... | collective-permute-start | bytes 1671176 | tf_op jit(solution)/shard_map/ppermute | solution.py:675
  598.6 15.6 %collective-permute-start.75 = (bf16[136,320]{1,0:T(8,128)(2,1)}, bf16[136,320]{1,0:T(8,128)(2,1)S(1)}, u32[]{:S(2)}, u32[]{:S(2)}) collective-permute-start(bf16[136,320]{1,0:T(8,128)(2,1)} %convolution_convert_fusion.12), channel_id=1, source_target_pairs={{0,1},{1,0},{2,3},{3,2},{4,5},{5,4},{6,7},{7,6},{8,9},{9,8},{10,11... | collective-permute-start | bytes 261128 | tf_op jit(solution)/shard_map/ppermute | solution.py:675
  (150 other events, 1605.4 us)
Sparse Core Ops, SparseCore 0:
  142.4 30.6 all-gather.5
  235.4 32.9 all-gather.7
  417.5 31.5 reduce-scatter.8
  525.1 43.6 reduce-scatter.6

commit v2 on v1

--- a/solution.py
+++ b/solution.py
@@ -372,7 +372,8 @@
 LOG2E = 1.4426950408889634
 LN2 = 0.6931471805599453
 PAD = 16
-VMEM_LIMIT = 56 * 1024 * 1024
+MEBI = 1024 * 1024
+VMEM_LIMIT = 56 * MEBI
 
 
 def swap(value, step):
@@ -393,13 +394,16 @@
     return [parts[0], swap(parts[1], 1), swap(parts[2], 2), swap(parts[3], 3)]
 
 
-def row_reduce(parts):
+def row_reduce_parts(parts):
     low = [p.astype(jnp.bfloat16) for p in parts]
     beyond = swap(low[3], 1)
     near = swap(low[1], 1)
-    pair = (parts[2].astype(jnp.float32) + beyond.astype(jnp.float32)).astype(jnp.bfloat16)
-    far = swap(pair, 2)
-    return parts[0].astype(jnp.float32) + near.astype(jnp.float32) + far.astype(jnp.float32)
+    far = swap(add_low(parts[2], beyond), 2)
+    return [parts[0], near, far]
+
+
+def row_reduce(parts):
+    return sum(p.astype(jnp.float32) for p in row_reduce_parts(parts))
 
 
 def in_order(parts, me):
@@ -425,14 +429,15 @@
 
 
 def load_pieces(info, pieces, slot, transposed, plain, tok_b, block):
+    rows = 4
+    groups = len(pieces) // rows
     cols = pieces[0].shape[-1] // tok_b
     per_block = block // tok_b
-    rows = len(pieces)
-    for s, piece in enumerate(pieces):
-        source = info[0] ^ s
+    for p, piece in enumerate(pieces):
+        source = info[0] ^ (p // groups)
         for c in range(cols):
             part = piece[slot, :, c * tok_b : (c + 1) * tok_b]
-            number = (info[3] ^ c) * rows + source
+            number = (info[3] ^ (p % groups * cols + c)) * rows + source
             where = number // per_block
             offset = pl.multiple_of((number % per_block) * tok_b, tok_b)
             if transposed is not None:
@@ -447,7 +452,7 @@
     return (key_pos < prefix) | (key_pos <= query_pos)
 
 
-def forward_kernel(n_pieces, own_query, tok_b, block, info, *refs):
+def forward_kernel(n_pieces, own_query, n_earlier, tok_b, block, info, *refs):
     prefix, first = info[1], info[2]
     pieces = refs[:n_pieces]
     refs = refs[n_pieces:]
@@ -458,7 +463,7 @@
     else:
         q_len = block
         n_query = n_pieces * pieces[0].shape[-1] // block
-    out_ref, full_ref, lse_ref, q_t, k_n, v_t, acc = refs
+    out_ref, full_ref, lse_ref, q_t, k_n, v_t, acc = refs[n_earlier:]
     key_slot = 0 if own_query else 1
     if not own_query:
         load_pieces(info, pieces, 0, q_t, None, tok_b, block)
@@ -508,7 +513,7 @@
     lax.fori_loop(0, n_query, one_query, 0)
 
 
-def attend(info, pieces, query, tok_b, block):
+def attend(info, pieces, query, tok_b, block, earlier=()):
     total = len(pieces) * pieces[0].shape[-1]
     own = query is not None
     q_len = query.shape[1] if own else block
@@ -516,13 +521,13 @@
     n_out = n_query * q_len // tok_b
     vmem = pl.BlockSpec(memory_space=pltpu.VMEM)
     return pl.pallas_call(
-        partial(forward_kernel, len(pieces), own, tok_b, block),
+        partial(forward_kernel, len(pieces), own, len(earlier), tok_b, block),
         out_shape=(
             jax.ShapeDtypeStruct((n_out, HDIM, tok_b), jnp.bfloat16),
             jax.ShapeDtypeStruct((n_out, HDIM, tok_b), jnp.float32),
             jax.ShapeDtypeStruct((n_query, 1, q_len), jnp.float32),
         ),
-        in_specs=[pl.BlockSpec(memory_space=pltpu.SMEM)] + [vmem] * (len(pieces) + own),
+        in_specs=[IN_SMEM] + [vmem] * (len(pieces) + own) + [ANY] * len(earlier),
         out_specs=(vmem, vmem, vmem),
         scratch_shapes=[
             pltpu.VMEM((total // block, HDIM, block), jnp.bfloat16),
@@ -532,9 +537,9 @@
         ],
         compiler_params=pltpu.CompilerParams(vmem_limit_bytes=VMEM_LIMIT),
         cost_estimate=pl.CostEstimate(
-            flops=n_query * q_len * total * HDIM * 8, bytes_accessed=4 << 20, transcendentals=0
+            flops=n_query * q_len * total * 1700, bytes_accessed=4 << 20, transcendentals=0
         ),
-    )(info, *pieces, *([query] if own else []))
+    )(info, *pieces, *([query] if own else []), *earlier)
 
 
 def backward_kernel(n_pieces, own_query, tok_b, block, info, *refs):
@@ -546,10 +551,11 @@
     full_ref, lse_ref, grad_ref = refs[:3]
     refs = refs[3:]
     total = n_pieces * pieces[0].shape[-1]
+    rows = 4
     q_len = lse_ref.shape[-1]
     n_query = lse_ref.shape[0]
-    outs = refs[:n_pieces]
-    refs = refs[n_pieces:]
+    outs = refs[:rows]
+    refs = refs[rows:]
     if own_query:
         dq_ref, refs = refs[0], refs[1:]
     q_t, q_n, k_t, k_n, v_n, g_t, g_n, delta, dq_t, dk, dv = refs
@@ -601,7 +607,6 @@
         return 0
 
     lax.fori_loop(0, n_query, one_query, 0)
-    rows = n_pieces
     per_block = block // tok_b
     for s, out in enumerate(outs):
         source = info[0] ^ s
@@ -630,7 +635,9 @@
     n_query, _, q_len = lse.shape
     vmem = pl.BlockSpec(memory_space=pltpu.VMEM)
     n_key = total // block
-    out_shape = tuple(jax.ShapeDtypeStruct(p.shape, jnp.bfloat16) for p in pieces)
+    out_shape = tuple(
+        jax.ShapeDtypeStruct(pieces[0].shape[:2] + (total // 4,), jnp.bfloat16) for _ in range(4)
+    )
     if own:
         out_shape += (jax.ShapeDtypeStruct(query.shape, jnp.bfloat16),)
     return pl.pallas_call(
@@ -653,7 +660,7 @@
         ],
         compiler_params=pltpu.CompilerParams(vmem_limit_bytes=VMEM_LIMIT),
         cost_estimate=pl.CostEstimate(
-            flops=n_query * q_len * total * HDIM * 20, bytes_accessed=4 << 20, transcendentals=0
+            flops=n_query * q_len * total * 2200, bytes_accessed=4 << 20, transcendentals=0
         ),
     )(info, *pieces, *([query] if own else []), full, lse, grad)
 
@@ -679,31 +686,28 @@
 MIDDLE = [(1, 2), (2, 1)]
 
 
-def line_gather(own, col):
-    near = col_send(own, NEAR)
-    mid = col_send(own, MIDDLE)
-    first = col == 1
-    left = col_send(jnp.where(first, mid, near), [(1, 0), (2, 1)])
-    right = col_send(jnp.where(first, near, mid), [(1, 2), (2, 3)])
-    two = jnp.where(col < 2, left, right)
-    ends = col_send(two, [(1, 0), (2, 3)])
-    three = jnp.where(first | (col == 2), mid, ends)
-    return [own, near, two, three]
+OUTWARD = [(1, 0), (2, 3)]
+INWARD = [(0, 1), (3, 2)]
+
+
+def pair_sum(value):
+    return value.astype(jnp.float32) + dp_swap(value).astype(jnp.float32)
 
 
 def add_low(left, right):
     return (left.astype(jnp.float32) + right.astype(jnp.float32)).astype(jnp.bfloat16)
 
 
-def line_reduce(parts, col):
-    first = col == 1
-    ends = col_send(parts[3], [(0, 1), (3, 2)])
-    second = add_low(parts[2], ends)
-    right = col_send(second, [(0, 1), (1, 2)])
-    left = col_send(second, [(3, 2), (2, 1)])
-    near = col_send(add_low(parts[1], jnp.where(first, left, right)), NEAR)
-    mid = col_send(add_low(parts[3], jnp.where(first, right, left)), MIDDLE)
-    return parts[0].astype(jnp.float32) + near.astype(jnp.float32) + mid.astype(jnp.float32)
+def line_reduce(parts, beside=lambda stage, arrived: ()):
+    ends = col_send(parts[3], INWARD)
+    ends = after(ends, *parts[:3], *beside(0, None))
+    outer = col_send(after(parts[2], ends), INWARD)
+    inner = col_send(add_low(parts[2], ends), MIDDLE)
+    inner, outer = after([inner, outer], *beside(1, ends))
+    mid = col_send(add_low(parts[3], outer), MIDDLE)
+    near = col_send(add_low(parts[1], inner), NEAR)
+    near, mid = after([near, mid], *beside(2, inner))
+    return [parts[0], near, mid]
 
 
 def col_exchange(parts):
@@ -734,8 +738,405 @@
     )
 
 
-def after(value, *earlier):
-    return lax.optimization_barrier((value,) + earlier)[0]
+ANY = pl.BlockSpec(memory_space=pl.ANY)
+IN_VMEM = pl.BlockSpec(memory_space=pltpu.VMEM)
+IN_SMEM = pl.BlockSpec(memory_space=pltpu.SMEM)
+
+
+def after(values, *earlier):
+    single = not isinstance(values, (list, tuple))
+    arrays = [values] if single else list(values)
+
+    def nothing(*refs):
+        pass
+
+    got = pl.pallas_call(
+        nothing,
+        out_shape=[jax.ShapeDtypeStruct(a.shape, a.dtype) for a in arrays],
+        in_specs=[ANY] * (len(arrays) + len(earlier)),
+        out_specs=[ANY] * len(arrays),
+        input_output_aliases={i: i for i in range(len(arrays))},
+        cost_estimate=pl.CostEstimate(flops=0, bytes_accessed=0, transcendentals=0),
+    )(*arrays, *earlier)
+    return got[0] if single else list(got)
+
+
+def cost(flops, *arrays):
+    moved = sum(a.size * a.dtype.itemsize for a in arrays)
+    return pl.CostEstimate(flops=flops, bytes_accessed=moved, transcendentals=0)
+
+
+def small_kernel(body, out_shape, *operands, scalars=1, flops=0):
+    return pl.pallas_call(
+        body,
+        out_shape=out_shape,
+        in_specs=[IN_SMEM] * scalars + [IN_VMEM] * (len(operands) - scalars),
+        out_specs=jax.tree.map(lambda _: IN_VMEM, out_shape),
+        compiler_params=pltpu.CompilerParams(vmem_limit_bytes=VMEM_LIMIT),
+        cost_estimate=cost(flops, *operands[scalars:], *jax.tree.leaves(out_shape)),
+    )(*operands)
+
+
+def shape_of(shape, dtype):
+    return jax.ShapeDtypeStruct(shape, dtype)
+
+
+def assemble(me, pieces, keep):
+    def body(info, *refs):
+        out = refs[-1]
+        for s in range(len(pieces)):
+            at = pl.multiple_of((info[0] ^ s) * keep, 16)
+            out[pl.ds(at, keep), :] = refs[s][0:keep, :]
+
+    piece = pieces[0]
+    return small_kernel(
+        body, shape_of((len(pieces) * keep, piece.shape[1]), piece.dtype), me, *pieces
+    )
+
+
+def feature_sums(values):
+    return jnp.sum(values, 0, keepdims=True)
+
+
+def normalised(total, squares, width):
+    mean = total / width
+    return mean, lax.rsqrt(squares / width - mean * mean + 1e-05)
+
+
+def token_tiles(me, values, narrow, count):
+    feat, tokens = values.shape
+    tok = tokens // count
+    extra = 0 if narrow is None else 128
+
+    def body(info, *refs):
+        outs = refs[-count:]
+        if narrow is not None:
+            rest = refs[1][...].T[:feat, :]
+            cuts = []
+            for _ in range(3):
+                cuts.append(rest.astype(jnp.bfloat16))
+                rest = rest - cuts[-1].astype(jnp.float32)
+        for s in range(count):
+            at = pl.multiple_of((info[0] ^ s) * tok, tok)
+            outs[s][:, 0:tok] = refs[0][:, pl.ds(at, tok)]
+            if narrow is not None:
+                for n, cut in enumerate(cuts):
+                    outs[s][:, tok + n * cut.shape[1] : tok + (n + 1) * cut.shape[1]] = cut
+                outs[s][:, tok + 3 * cuts[0].shape[1] :] = jnp.zeros(
+                    (feat, extra - 3 * cuts[0].shape[1]), jnp.bfloat16
+                )
+
+    return small_kernel(
+        body,
+        (shape_of((feat, tok + extra), jnp.bfloat16),) * count,
+        me,
+        values,
+        *(() if narrow is None else (narrow,)),
+    )
+
+
+def first_norm(me, pieces, tok, kinds):
+    count = len(pieces)
+    feat = pieces[0].shape[0]
+
+    def body(info, *refs):
+        x_refs = refs[:count]
+        x_out, n_out, cols_out = refs[count:]
+        total = sum(feature_sums(x[:, 0:tok].astype(jnp.float32)) for x in x_refs)
+        squares = sum(feature_sums(jnp.square(x[:, 0:tok].astype(jnp.float32))) for x in x_refs)
+        mean, inv_std = normalised(total, squares, count * feat)
+        for s in range(count):
+            at = pl.multiple_of((info[0] ^ s) * feat, 16)
+            extra = x_refs[s][:, tok:].astype(jnp.float32)
+            cols = (
+                extra[:, 0:kinds]
+                + extra[:, kinds : 2 * kinds]
+                + extra[:, 2 * kinds : 3 * kinds]
+            )
+            cols_out[pl.ds(at, feat), :] = cols
+            value = x_refs[s][:, 0:tok]
+            x_out[pl.ds(at, feat), :] = value
+            n_out[pl.ds(at, feat), :] = (
+                (value.astype(jnp.float32) - mean) * inv_std * cols[:, 0:1] + cols[:, 1:2]
+            ).astype(jnp.bfloat16)
+
+    return small_kernel(
+        body,
+        (
+            shape_of((count * feat, tok), jnp.bfloat16),
+            shape_of((count * feat, tok), jnp.bfloat16),
+            shape_of((count * feat, kinds), jnp.float32),
+        ),
+        me,
+        *pieces,
+    )
+
+
+def project_out(info, heads, last, out_full, x_tok, cols):
+    width, tok = x_tok.shape
+
+    def body(info, heads_ref, last_ref, out_ref, x_ref, cols_ref, att_ref, res_ref, n_ref):
+        inner = heads_ref.shape[0] * heads_ref.shape[1]
+        att_ref[0:inner, :] = heads_ref[...].reshape(inner, tok)
+        att_ref[inner:width, :] = last_ref[0]
+        blocks, feat, hd = out_ref.shape
+        per_row = width // hd
+        for r in range(blocks // per_row):
+            span = slice(r * feat, (r + 1) * feat)
+            res_ref[span, :] = (
+                sum(
+                    jnp.dot(
+                        out_ref[r * per_row + (c ^ info[3])],
+                        att_ref[c * hd : (c + 1) * hd, :],
+                        preferred_element_type=jnp.float32,
+                    )
+                    for c in range(per_row)
+                )
+                + x_ref[span, :].astype(jnp.float32)
+                + cols_ref[span, 2:3]
+            )
+        value = res_ref[...]
+        mean, inv_std = normalised(feature_sums(value), feature_sums(value * value), width)
+        n_ref[...] = ((value - mean) * inv_std * cols_ref[:, 3:4] + cols_ref[:, 4:5]).astype(
+            jnp.bfloat16
+        )
+
+    return small_kernel(
+        body,
+        (
+            shape_of((width, tok), jnp.bfloat16),
+            shape_of((width, tok), jnp.float32),
+            shape_of((width, tok), jnp.bfloat16),
+        ),
+        info,
+        heads,
+        last,
+        out_full,
+        x_tok,
+        cols,
+    )
+
+
+def norm_gradient(parts, values_ref, gain):
+    d_normed = sum(p[...].astype(jnp.float32) for p in parts)
+    values = values_ref[...].astype(jnp.float32)
+    width = values.shape[0]
+    mean, inv_std = normalised(feature_sums(values), feature_sums(values * values), width)
+    centred = (values - mean) * inv_std
+    scaled = d_normed * gain
+    d_values = inv_std * (
+        scaled - feature_sums(scaled) / width - centred * (feature_sums(scaled * centred) / width)
+    )
+    return (
+        d_values,
+        jnp.sum(d_normed * centred, 1, keepdims=True),
+        jnp.sum(d_normed, 1, keepdims=True),
+    )
+
+
+def second_norm_back(info, parts, residual, cot, cols, out_full):
+    width, tok = residual.shape
+
+    def body(info, *refs):
+        parts_refs = refs[:3]
+        res_ref, cot_ref, cols_ref, out_ref, d_ref, low_ref, sums_ref, att_ref = refs[3:]
+        d_values, gain_sum, shift_sum = norm_gradient(parts_refs, res_ref, cols_ref[:, 3:4])
+        d_res = cot_ref[...].astype(jnp.float32) + d_values
+        low = d_res.astype(jnp.bfloat16)
+        d_ref[...] = d_res
+        low_ref[...] = low
+        sums_ref[:, 0:1] = gain_sum
+        sums_ref[:, 1:2] = shift_sum
+        sums_ref[:, 2:3] = jnp.sum(low.astype(jnp.float32), 1, keepdims=True)
+        blocks, feat, hd = out_ref.shape
+        per_row = width // hd
+        for c in range(per_row):
+            att_ref[c * hd : (c + 1) * hd, :] = sum(
+                lax.dot_general(
+                    out_ref[r * per_row + (c ^ info[3])],
+                    low_ref[r * feat : (r + 1) * feat, :],
+                    (((0,), (0,)), ((), ())),
+                    preferred_element_type=jnp.float32,
+                )
+                for r in range(blocks // per_row)
+            ).astype(jnp.bfloat16)
+
+    return small_kernel(
+        body,
+        (
+            shape_of((width, tok), jnp.float32),
+            shape_of((width, tok), jnp.bfloat16),
+            shape_of((width, 3), jnp.float32),
+            shape_of((width, tok), jnp.bfloat16),
+        ),
+        info,
+        *parts,
+        residual,
+        cot,
+        cols,
+        out_full,
+    )
+
+
+def first_norm_back(me, parts, x_tok, d_residual, cols, count):
+    width, tok = x_tok.shape
+    feat = width // count
+
+    def body(info, *refs):
+        parts_refs = refs[:3]
+        x_ref, d_ref, cols_ref = refs[3:6]
+        outs = refs[6 : 6 + count]
+        sums_ref, whole = refs[6 + count :]
+        d_values, gain_sum, shift_sum = norm_gradient(parts_refs, x_ref, cols_ref[:, 0:1])
+        whole[...] = d_ref[...] + d_values
+        for s in range(count):
+            at = pl.multiple_of((info[0] ^ s) * feat, 16)
+            outs[s][...] = whole[pl.ds(at, feat), :].astype(jnp.bfloat16)
+        sums_ref[:, 0:1] = gain_sum
+        sums_ref[:, 1:2] = shift_sum
+
+    vmem_count = 6
+    return pl.pallas_call(
+        body,
+        out_shape=tuple(shape_of((feat, tok), jnp.bfloat16) for _ in range(count))
+        + (shape_of((width, 2), jnp.float32),),
+        in_specs=[IN_SMEM] + [IN_VMEM] * vmem_count,
+        out_specs=(IN_VMEM,) * (count + 1),
+        scratch_shapes=[pltpu.VMEM((width, tok), jnp.float32)],
+        compiler_params=pltpu.CompilerParams(vmem_limit_bytes=VMEM_LIMIT),
+        cost_estimate=cost(0, *parts, x_tok, d_residual, d_residual),
+    )(me, *parts, x_tok, d_residual, cols)
+
+
+def side_by_side(me, pieces, dtype):
+    feat, tok = pieces[0].shape
+
+    def body(info, *refs):
+        for s in range(len(pieces)):
+            at = pl.multiple_of((info[0] ^ s) * tok, tok)
+            refs[-1][:, pl.ds(at, tok)] = refs[s][...].astype(dtype)
+
+    return small_kernel(body, shape_of((feat, len(pieces) * tok), dtype), me, *pieces)
+
+
+def normal_tail(value):
+    z = value * 0.7071067811865476
+    t = 1.0 / (1.0 + 0.5 * z)
+    poly = jnp.full_like(t, 0.17087277)
+    for factor in (
+        -0.82215223,
+        1.48851587,
+        -1.13520398,
+        0.27886807,
+        -0.18628806,
+        0.09678418,
+        0.37409196,
+        1.00002368,
+        -1.26551223,
+    ):
+        poly = poly * t + factor
+    return t * jnp.exp(poly - z * z)
+
+
+def feed_forward(normed, cot, up, down, bias):
+    width, tok = normed.shape
+    hidden_len = up.shape[1]
+
+    def body(n_ref, cot_ref, up_ref, down_ref, bias_ref, active_ref, d_ref, sent_ref):
+        hidden = (
+            jnp.dot(n_ref[...].T, up_ref[...], preferred_element_type=jnp.float32) + bias_ref[...]
+        )
+        d_active = jnp.dot(cot_ref[...].T, down_ref[...], preferred_element_type=jnp.float32)
+        tail = 0.5 * normal_tail(jnp.abs(hidden))
+        below = jnp.where(hidden < 0, tail, 1.0 - tail)
+        density = 0.3989422804014327 * jnp.exp(-0.5 * hidden * hidden)
+        active_ref[...] = (hidden * below).astype(jnp.bfloat16)
+        d_hidden = (d_active * (below + hidden * density)).astype(jnp.bfloat16)
+        d_ref[...] = d_hidden
+        sent_ref[...] = lax.dot_general(
+            up_ref[...],
+            d_hidden,
+            (((1,), (1,)), ((), ())),
+            preferred_element_type=jnp.float32,
+        ).astype(jnp.bfloat16)
+
+    return small_kernel(
+        body,
+        (
+            shape_of((tok, hidden_len), jnp.bfloat16),
+            shape_of((tok, hidden_len), jnp.bfloat16),
+            shape_of((width, tok), jnp.bfloat16),
+        ),
+        normed,
+        cot,
+        up,
+        down,
+        bias,
+        scalars=0,
+        flops=10 * tok * width * hidden_len,
+    )
+
+
+def block_products(left, right, feat, hd):
+    rows, cols = left.shape[0] // feat, right.shape[0] // hd
+
+    def body(left_ref, right_ref, out_ref):
+        for r in range(rows):
+            whole = lax.dot_general(
+                left_ref[r * feat : (r + 1) * feat, :],
+                right_ref[...],
+                (((1,), (1,)), ((), ())),
+                preferred_element_type=jnp.float32,
+            ).astype(jnp.bfloat16)
+            for c in range(cols):
+                out_ref[r * cols + c] = whole[:, c * hd : (c + 1) * hd]
+
+    return small_kernel(
+        body, shape_of((rows * cols, feat, hd), jnp.bfloat16), left, right, scalars=0
+    )
+
+
+def row_products(me, left, right, count):
+    feat = left.shape[0] // count
+
+    def body(info, left_ref, right_ref, *outs):
+        for s in range(count):
+            at = pl.multiple_of((info[0] ^ s) * feat, 16)
+            outs[s][...] = lax.dot_general(
+                left_ref[pl.ds(at, feat), :],
+                right_ref[...],
+                (((1,), (1,)), ((), ())),
+                preferred_element_type=jnp.float32,
+            ).astype(jnp.bfloat16)
+
+    shape = shape_of((feat, right.shape[0]), jnp.bfloat16)
+    return small_kernel(body, (shape,) * count, me, left, right)
+
+
+def mixed_gradient(me, heads, d_query, last_parts):
+    count = len(heads)
+    kinds, hdim, tokens = heads[0].shape
+    rows = kinds * count * hdim + kinds * hdim
+
+    def body(info, *refs):
+        query_ref = refs[count]
+        last_refs = refs[count + 1 : count + 4]
+        out = refs[count + 4]
+        for s in range(count):
+            for k in range(kinds):
+                at = pl.multiple_of((k * count + (info[0] ^ s)) * hdim, hdim)
+                out[pl.ds(at, hdim), :] = refs[s][k]
+        base = kinds * count * hdim
+        out[base : base + hdim, :] = jnp.zeros((hdim, tokens), jnp.bfloat16)
+        out[base : base + hdim, 0 : query_ref.shape[1]] = query_ref[...]
+        for k in range(2):
+            out[base + (k + 1) * hdim : base + (k + 2) * hdim, :] = sum(
+                ref[k].astype(jnp.float32) for ref in last_refs
+            ).astype(jnp.bfloat16)
+
+    return small_kernel(
+        body, shape_of((rows, tokens), jnp.bfloat16), me, *heads, d_query, *last_parts
+    )
 
 
 def with_bias_rows(weight, bias):
@@ -808,42 +1209,56 @@
     hidden_len = up_weight.shape[1]
     from_native, to_strip = strip_tables(cols, wide)
 
-    narrow = jnp.stack(
-        [first_gain, first_shift, out_bias, second_gain, second_shift, down_bias]
-        + [jnp.zeros_like(first_gain)] * 2
-    )
-    narrow_all = jnp.concatenate(in_order(row_gather(narrow), row), 1)
-
-    def to_tokens(values):
-        tiles = values.reshape(rows, tok_b, feat)
-        got = row_exchange([pick(tiles, row ^ s) for s in range(rows)])
-        return jnp.concatenate(in_order(got, row), 1)
-
-    def to_features(values):
-        tiles = [
-            lax.dynamic_slice_in_dim(values, (row ^ s) * feat, feat, 1) for s in range(rows)
-        ]
-        return jnp.concatenate(in_order(row_exchange(tiles), row), 0)
-
-    x_tok = to_tokens(block_input[0]).astype(jnp.float32)
-    normed_one, centred_one, inv_one = layer_norm(x_tok, narrow_all[0], narrow_all[1])
-    normed_one = normed_one.astype(jnp.bfloat16)
-    normed_parts = line_gather(normed_one, col)
-
+    me = row[None]
+    narrow = jnp.concatenate(
+        [
+            jnp.stack(
+                [first_gain, first_shift, out_bias, second_gain, second_shift, down_bias]
+                + [jnp.zeros_like(first_gain)] * 2
+            ),
+            jnp.zeros((8, 384 - feat), jnp.float32),
+        ],
+        1,
+    )
+
+    x_got = row_exchange(list(token_tiles(me, block_input[0].T, narrow, rows)))
     spread = one_hot(from_native, col, qkv_weight.shape[1])
     sent = dot(with_bias_rows(qkv_weight, qkv_bias), spread, 1, 0).astype(jnp.bfloat16)
-    got = col_exchange([sent[:, s * slots : (s + 1) * slots] for s in range(cols)])
+    out_rows = jnp.concatenate([out_weight.T, jnp.zeros((PAD, out_weight.shape[0]), jnp.bfloat16)])
+    got = col_exchange(
+        [
+            jnp.concatenate([sent[:, s * slots : (s + 1) * slots], out_rows], 1)
+            for s in range(cols)
+        ]
+    )
+    x_got[1], *got[1:] = after([x_got[1], *got[1:]])
+    out_got = [g[:feat, slots:] for g in got]
+    got = [g[:, :slots] for g in got]
+    x_tok, normed_one, cols_all = first_norm(me, x_got, tok_b, narrow.shape[0])
+
+    near = col_send(normed_one, NEAR)
+    mid = col_send(normed_one, MIDDLE)
+    cot_got = row_exchange(
+        list(token_tiles(me, after(cotangent[0].T, normed_one), None, rows))
+    )
+    near, mid, *cot_got[1:] = after([near, mid, *cot_got[1:]])
+    inner = col_send(near, MIDDLE)
+    outer = col_send(mid, OUTWARD)
     placed = one_hot(to_strip, col, 3 * slots)
-    strip = sum(
-        dot(g, placed[:, s * slots : (s + 1) * slots], 1, 1) for s, g in enumerate(got)
-    ).astype(jnp.bfloat16)
-    strip_rows = in_order(row_gather(strip), row)
-    qkv_strip = jnp.concatenate([s[:feat] for s in strip_rows], 0)
+    strip = dot(jnp.concatenate(got, 1), placed, 1, 1).astype(jnp.bfloat16)
     strip_bias = strip[feat].astype(jnp.float32)
-
-    out_cols = lax.all_gather(out_weight.T, "col")
-    out_rows = out_cols.transpose(1, 0, 2).reshape(feat, -1)
-    out_full = jnp.concatenate(in_order(row_gather(out_rows), row), 0)
+    strip_near = swap(strip, 1)
+    strip_far = swap(strip, 2)
+    cot_tok = assemble(me, cot_got, feat)
+    inner, outer, strip_near, strip_far = after([inner, outer, strip_near, strip_far], cot_tok)
+    ends = col_send(inner, OUTWARD)
+    qkv_strip = assemble(me, [strip, strip_near, strip_far, swap(strip_far, 1)], feat)
+
+    up_down = lax.all_gather(jnp.stack([up_weight, down_weight.T]), "row")
+    up_slice = up_down[:, 0].reshape(rows * feat, hidden_len)
+    down_slice = up_down[:, 1].reshape(rows * feat, hidden_len)
+
+    out_full = lax.all_gather(jnp.stack(out_got), "row").reshape((-1,) + out_weight.shape)
 
     query_scale = LOG2E * HDIM ** (-0.5)
     scale = jnp.concatenate(
@@ -854,62 +1269,83 @@
             jnp.ones((2 * HDIM,), jnp.float32),
         ]
     )
-    normed_set = jnp.concatenate(normed_parts, 0)
-    mixed = (
-        (dot(qkv_strip, normed_set, 0, 1) + strip_bias[:, None]) * scale[:, None]
-    ).astype(jnp.bfloat16)
-    by_head = mixed[: 3 * wide].reshape(3, rows, HDIM, tok_a)
-    pieces = row_exchange([pick(by_head, row ^ s, 1) for s in range(rows)])
-    last_query = mixed[3 * wide : 3 * wide + HDIM, :tok_b]
-    last_pieces = row_gather(after(mixed[3 * wide + HDIM :], pieces[3]).reshape(2, HDIM, tok_a))
-
-    def hidden_slice(native, earlier):
-        half = native.shape[0] // 2
-        mine = after(lax.dynamic_slice_in_dim(native, dp * half, half, 0), earlier)
-        blocks = lax.all_gather(mine, "col")
-        got = row_exchange([pick(blocks, row ^ s) for s in range(rows)])
-        got = jnp.stack(in_order(got, row))
-        return blocks, dp_gather(got, dp, 1)
-
-    up_blocks, up_got = hidden_slice(with_bias_rows(up_weight, up_bias), normed_parts[3])
-    up_slice = up_got[:, :feat].reshape(rows * feat, hidden_len)
-    up_slice_bias = up_got[0, feat].astype(jnp.float32)
-    _, down_got = hidden_slice(down_weight.T, up_blocks)
-    down_slice = down_got.reshape(rows * feat, hidden_len)
-
-    cot_tok = to_tokens(after(cotangent[0], x_tok))
-    cot_all = jnp.concatenate(row_gather(cot_tok), 0)
+    def project(normed):
+        mixed = (
+            (dot(qkv_strip, normed, 0, 0) + strip_bias[:, None]) * scale[:, None]
+        ).astype(jnp.bfloat16)
+        by_head = mixed[: 3 * wide].reshape(3, rows, HDIM, -1)
+        return mixed, [pick(by_head, row ^ s, 1) for s in range(rows)]
+
+    first_set = jnp.concatenate([normed_one, near], 1)
+    mixed_first, tiles_first = project(first_set)
+    got_first = row_exchange(tiles_first)
+    ends = after(ends, *tiles_first)
+    middle = (col == 1) | (col == 2)
+    second_set = jnp.concatenate(
+        [jnp.where(middle, inner, outer), jnp.where(middle, mid, ends)], 1
+    )
+    mixed_second, tiles_second = project(second_set)
+    got_second = row_exchange(tiles_second)
+    pieces = [p for pair in zip(got_first, got_second) for p in pair]
+    last_query = mixed_first[3 * wide : 3 * wide + HDIM, :tok_b]
+    last_pieces = row_gather(
+        jnp.concatenate(
+            [m[3 * wide + HDIM :].reshape(2, HDIM, -1) for m in (mixed_first, mixed_second)], 2
+        )
+    )
+    normed_set = jnp.concatenate([first_set, second_set], 1)
+    cot_tok = after(cot_tok, second_set)
+    cot_cols = lax.all_gather(cot_tok, "col")
+    cot_parts = [cot_tok] + [pick(cot_cols, col ^ s) for s in range(1, cols)]
 
     zero = jnp.int32(0)
     info = jnp.stack([row, prefix_len[0], zero, col])
     last_info = jnp.stack([row, prefix_len[0], col * tok_a + row * tok_b, col])
-    heads_out, heads_full, heads_lse = attend(info, pieces, None, tok_b, block)
+    heads_out, heads_full, heads_lse = attend(
+        info, pieces, None, tok_b, block, (up_slice, down_slice, last_pieces[1])
+    )
     last_out, last_full, last_lse = attend(last_info, last_pieces, last_query, tok_b, block)
-    attended = jnp.concatenate(
-        [
-            lax.all_to_all(heads_out, ("col", "row"), 0, 0, tiled=True).reshape(-1, tok_b),
-            last_out[0],
-        ],
-        0,
-    )
-    residual = x_tok + dot(attended, out_full, 0, 1) + narrow_all[2]
-    normed_two, centred_two, inv_two = layer_norm(residual, narrow_all[3], narrow_all[4])
-    normed_two = jnp.concatenate(row_gather(normed_two.astype(jnp.bfloat16)), 0)
-    hidden = dot(normed_two, up_slice, 1, 0) + up_slice_bias
-    active, gelu_back = jax.vjp(partial(jax.nn.gelu, approximate=False), hidden)
-    active = active.astype(jnp.bfloat16)
-    d_active = dot(cot_all, down_slice, 1, 0)
-    d_hidden = gelu_back(d_active)[0].astype(jnp.bfloat16)
-
-    def token_parts(values):
-        return [values[s * tok_b : (s + 1) * tok_b] for s in range(rows)]
-
-    d_norm_two = row_reduce(token_parts(dot(d_hidden, up_slice, 1, 1)))
-    d_residual = cot_tok.astype(jnp.float32) + layer_norm_back(
-        d_norm_two, centred_two, inv_two, narrow_all[3]
-    )
-    branch = d_residual.astype(jnp.bfloat16)
-    d_attended = dot(out_full, branch, 0, 1).astype(jnp.bfloat16)
+    heads_got = lax.all_to_all(heads_out, ("col", "row"), 0, 0, tiled=True)
+    attended, residual, normed_two = project_out(
+        info, heads_got, last_out, out_full, x_tok, cols_all
+    )
+    hidden_bias = up_bias.astype(jnp.float32)[None]
+
+    def through_hidden(normed, s):
+        return feed_forward(normed, cot_parts[s], up_slice, down_slice, hidden_bias)
+
+    near = col_send(normed_two, NEAR)
+    mid = col_send(normed_two, MIDDLE)
+    through = [through_hidden(normed_two, 0)]
+    near, mid = after([near, mid], through[0][2])
+    inner = col_send(near, MIDDLE)
+    outer = col_send(mid, OUTWARD)
+    through.append(through_hidden(near, 1))
+    inner, outer = after([inner, outer], through[1][2])
+    ends = col_send(inner, OUTWARD)
+    second = jnp.where(middle, inner, outer)
+    through.append(through_hidden(second, 2))
+    ends = after(ends, through[2][2])
+    third = jnp.where(middle, mid, ends)
+    through.append(through_hidden(third, 3))
+    d_norm_sent = [t[2] for t in through]
+    normed_two = jnp.concatenate([normed_two, near, second, third], 1)
+    cot_all = jnp.concatenate(cot_parts, 1)
+    work = {}
+
+    def weight_products(stage, arrived):
+        if stage == 0:
+            return ()
+        source, left = ((1, normed_two), (0, cot_all))[stage - 1]
+        right = jnp.concatenate(after([t[source] for t in through], arrived), 0)
+        work[stage] = right, dot(left, right, 1, 0).astype(jnp.bfloat16)
+        return (work[stage][1],)
+
+    d_norm_two = line_reduce(d_norm_sent, weight_products)
+    (low_hidden, up_part), (low_active, down_part) = work[1], work[2]
+    d_residual, branch, second_sums, d_attended = second_norm_back(
+        info, d_norm_two, residual, cot_tok, cols_all, out_full
+    )
     d_heads = lax.all_to_all(
         d_attended[: D - HDIM].reshape(rows * cols, HDIM, tok_b), ("col", "row"), 0, 0, tiled=True
     )
@@ -924,69 +1360,92 @@
         block,
     )
     head_grads = attend_back(info, pieces, None, heads_full, heads_lse, d_heads, tok_b, block)
-    d_last_keys = row_reduce([after(g, d_heads) for g in last_grads]).astype(jnp.bfloat16)
-
-    partial_out = dot(after(active, d_heads), down_slice, 1, 1)
-    block_output = to_features(
-        (row_reduce(token_parts(partial_out)) + residual + narrow_all[5]).astype(jnp.bfloat16)
-    )
-
-    def hidden_grad(left, right):
-        whole = dot(left, right, 0, 0).reshape(rows, feat, hidden_len)
-        half = dp_scatter(whole, dp, 1)
-        return jnp.stack(
-            in_order(row_exchange([pick(half, row ^ s) for s in range(rows)]), row)
-        )
-
-    up_half = lax.psum_scatter(
-        hidden_grad(normed_two, d_hidden), "col", scatter_dimension=0
-    )
-    up_grad = dp_gather(up_half, dp, 0).astype(jnp.float32)
-    out_part = dp_scatter(dot(branch, attended, 0, 1).reshape(rows, feat, -1), dp, 1)
-    out_sum = row_reduce([pick(out_part, row ^ s) for s in range(rows)]).astype(jnp.bfloat16)
-    out_got = out_sum.reshape(feat // 2, cols, -1).transpose(1, 0, 2)
-    down_out_half = lax.psum_scatter(
-        jnp.concatenate([hidden_grad(cot_all, active), out_got], 2), "col", scatter_dimension=0
-    )
-    down_out_grad = dp_gather(down_out_half, dp, 0).astype(jnp.float32)
-
-    got = jnp.stack(in_order(row_exchange(list(head_grads)), row), 1)
-    d_mixed = jnp.concatenate(
+    d_last_parts = row_reduce_parts(last_grads)
+
+    up_down_part = jnp.stack(
+        [p.reshape(rows, feat, hidden_len) for p in (up_part, down_part)], 1
+    )
+    up_down_half = lax.psum_scatter(up_down_part, "row", scatter_dimension=0)
+    active_parts = after(low_active, d_attended).reshape(cols, tok_b, hidden_len)
+    partial_out = jnp.stack(
         [
-            got.reshape(3 * wide, tok_a),
-            jnp.concatenate(
-                [d_last_query, jnp.zeros((HDIM, tok_a - tok_b), jnp.bfloat16)], 1
-            ),
-            d_last_keys.reshape(2 * HDIM, tok_a),
-        ],
-        0,
-    )
-    d_norm_one = line_reduce(
-        [
-            dot(d_mixed[:, s * tok_b : (s + 1) * tok_b], qkv_strip, 0, 1).astype(jnp.bfloat16)
-            for s in range(cols)
-        ],
-        col,
-    )
-    qkv_part = dp_scatter(dot(normed_set, d_mixed, 0, 1).reshape(rows, feat, -1), dp, 1)
-    qkv_sum = row_reduce([pick(qkv_part, row ^ s) for s in range(rows)]).astype(jnp.bfloat16)
+            dot(down_slice, pick(active_parts, col ^ i), 1, 1).astype(jnp.bfloat16)
+            for i in range(cols)
+        ]
+    )
+    sent_out = lax.psum_scatter(partial_out, "col", scatter_dimension=0)
+    out_half = lax.psum_scatter(
+        block_products(branch, attended, feat, D).reshape(rows, feat, D),
+        "row",
+        scatter_dimension=0,
+    )
+
+    up_down_grad = pair_sum(up_down_half)
+    head_got = row_exchange(list(head_grads))
+    head_got[1] = after(head_got[1], up_down_grad)
+    d_mixed = mixed_gradient(me, head_got, d_last_query, d_last_parts)
+    d_normed_sent = [
+        dot(qkv_strip, d_mixed[:, s * tok_b : (s + 1) * tok_b], 1, 0).astype(jnp.bfloat16)
+        for s in range(cols)
+    ]
+    kept = {}
+
+    def beside(stage, arrived):
+        if stage == 0:
+            parts = row_products(me, normed_set, after(d_mixed, *d_normed_sent), rows)
+            beyond, kept["near"] = swap(parts[3], 1), swap(parts[1], 1)
+            pair = add_low(parts[2], beyond)
+            kept["own"], kept["far"] = parts[0], swap(pair, 2)
+            return (pair,)
+        kept[stage] = arrived
+        return ()
+
+    d_norm_one = line_reduce(d_normed_sent, beside)
+    arrived = [kept[1], kept[2], d_norm_one[1]]
+    near, far = after([kept["near"], kept["far"]], arrived[1])
+    total = sum(p.astype(jnp.float32) for p in (kept["own"], near, far)).astype(jnp.bfloat16)
+    both = jnp.concatenate([total, out_half], 1)
+    half = feat // 2
+    other = dp_swap(lax.dynamic_slice_in_dim(both, (1 - dp) * half, half, 0))
+    total = add_low(lax.dynamic_slice_in_dim(both, dp * half, half, 0), other)
+    sent = dot(total[:, : 3 * slots], placed, 1, 0).astype(jnp.bfloat16)
+    hd = D // cols
     got = col_exchange(
         [
-            dot(qkv_sum, placed[:, s * slots : (s + 1) * slots], 1, 0).astype(jnp.bfloat16)
+            jnp.concatenate(
+                [
+                    sent[:, s * slots : (s + 1) * slots],
+                    lax.dynamic_slice_in_dim(total, 3 * slots + (col ^ s) * hd, hd, 1),
+                ],
+                1,
+            )
             for s in range(cols)
         ]
     )
-    qkv_half = sum(
-        dot(g, spread[:, s * slots : (s + 1) * slots], 1, 1) for s, g in enumerate(got)
+    qkv = dot(jnp.concatenate([g[:, :slots] for g in got], 1), spread, 1, 1)
+    out = sum(g[:, slots:].astype(jnp.float32) for g in got)
+    last_grad = dp_gather(jnp.concatenate([qkv, out], 1).astype(jnp.bfloat16), dp, 0)
+    qkv_grad, out_grad = jnp.split(last_grad.astype(jnp.float32), [qkv_weight.shape[1]], 1)
+
+    out_value = (
+        after(sent_out, arrived[0]).astype(jnp.float32) + residual + cols_all[:, 5:6]
     ).astype(jnp.bfloat16)
-    qkv_grad = dp_gather(qkv_half, dp, 0).astype(jnp.float32)
-    input_grad = d_residual + layer_norm_back(d_norm_one, centred_one, inv_one, narrow_all[0])
-    input_grad = to_features(input_grad.astype(jnp.bfloat16)).astype(jnp.float32)
+    block_got = row_exchange(
+        [lax.dynamic_slice_in_dim(out_value, (row ^ s) * feat, feat, 0) for s in range(rows)]
+    )
+    block_output = side_by_side(me, after(block_got, arrived[1]), jnp.bfloat16)
+    *input_parts, first_sums = first_norm_back(
+        me, d_norm_one, x_tok, d_residual, cols_all, rows
+    )
+    input_grad = side_by_side(me, row_exchange(input_parts), jnp.float32)
 
     at_row = (jnp.arange(rows) == row)[:, None]
 
     def own_row(values):
         return jnp.where(at_row, values[None], 0.0).reshape(-1)
+
+    def own_col(values):
+        return jnp.where((jnp.arange(cols) == col)[:, None], values[None], 0.0).reshape(-1)
 
     bias_strip = jnp.sum(d_mixed.astype(jnp.float32), 1)
     at_col = (jnp.arange(cols) == col)[None, :, None]
@@ -996,13 +1455,13 @@
     ).reshape(-1)
     early = [
         own_row(jnp.sum(cotangent[0].astype(jnp.float32), 0)),
-        jnp.sum(branch.astype(jnp.float32), 0),
-        jnp.sum(d_norm_two * centred_two, 0),
-        jnp.sum(d_norm_two, 0),
-        own_row(jnp.sum(d_hidden.astype(jnp.float32), 0)),
+        second_sums[:, 2],
+        second_sums[:, 0],
+        second_sums[:, 1],
+        own_col(jnp.sum(low_hidden.astype(jnp.float32), 0)),
         bias_all,
-        jnp.sum(d_norm_one * centred_one, 0),
-        jnp.sum(d_norm_one, 0),
+        first_sums[:, 0],
+        first_sums[:, 1],
     ]
     total = sum_everywhere(jnp.concatenate(early).reshape(8, -1)).reshape(-1)
 
@@ -1011,22 +1470,22 @@
 
     width = rows * feat
     up_at = 4 * width
-    qkv_at = up_at + rows * hidden_len
+    qkv_at = up_at + cols * hidden_len
     first_at = qkv_at + 3 * width
     return (
-        block_output[None],
-        input_grad[None],
+        block_output.T[None],
+        input_grad.T[None],
         own_part(first_at, feat, row),
         own_part(first_at + width, feat, row),
         qkv_grad,
         own_part(qkv_at, 3 * width // cols, col),
-        down_out_grad[:, hidden_len:].T,
+        out_grad.T,
         own_part(width, feat, row),
         own_part(2 * width, feat, row),
         own_part(3 * width, feat, row),
-        up_grad,
+        up_down_grad[0],
         own_part(up_at, hidden_len, col),
-        down_out_grad[:, :hidden_len].T,
+        up_down_grad[1].T,
         own_part(0, feat, row),
     )
 

time: 655 us -> 561 us (0.86)
  Pallas kernels: 67.4 us -> 151 us
  matrix products: 93.7 us -> 32.1 us
  waiting for transfers between devices: 204 us -> 164 us
  other arithmetic: 60.3 us -> 35.9 us
  starting transfers between devices: 110 us -> 89.2 us
  blocking collectives: 18.9 us -> 0 us
  local copies, waits for them, and re-layouts: 77.8 us -> 63.8 us
    pallas_call x2 -> x44, Pallas kernels: 29.6 us -> 107 us  [the longest x16 68.2 us: small_kernel(): pl.pallas_call(body, out_shape=out_shape, in_specs=[IN_SMEM] * scalars +...]
    dot_general x27 -> x16, matrix products: 93.7 us -> 32.1 us  [dot(): lax.dot_general(left, right, (((left_dim,), (right_dim,)), ((), ())), pre...]
    ppermute x63 -> x33, waiting for transfers between devices: 113 us -> 60.1 us  [swap(): return lax.ppermute(value, 'row', [(i, i ^ step) for i in range(size)])]
    ppermute x16 -> x26, waiting for transfers between devices: 45.4 us -> 81.9 us  [col_send(): return lax.ppermute(value, 'col', pairs)]
    ppermute x63 -> x33, starting transfers between devices: 42.3 us -> 20.6 us  [swap(): return lax.ppermute(value, 'row', [(i, i ^ step) for i in range(size)])]
    ppermute x10 -> x4, waiting for transfers between devices: 34 us -> 12.8 us  [dp_swap(): return lax.ppermute(value, 'dp', [(0, 1), (1, 0)])]
    all_gather x1 -> x0, blocking collectives: 18.9 us -> none  [head_shards(): out_cols = lax.all_gather(out_weight.T, 'col')]
    ppermute x16 -> x26, starting transfers between devices: 30.8 us -> 48.6 us  [col_send(): return lax.ppermute(value, 'col', pairs)]
  transfers between devices with their start and end apart: 99 -> 75, of which waited for: 34 -> 28; matrix products, arithmetic and copies ran while one was open for 32% -> 15% of each run, Pallas kernels for 10% -> 26%
where the time goes in v2:
time: 561 us; the launch traced here: 554 us
  waiting for transfers between devices  164 us (29%)
  Pallas kernels  151 us (27%)
  starting transfers between devices  89.2 us (16%)
  local copies, waits for them, and re-layouts  63.8 us (11%)
  other arithmetic  35.9 us (6%)
  matrix products  32.1 us (6%)
  between operations  17.1 us (3%)
    ppermute x26, waiting for transfers between devices, col_send(): return lax.ppermute(value, 'col', pairs)  81.9 us
    pallas_call x16, Pallas kernels, small_kernel(): pl.pallas_call(body, out_shape=out_shape, in_specs=[IN_SMEM] * scalars +...  68.2 us
    ppermute x33, waiting for transfers between devices, swap(): return lax.ppermute(value, 'row', [(i, i ^ step) for i in range(size)])  60.1 us
    ppermute x26, starting transfers between devices, col_send(): return lax.ppermute(value, 'col', pairs)  48.6 us
    pallas_call x2, Pallas kernels, attend_back(): pl.pallas_call(partial(backward_kernel, len(pieces), own, tok_b, block),...  43.9 us
    pallas_call x2, Pallas kernels, attend(): pl.pallas_call(partial(forward_kernel, len(pieces), own, len(earlier), to...  34.7 us
    unnamed x279, local copies, waits for them, and re-layouts  34.4 us
    dot_general x16, matrix products, dot(): lax.dot_general(left, right, (((left_dim,), (right_dim,)), ((), ())), pre...  32.1 us
  transfers between devices with their start and end apart: 75, of which 28 were waited for; matrix products, arithmetic and copies ran while one was open for 15% of the time, Pallas kernels for 26%

profile of v2, /device:TPU:0, one launch (start us, length us, event | category | flops | bytes accessed | tf_op | source)
XLA Modules:
  0.0 553.7 jit_solution(7716202006222406688)
XLA Ops:
  8.4 2.7 pad_maximum_fusion.3
  11.9 2.2 shard_map.272
  17.9 4.7 collective-permute-start.3
  25.1 7.0 %collective-permute-done.3.refs_3_ = bf16[288,592]{1,0:T(8,128)(2,1)S(1)} collective-permute-done((bf16[288,592]{1,0:T(8,128)(2,1)S(1)}, bf16[288,592]{1,0:T(8,128)(2,1)S(1)}, u32[]{:S(2)}, u32[]{:S(2)}) %collective-permute-start.3) | collective-permute-done | bytes 341024 | tf_op jit(solution)/shard_map/ppermute | solution.py:682
  32.1 8.8 %collective-permute-done.1.refs_1_ = bf16[288,592]{1,0:T(8,128)(2,1)S(1)} collective-permute-done((bf16[288,592]{1,0:T(8,128)(2,1)S(1)}, bf16[288,592]{1,0:T(8,128)(2,1)S(1)}, u32[]{:S(2)}, u32[]{:S(2)}) %collective-permute-start.1) | collective-permute-done | bytes 341024 | tf_op jit(solution)/shard_map/ppermute | solution.py:682
  40.8 13.8 %collective-permute-done.2.refs_2_ = bf16[288,592]{1,0:T(8,128)(2,1)S(1)} collective-permute-done((bf16[288,592]{1,0:T(8,128)(2,1)S(1)}, bf16[288,592]{1,0:T(8,128)(2,1)S(1)}, u32[]{:S(2)}, u32[]{:S(2)}) %collective-permute-start.2) | collective-permute-done | bytes 341024 | tf_op jit(solution)/shard_map/ppermute | solution.py:682
  56.2 3.2 shard_map.274
  62.5 2.0 shard_map.276
  71.2 2.2 collective-permute-done.10.refs_4_
  77.5 2.1 fusion.28.refs_0_
  84.5 23.8 %collective-permute-done.14.refs_3_ = bf16[288,960]{1,0:T(8,128)(2,1)S(1)} collective-permute-done((bf16[288,960]{1,0:T(8,128)(2,1)S(1)}, bf16[288,960]{1,0:T(8,128)(2,1)S(1)}, u32[]{:S(2)}, u32[]{:S(2)}) %collective-permute-start.14) | collective-permute-done | bytes 552992 | tf_op jit(solution)/shard_map/ppermute | solution.py:381
  113.8 3.2 shard_map.280
  117.0 3.1 multiply_convert_fusion.1
  123.1 4.3 collective-permute-done.16.refs_0_
  129.4 3.3 multiply_convert_fusion
  136.8 5.0 fusion.64
  141.9 4.2 collective-permute-done.20.refs_5_
  147.0 30.4 %shard_map.282 = (bf16[16,64,256]{2,1,0:T(8,128)(2,1)}, f32[16,64,256]{2,1,0:T(8,128)}, f32[8,1,512]{2,1,0:T(1,128)}) custom-call(s32[4]{0:T(128)} %add_add_fusion.info, bf16[3,64,512]{2,1,0:T(8,128)(2,1)} %get-tuple-element.261.refs_1_.refs_0_, bf16[3,64,512]{2,1,0:T(8,128)(2,1)} %get-tuple-element.257.refs_1_, ...), custom_call_target="tpu_custom_call" | custom-call | flops 28521267200 | bytes 4194304 | tf_op jit(solution)/shard_map/pallas_call | solution.py:523
  177.4 4.9 all-to-all-start
  182.3 2.0 collective-permute-start.24
  184.3 11.7 %collective-permute-done.24.refs_2_ = bf16[2,64,1024]{2,1,0:T(8,128)(2,1)S(1)} collective-permute-done((bf16[2,64,1024]{2,1,0:T(8,128)(2,1)S(1)}, bf16[2,64,1024]{2,1,0:T(8,128)(2,1)S(1)}, u32[]{:S(2)}, u32[]{:S(2)}) %collective-permute-start.24) | collective-permute-done | bytes 262176 | tf_op jit(solution)/shard_map/ppermute | solution.py:381
  198.2 4.3 shard_map.283
  203.3 5.2 shard_map.284
  209.4 5.0 collective-permute-start.26
  215.0 6.8 %shard_map.286 = (bf16[256,1088]{1,0:T(8,128)(2,1)}, bf16[256,1088]{1,0:T(8,128)(2,1)}, bf16[1088,256]{1,0:T(8,128)(2,1)}) custom-call(bf16[1088,256]{1,0:T(8,128)(2,1)} %get-tuple-element.133.n_ref, bf16[1088,256]{1,0:T(8,128)(2,1)} %shard_map.285.cot_ref.refs_4_, bf16[1088,1088]{1,0:T(8,128)(2,1)} %bitcast.140, bf16[1088,1088]{1,0:T(8,128)(2,1)} %bitcast.131, ...), custom_call_target="tpu_custom_call" | custom-call | flops 3030384640 | bytes 7524608 | tf_op jit(solution)/shard_map/pallas_call | solution.py:770
  221.8 5.5 collective-permute-done.26.refs_0_
  230.1 2.6 dynamic-slice_bitcast_fusion
  232.8 6.8 %shard_map.288 = (bf16[256,1088]{1,0:T(8,128)(2,1)}, bf16[256,1088]{1,0:T(8,128)(2,1)}, bf16[1088,256]{1,0:T(8,128)(2,1)}) custom-call(bf16[1088,256]{1,0:T(8,128)(2,1)} %get-tuple-element.136.n_ref, bf16[1088,256]{1,0:T(8,128)(2,1)} %get-tuple-element.253.cot_ref, bf16[1088,1088]{1,0:T(8,128)(2,1)} %bitcast.141, bf16[1088,1088]{1,0:T(8,128)(2,1)} %bitcast.132, ...), custom_call_target="tpu_custom_call" | custom-call | flops 3030384640 | bytes 7524608 | tf_op jit(solution)/shard_map/pallas_call | solution.py:770
  239.5 4.6 collective-permute-done.29.refs_1_
  248.8 6.8 %shard_map.290 = (bf16[256,1088]{1,0:T(8,128)(2,1)}, bf16[256,1088]{1,0:T(8,128)(2,1)}, bf16[1088,256]{1,0:T(8,128)(2,1)}) custom-call(bf16[1088,256]{1,0:T(8,128)(2,1)} %broadcast_select_fusion.1.n_ref, bf16[1088,256]{1,0:T(8,128)(2,1)} %get-tuple-element.252.cot_ref, bf16[1088,1088]{1,0:T(8,128)(2,1)} %bitcast.142, bf16[1088,1088]{1,0:T(8,128)(2,1)} %bitcast.133, ...), custom_call_target="tpu_custom_call" | custom-call | flops 3030384640 | bytes 7524608 | tf_op jit(solution)/shard_map/pallas_call | solution.py:770
  255.6 5.4 collective-permute-done.30.refs_0_
  263.8 6.8 %shard_map.292 = (bf16[256,1088]{1,0:T(8,128)(2,1)}, bf16[256,1088]{1,0:T(8,128)(2,1)}, bf16[1088,256]{1,0:T(8,128)(2,1)}) custom-call(bf16[1088,256]{1,0:T(8,128)(2,1)} %broadcast_select_fusion.n_ref, bf16[1088,256]{1,0:T(8,128)(2,1)} %get-tuple-element.251.cot_ref, bf16[1088,1088]{1,0:T(8,128)(2,1)} %bitcast.143, bf16[1088,1088]{1,0:T(8,128)(2,1)} %bitcast.134, ...), custom_call_target="tpu_custom_call" | custom-call | flops 3030384640 | bytes 7524608 | tf_op jit(solution)/shard_map/pallas_call | solution.py:770
  272.0 10.1 %collective-permute-done.31.refs_0_ = bf16[1088,256]{1,0:T(8,128)(2,1)S(1)} collective-permute-done((bf16[1088,256]{1,0:T(8,128)(2,1)}, bf16[1088,256]{1,0:T(8,128)(2,1)S(1)}, u32[]{:S(2)}, u32[]{:S(2)}) %collective-permute-start.31) | collective-permute-done | bytes 557088 | tf_op jit(solution)/shard_map/ppermute | solution.py:682
  284.8 7.1 %collective-permute-start.33 = (bf16[1088,256]{1,0:T(8,128)(2,1)}, bf16[1088,256]{1,0:T(8,128)(2,1)S(1)}, u32[]{:S(2)}, u32[]{:S(2)}) collective-permute-start(bf16[1088,256]{1,0:T(8,128)(2,1)} %shard_map.294), channel_id=1, source_target_pairs={{0,1},{3,2},{4,5},{7,6},{8,9},{11,10},{12,13},{15,14},{16,17},{19,... | collective-permute-start | bytes 1671176 | tf_op jit(solution)/shard_map/ppermute | solution.py:682
  294.6 4.3 convolution_convert_fusion.1.refs_2_
  305.1 3.3 convolution_convert_fusion.refs_2_
  308.4 3.0 pad_maximum_fusion
  313.1 2.4 collective-permute-start.34
  316.4 7.6 %collective-permute-done.34.refs_0_ = bf16[1088,256]{1,0:T(8,128)(2,1)S(1)} collective-permute-done((bf16[1088,256]{1,0:T(8,128)(2,1)S(1)}, bf16[1088,256]{1,0:T(8,128)(2,1)S(1)}, u32[]{:S(2)}, u32[]{:S(2)}) %collective-permute-start.34) | collective-permute-done | bytes 557088 | tf_op jit(solution)/shard_map/ppermute | solution.py:682
  325.6 6.7 %shard_map.299 = (f32[1088,256]{1,0:T(8,128)}, bf16[1088,256]{1,0:T(8,128)(2,1)}, f32[1088,3]{1,0:T(8,128)}, bf16[1088,256]{1,0:T(8,128)(2,1)}) custom-call(s32[4]{0:T(128)} %add_add_fusion.info, bf16[1088,256]{1,0:T(8,128)(2,1)} %get-tuple-element.135.refs_2_.refs_1_.refs_0_, bf16[1088,256]{1,0:T(8,128)(2,1)} %get-tuple-element.160.refs_1_, ...), custom_call_target="tpu_custom_call" | custom-call | bytes 7985920 | tf_op jit(solution)/shard_map/pallas_call | solution.py:770
  334.0 2.1 fusion.8
  342.9 5.0 all-to-all-start.1
  348.5 5.6 %shard_map.303 = (bf16[2,64,1024]{2,1,0:T(8,128)(2,1)}, bf16[2,64,1024]{2,1,0:T(8,128)(2,1)}, bf16[2,64,1024]{2,1,0:T(8,128)(2,1)}, bf16[2,64,1024]{2,1,0:T(8,128)(2,1)}, bf16[64,256]{1,0:T(8,128)(2,1)}) custom-call(s32[4]{0:T(128)} %add_add_fusion.1.info, bf16[2,64,1024]{2,1,0:T(8,128)(2,1)} %copy-done.104, bf16[2,64,1024]{2,1,0:T(8,128)(2,1)} %copy-done.125, ...), custom_call_target="tpu_custom_call" | custom-call | flops 2306867200 | bytes 4194304 | tf_op jit(solution)/shard_map/pallas_call | solution.py:643
  357.6 3.7 shard_map.317
  362.8 3.5 reduce-scatter.6.cloned.1.call-done
  366.2 3.6 collective-permute-start.37
  370.7 38.3 %shard_map.301 = (bf16[3,64,1024]{2,1,0:T(8,128)(2,1)}, bf16[3,64,1024]{2,1,0:T(8,128)(2,1)}, bf16[3,64,1024]{2,1,0:T(8,128)(2,1)}, bf16[3,64,1024]{2,1,0:T(8,128)(2,1)}) custom-call(s32[4]{0:T(128)} %add_add_fusion.info, bf16[3,64,512]{2,1,0:T(8,128)(2,1)} %get-tuple-element.261.refs_1_.refs_0_, bf16[3,64,512]{2,1,0:T(8,128)(2,1)} %get-tuple-element.257.refs_1_, ...), custom_call_target="tpu_custom_call" | custom-call | flops 36909875200 | bytes 4194304 | tf_op jit(solution)/shard_map/pallas_call | solution.py:643
  413.3 7.8 %collective-permute-done.38.refs_2_ = bf16[3,64,1024]{2,1,0:T(8,128)(2,1)S(1)} collective-permute-done((bf16[3,64,1024]{2,1,0:T(8,128)(2,1)}, bf16[3,64,1024]{2,1,0:T(8,128)(2,1)S(1)}, u32[]{:S(2)}, u32[]{:S(2)}) %collective-permute-start.38) | collective-permute-done | bytes 393248 | tf_op jit(solution)/shard_map/ppermute | solution.py:381
  421.2 7.5 %collective-permute-done.39.refs_3_ = bf16[3,64,1024]{2,1,0:T(8,128)(2,1)S(1)} collective-permute-done((bf16[3,64,1024]{2,1,0:T(8,128)(2,1)}, bf16[3,64,1024]{2,1,0:T(8,128)(2,1)S(1)}, u32[]{:S(2)}, u32[]{:S(2)}) %collective-permute-start.39) | collective-permute-done | bytes 393248 | tf_op jit(solution)/shard_map/ppermute | solution.py:381
  429.4 3.1 shard_map.304.refs_0_
  434.4 3.4 collective-permute-start.43
  443.0 5.6 %shard_map.306 = (bf16[272,960]{1,0:T(8,128)(2,1)}, bf16[272,960]{1,0:T(8,128)(2,1)}, bf16[272,960]{1,0:T(8,128)(2,1)}, bf16[272,960]{1,0:T(8,128)(2,1)}) custom-call(s32[1]{0:T(128)} %bitcast.info, bf16[1088,1024]{1,0:T(8,128)(2,1)} %pad_maximum_fusion.2.left_ref, bf16[960,1024]{1,0:T(8,128)(2,1)} %shard_map.305.right_ref), custom_call_target="tpu_custom_call" | custom-call | bytes 6283264 | tf_op jit(solution)/shard_map/pallas_call | solution.py:770
  453.7 2.0 add_convert_fusion.4
  456.4 3.3 collective-permute-start.49
  459.9 11.9 %collective-permute-done.49.refs_1_ = bf16[1088,256]{1,0:T(8,128)(2,1)S(1)} collective-permute-done((bf16[1088,256]{1,0:T(8,128)(2,1)}, bf16[1088,256]{1,0:T(8,128)(2,1)S(1)}, u32[]{:S(2)}, u32[]{:S(2)}) %collective-permute-start.49) | collective-permute-done | bytes 557088 | tf_op jit(solution)/shard_map/ppermute | solution.py:682
  477.6 2.4 collective-permute-start.50
  481.2 9.7 %collective-permute-done.62 = bf16[136,2048]{1,0:T(8,128)(2,1)S(1)} collective-permute-done((bf16[136,2048]{1,0:T(8,128)(2,1)S(1)}, bf16[136,2048]{1,0:T(8,128)(2,1)S(1)}, u32[]{:S(2)}, u32[]{:S(2)}) %collective-permute-start.62) | collective-permute-done | bytes 557088 | tf_op jit(solution)/shard_map/ppermute | solution.py:678
  493.4 2.4 collective-permute-start.63
  501.3 4.5 shard_map.314
  518.9 2.0 fusion.29
  524.9 3.1 collective-permute-done.58
  533.0 2.0 shard_map.312
  535.6 2.2 shard_map.315
  537.8 3.1 collective-permute-done.59
  (546 shorter events, 150.0 us)
Async XLA Ops:
  7.2 129.6 %all-gather.7.cloned.1.call-start = ((), (), s32[]{:S(2)}) async-start(), calls=%async_computation.8 | async-start | bytes 6266880 | tf_op jit(solution)/shard_map/all_gather | solution.py:1257
  11.1 191.4 %all-gather.9.cloned.1.call-start = ((), (), s32[]{:S(2)}) async-start(), calls=%async_computation.9 | async-start | bytes 4177920 | tf_op jit(solution)/shard_map/all_gather | solution.py:1261
  14.1 10.7 %collective-permute-start = (bf16[272,384]{1,0:T(8,128)(2,1)}, bf16[272,384]{1,0:T(8,128)(2,1)S(1)}, u32[]{:S(2)}, u32[]{:S(2)}) collective-permute-start(bf16[272,384]{1,0:T(8,128)(2,1)} %get-tuple-element.107), channel_id=1, source_target_pairs={{0,4},{4,0},{8,12},{12,8},{1,5},{5,1},{9,13},{13,9},{2,6},{6,2},{1... | collective-permute-start | bytes 626696 | tf_op jit(solution)/shard_map/ppermute | solution.py:381
  17.9 14.2 %collective-permute-start.3 = (bf16[288,592]{1,0:T(8,128)(2,1)S(1)}, bf16[288,592]{1,0:T(8,128)(2,1)S(1)}, u32[]{:S(2)}, u32[]{:S(2)}) collective-permute-start(bf16[288,592]{1,0:T(8,128)(2,1)S(1)} %get-tuple-element.279), channel_id=1, source_target_pairs={{0,3},{1,2},{2,1},{3,0},{4,7},{5,6},{6,5},{7,4},{8,11},{9,10},{10,... | collective-permute-start | bytes 1022984 | tf_op jit(solution)/shard_map/ppermute | solution.py:682
  22.5 18.3 %collective-permute-start.1 = (bf16[288,592]{1,0:T(8,128)(2,1)S(1)}, bf16[288,592]{1,0:T(8,128)(2,1)S(1)}, u32[]{:S(2)}, u32[]{:S(2)}) collective-permute-start(bf16[288,592]{1,0:T(8,128)(2,1)S(1)} %get-tuple-element.280), channel_id=1, source_target_pairs={{0,1},{1,0},{2,3},{3,2},{4,5},{5,4},{6,7},{7,6},{8,9},{9,8},{10,11... | collective-permute-start | bytes 1022984 | tf_op jit(solution)/shard_map/ppermute | solution.py:682
  22.6 32.1 %collective-permute-start.2 = (bf16[288,592]{1,0:T(8,128)(2,1)S(1)}, bf16[288,592]{1,0:T(8,128)(2,1)S(1)}, u32[]{:S(2)}, u32[]{:S(2)}) collective-permute-start(bf16[288,592]{1,0:T(8,128)(2,1)S(1)} %get-tuple-element.281), channel_id=1, source_target_pairs={{0,2},{1,3},{2,0},{3,1},{4,6},{5,7},{6,4},{7,5},{8,10},{9,11},{10,... | collective-permute-start | bytes 1022984 | tf_op jit(solution)/shard_map/ppermute | solution.py:682
  23.2 32.2 %collective-permute-start.4 = (bf16[272,384]{1,0:T(8,128)(2,1)S(1)}, bf16[272,384]{1,0:T(8,128)(2,1)S(1)}, u32[]{:S(2)}, u32[]{:S(2)}) collective-permute-start(bf16[272,384]{1,0:T(8,128)(2,1)S(1)} %copy-done.129), channel_id=1, source_target_pairs={{0,8},{4,12},{8,0},{12,4},{1,9},{5,13},{9,1},{13,5},{2,10},{6,14},... | collective-permute-start | bytes 626696 | tf_op jit(solution)/shard_map/ppermute | solution.py:381
  24.8 30.6 %collective-permute-start.5 = (bf16[272,384]{1,0:T(8,128)(2,1)S(1)}, bf16[272,384]{1,0:T(8,128)(2,1)S(1)}, u32[]{:S(2)}, u32[]{:S(2)}) collective-permute-start(bf16[272,384]{1,0:T(8,128)(2,1)S(1)} %copy-done.128), channel_id=1, source_target_pairs={{0,12},{4,8},{8,4},{12,0},{1,13},{5,9},{9,5},{13,1},{2,14},{6,10},... | collective-permute-start | bytes 626696 | tf_op jit(solution)/shard_map/ppermute | solution.py:381
  59.4 14.1 %collective-permute-start.7 = (bf16[1088,256]{1,0:T(8,128)(2,1)}, bf16[1088,256]{1,0:T(8,128)(2,1)S(1)}, u32[]{:S(2)}, u32[]{:S(2)}) collective-permute-start(bf16[1088,256]{1,0:T(8,128)(2,1)} %get-tuple-element.115.refs_1_), channel_id=1, source_target_pairs={{1,2},{2,1},{5,6},{6,5},{9,10},{10,9},{13,14},{14,13},{17,18},{18,... | collective-permute-start | bytes 1671176 | tf_op jit(solution)/shard_map/ppermute | solution.py:682
  60.1 14.5 %collective-permute-start.6 = (bf16[1088,256]{1,0:T(8,128)(2,1)}, bf16[1088,256]{1,0:T(8,128)(2,1)S(1)}, u32[]{:S(2)}, u32[]{:S(2)}) collective-permute-start(bf16[1088,256]{1,0:T(8,128)(2,1)} %get-tuple-element.115.refs_1_), channel_id=1, source_target_pairs={{0,1},{1,0},{2,3},{3,2},{4,5},{5,4},{6,7},{7,6},{8,9},{9,8},{10,11... | collective-permute-start | bytes 1671176 | tf_op jit(solution)/shard_map/ppermute | solution.py:682
  66.1 7.4 %collective-permute-start.10 = (bf16[272,256]{1,0:T(8,128)(2,1)}, bf16[272,256]{1,0:T(8,128)(2,1)S(1)}, u32[]{:S(2)}, u32[]{:S(2)}) collective-permute-start(bf16[272,256]{1,0:T(8,128)(2,1)} %get-tuple-element.118), channel_id=1, source_target_pairs={{0,12},{4,8},{8,4},{12,0},{1,13},{5,9},{9,5},{13,1},{2,14},{6,10},... | collective-permute-start | bytes 417800 | tf_op jit(solution)/shard_map/ppermute | solution.py:381
  67.7 162.4 %all-gather.11.cloned.1.call-start = ((), (), s32[]{:S(2)}) async-start(), calls=%async_computation.10 | async-start | bytes 2785280 | tf_op jit(solution)/shard_map/all_gather | solution.py:1298
  75.5 32.8 %collective-permute-start.12 = (bf16[1088,256]{1,0:T(8,128)(2,1)}, bf16[1088,256]{1,0:T(8,128)(2,1)S(1)}, u32[]{:S(2)}, u32[]{:S(2)}) collective-permute-start(bf16[1088,256]{1,0:T(8,128)(2,1)} %get-tuple-element.120), channel_id=1, source_target_pairs={{1,0},{2,3},{5,4},{6,7},{9,8},{10,11},{13,12},{14,15},{17,16},{18,... | collective-permute-start | bytes 1671176 | tf_op jit(solution)/shard_map/ppermute | solution.py:682
  76.8 31.5 %collective-permute-start.11 = (bf16[1088,256]{1,0:T(8,128)(2,1)}, bf16[1088,256]{1,0:T(8,128)(2,1)S(1)}, u32[]{:S(2)}, u32[]{:S(2)}) collective-permute-start(bf16[1088,256]{1,0:T(8,128)(2,1)} %get-tuple-element.119), channel_id=1, source_target_pairs={{1,2},{2,1},{5,6},{6,5},{9,10},{10,9},{13,14},{14,13},{17,18},{18,... | collective-permute-start | bytes 1671176 | tf_op jit(solution)/shard_map/ppermute | solution.py:682
  79.6 28.6 %collective-permute-start.14 = (bf16[288,960]{1,0:T(8,128)(2,1)S(1)}, bf16[288,960]{1,0:T(8,128)(2,1)S(1)}, u32[]{:S(2)}, u32[]{:S(2)}) collective-permute-start(bf16[288,960]{1,0:T(8,128)(2,1)S(1)} %fusion.28.refs_0_), channel_id=1, source_target_pairs={{0,8},{4,12},{8,0},{12,4},{1,9},{5,13},{9,1},{13,5},{2,10},{6,14},... | collective-permute-start | bytes 1658888 | tf_op jit(solution)/shard_map/ppermute | solution.py:381
  81.2 27.0 %collective-permute-start.13 = (bf16[288,960]{1,0:T(8,128)(2,1)S(1)}, bf16[288,960]{1,0:T(8,128)(2,1)S(1)}, u32[]{:S(2)}, u32[]{:S(2)}) collective-permute-start(bf16[288,960]{1,0:T(8,128)(2,1)S(1)} %fusion.28.refs_0_), channel_id=1, source_target_pairs={{0,4},{4,0},{8,12},{12,8},{1,5},{5,1},{9,13},{13,9},{2,6},{6,2},{1... | collective-permute-start | bytes 1658888 | tf_op jit(solution)/shard_map/ppermute | solution.py:381
  110.3 17.1 %collective-permute-start.16 = (bf16[1088,256]{1,0:T(8,128)(2,1)}, bf16[1088,256]{1,0:T(8,128)(2,1)S(1)}, u32[]{:S(2)}, u32[]{:S(2)}) collective-permute-start(bf16[1088,256]{1,0:T(8,128)(2,1)} %get-tuple-element.127), channel_id=1, source_target_pairs={{1,0},{2,3},{5,4},{6,7},{9,8},{10,11},{13,12},{14,15},{17,16},{18,... | collective-permute-start | bytes 1671176 | tf_op jit(solution)/shard_map/ppermute | solution.py:682
  121.0 15.3 %collective-permute-start.21 = (bf16[3,64,512]{2,1,0:T(8,128)(2,1)S(1)}, bf16[3,64,512]{2,1,0:T(8,128)(2,1)}, u32[]{:S(2)}, u32[]{:S(2)}) collective-permute-start(bf16[3,64,512]{2,1,0:T(8,128)(2,1)S(1)} %get-tuple-element.258.refs_4_), channel_id=1, source_target_pairs={{0,12},{4,8},{8,4},{12,0},{1,13},{5,9},{9,5},{13,1},{2,14},{6,10},... | collective-permute-start | bytes 589832 | tf_op jit(solution)/shard_map/ppermute | solution.py:381
  121.9 14.8 %collective-permute-start.19 = (bf16[3,64,512]{2,1,0:T(8,128)(2,1)S(1)}, bf16[3,64,512]{2,1,0:T(8,128)(2,1)}, u32[]{:S(2)}, u32[]{:S(2)}) collective-permute-start(bf16[3,64,512]{2,1,0:T(8,128)(2,1)S(1)} %get-tuple-element.259.refs_3_), channel_id=1, source_target_pairs={{0,8},{4,12},{8,0},{12,4},{1,9},{5,13},{9,1},{13,5},{2,10},{6,14},... | collective-permute-start | bytes 589832 | tf_op jit(solution)/shard_map/ppermute | solution.py:381
  123.1 18.8 %collective-permute-start.17 = (bf16[3,64,512]{2,1,0:T(8,128)(2,1)S(1)}, bf16[3,64,512]{2,1,0:T(8,128)(2,1)}, u32[]{:S(2)}, u32[]{:S(2)}) collective-permute-start(bf16[3,64,512]{2,1,0:T(8,128)(2,1)S(1)} %get-tuple-element.260.refs_2_), channel_id=1, source_target_pairs={{0,4},{4,0},{8,12},{12,8},{1,5},{5,1},{9,13},{13,9},{2,6},{6,2},{1... | collective-permute-start | bytes 589832 | tf_op jit(solution)/shard_map/ppermute | solution.py:381
  134.7 7.2 %collective-permute-start.22 = (bf16[3,64,512]{2,1,0:T(8,128)(2,1)S(1)}, bf16[3,64,512]{2,1,0:T(8,128)(2,1)S(1)}, u32[]{:S(2)}, u32[]{:S(2)}) collective-permute-start(bf16[3,64,512]{2,1,0:T(8,128)(2,1)S(1)} %get-tuple-element.254), channel_id=1, source_target_pairs={{0,12},{4,8},{8,4},{12,0},{1,13},{5,9},{9,5},{13,1},{2,14},{6,10},... | collective-permute-start | bytes 589832 | tf_op jit(solution)/shard_map/ppermute | solution.py:381
  135.0 11.1 %collective-permute-start.20 = (bf16[3,64,512]{2,1,0:T(8,128)(2,1)S(1)}, bf16[3,64,512]{2,1,0:T(8,128)(2,1)S(1)}, u32[]{:S(2)}, u32[]{:S(2)}) collective-permute-start(bf16[3,64,512]{2,1,0:T(8,128)(2,1)S(1)} %get-tuple-element.255), channel_id=1, source_target_pairs={{0,8},{4,12},{8,0},{12,4},{1,9},{5,13},{9,1},{13,5},{2,10},{6,14},... | collective-permute-start | bytes 589832 | tf_op jit(solution)/shard_map/ppermute | solution.py:381
  136.3 9.9 %collective-permute-start.18 = (bf16[3,64,512]{2,1,0:T(8,128)(2,1)S(1)}, bf16[3,64,512]{2,1,0:T(8,128)(2,1)S(1)}, u32[]{:S(2)}, u32[]{:S(2)}) collective-permute-start(bf16[3,64,512]{2,1,0:T(8,128)(2,1)S(1)} %get-tuple-element.256), channel_id=1, source_target_pairs={{0,4},{4,0},{8,12},{12,8},{1,5},{5,1},{9,13},{13,9},{2,6},{6,2},{1... | collective-permute-start | bytes 589832 | tf_op jit(solution)/shard_map/ppermute | solution.py:381
  136.7 9.4 %collective-permute-start.23 = (bf16[2,64,1024]{2,1,0:T(8,128)(2,1)S(1)}, bf16[2,64,1024]{2,1,0:T(8,128)(2,1)S(1)}, u32[]{:S(2)}, u32[]{:S(2)}) collective-permute-start(bf16[2,64,1024]{2,1,0:T(8,128)(2,1)S(1)} %pad_maximum_fusion.10.refs_0_), channel_id=1, source_target_pairs={{0,4},{4,0},{8,12},{12,8},{1,5},{5,1},{9,13},{13,9},{2,6},{6,2},{1... | collective-permute-start | bytes 786440 | tf_op jit(solution)/shard_map/ppermute | solution.py:381
  177.4 25.2 %all-to-all-start = ((bf16[16,64,256]{2,1,0:T(8,128)(2,1)}), bf16[16,64,256]{2,1,0:T(8,128)(2,1)S(1)}, u32[]{:S(2)}, u32[]{:S(2)}) async-start(bf16[16,64,256]{2,1,0:T(8,128)(2,1)} %get-tuple-element.129), calls=%async_computation | async-start | bytes 1048576 | tf_op jit(solution)/shard_map/all_to_all | solution.py:1308
  182.3 184.0 %reduce-scatter.6.cloned.1.call-start = ((), (), s32[]{:S(2)}) async-start(), calls=%async_computation.6 | async-start | bytes 6266880 | tf_op jit(solution)/shard_map/reduce_scatter | solution.py:1368
  182.3 13.7 %collective-permute-start.24 = (bf16[2,64,1024]{2,1,0:T(8,128)(2,1)S(1)}, bf16[2,64,1024]{2,1,0:T(8,128)(2,1)S(1)}, u32[]{:S(2)}, u32[]{:S(2)}) collective-permute-start(bf16[2,64,1024]{2,1,0:T(8,128)(2,1)S(1)} %pad_maximum_fusion.10.refs_0_), channel_id=1, source_target_pairs={{0,8},{4,12},{8,0},{12,4},{1,9},{5,13},{9,1},{13,5},{2,10},{6,14},... | collective-permute-start | bytes 786440 | tf_op jit(solution)/shard_map/ppermute | solution.py:381
  208.5 13.3 %collective-permute-start.27 = (bf16[1088,256]{1,0:T(8,128)(2,1)}, bf16[1088,256]{1,0:T(8,128)(2,1)S(1)}, u32[]{:S(2)}, u32[]{:S(2)}) collective-permute-start(bf16[1088,256]{1,0:T(8,128)(2,1)} %get-tuple-element.133.n_ref), channel_id=1, source_target_pairs={{1,2},{2,1},{5,6},{6,5},{9,10},{10,9},{13,14},{14,13},{17,18},{18,... | collective-permute-start | bytes 1671176 | tf_op jit(solution)/shard_map/ppermute | solution.py:682
  209.4 17.9 %collective-permute-start.26 = (bf16[1088,256]{1,0:T(8,128)(2,1)}, bf16[1088,256]{1,0:T(8,128)(2,1)S(1)}, u32[]{:S(2)}, u32[]{:S(2)}) collective-permute-start(bf16[1088,256]{1,0:T(8,128)(2,1)} %get-tuple-element.133.n_ref), channel_id=1, source_target_pairs={{0,1},{1,0},{2,3},{3,2},{4,5},{5,4},{6,7},{7,6},{8,9},{9,8},{10,11... | collective-permute-start | bytes 1671176 | tf_op jit(solution)/shard_map/ppermute | solution.py:682
  228.1 16.0 %collective-permute-start.29 = (bf16[1088,256]{1,0:T(8,128)(2,1)}, bf16[1088,256]{1,0:T(8,128)(2,1)S(1)}, u32[]{:S(2)}, u32[]{:S(2)}) collective-permute-start(bf16[1088,256]{1,0:T(8,128)(2,1)} %get-tuple-element.138), channel_id=1, source_target_pairs={{1,0},{2,3},{5,4},{6,7},{9,8},{10,11},{13,12},{14,15},{17,16},{18,... | collective-permute-start | bytes 1671176 | tf_op jit(solution)/shard_map/ppermute | solution.py:682
  229.4 14.7 %collective-permute-start.28 = (bf16[1088,256]{1,0:T(8,128)(2,1)}, bf16[1088,256]{1,0:T(8,128)(2,1)S(1)}, u32[]{:S(2)}, u32[]{:S(2)}) collective-permute-start(bf16[1088,256]{1,0:T(8,128)(2,1)} %get-tuple-element.136.n_ref), channel_id=1, source_target_pairs={{1,2},{2,1},{5,6},{6,5},{9,10},{10,9},{13,14},{14,13},{17,18},{18,... | collective-permute-start | bytes 1671176 | tf_op jit(solution)/shard_map/ppermute | solution.py:682
  245.1 15.9 %collective-permute-start.30 = (bf16[1088,256]{1,0:T(8,128)(2,1)}, bf16[1088,256]{1,0:T(8,128)(2,1)S(1)}, u32[]{:S(2)}, u32[]{:S(2)}) collective-permute-start(bf16[1088,256]{1,0:T(8,128)(2,1)} %get-tuple-element.140), channel_id=1, source_target_pairs={{1,0},{2,3},{5,4},{6,7},{9,8},{10,11},{13,12},{14,15},{17,16},{18,... | collective-permute-start | bytes 1671176 | tf_op jit(solution)/shard_map/ppermute | solution.py:682
  270.5 11.5 %collective-permute-start.31 = (bf16[1088,256]{1,0:T(8,128)(2,1)}, bf16[1088,256]{1,0:T(8,128)(2,1)S(1)}, u32[]{:S(2)}, u32[]{:S(2)}) collective-permute-start(bf16[1088,256]{1,0:T(8,128)(2,1)} %get-tuple-element.145), channel_id=1, source_target_pairs={{0,1},{3,2},{4,5},{7,6},{8,9},{11,10},{12,13},{15,14},{16,17},{19,... | collective-permute-start | bytes 1671176 | tf_op jit(solution)/shard_map/ppermute | solution.py:682
  284.1 16.7 %collective-permute-start.32 = (bf16[1088,256]{1,0:T(8,128)(2,1)S(1)}, bf16[1088,256]{1,0:T(8,128)(2,1)S(1)}, u32[]{:S(2)}, u32[]{:S(2)}) collective-permute-start(bf16[1088,256]{1,0:T(8,128)(2,1)S(1)} %add_convert_fusion.9), channel_id=1, source_target_pairs={{1,2},{2,1},{5,6},{6,5},{9,10},{10,9},{13,14},{14,13},{17,18},{18,... | collective-permute-start | bytes 1671176 | tf_op jit(solution)/shard_map/ppermute | solution.py:682
  284.8 16.0 %collective-permute-start.33 = (bf16[1088,256]{1,0:T(8,128)(2,1)}, bf16[1088,256]{1,0:T(8,128)(2,1)S(1)}, u32[]{:S(2)}, u32[]{:S(2)}) collective-permute-start(bf16[1088,256]{1,0:T(8,128)(2,1)} %shard_map.294), channel_id=1, source_target_pairs={{0,1},{3,2},{4,5},{7,6},{8,9},{11,10},{12,13},{15,14},{16,17},{19,... | collective-permute-start | bytes 1671176 | tf_op jit(solution)/shard_map/ppermute | solution.py:682
  311.4 148.5 %reduce-scatter.4.cloned.1.call-start = ((), (), s32[]{:S(2)}) async-start(), calls=%async_computation.5 | async-start | bytes 2785280 | tf_op jit(solution)/shard_map/reduce_scatter | solution.py:1376
  313.1 10.9 %collective-permute-start.34 = (bf16[1088,256]{1,0:T(8,128)(2,1)S(1)}, bf16[1088,256]{1,0:T(8,128)(2,1)S(1)}, u32[]{:S(2)}, u32[]{:S(2)}) collective-permute-start(bf16[1088,256]{1,0:T(8,128)(2,1)S(1)} %add_convert_fusion.8), channel_id=1, source_target_pairs={{0,1},{1,0},{2,3},{3,2},{4,5},{5,4},{6,7},{7,6},{8,9},{9,8},{10,11... | collective-permute-start | bytes 1671176 | tf_op jit(solution)/shard_map/ppermute | solution.py:682
  315.5 8.5 %collective-permute-start.35 = (bf16[1088,256]{1,0:T(8,128)(2,1)S(1)}, bf16[1088,256]{1,0:T(8,128)(2,1)S(1)}, u32[]{:S(2)}, u32[]{:S(2)}) collective-permute-start(bf16[1088,256]{1,0:T(8,128)(2,1)S(1)} %add_convert_fusion.7), channel_id=1, source_target_pairs={{1,2},{2,1},{5,6},{6,5},{9,10},{10,9},{13,14},{14,13},{17,18},{18,... | collective-permute-start | bytes 1671176 | tf_op jit(solution)/shard_map/ppermute | solution.py:682
  342.9 27.0 %all-to-all-start.1 = ((bf16[16,64,256]{2,1,0:T(8,128)(2,1)}), bf16[16,64,256]{2,1,0:T(8,128)(2,1)S(1)}, u32[]{:S(2)}, u32[]{:S(2)}) async-start(bf16[16,64,256]{2,1,0:T(8,128)(2,1)} %bitcast.45), calls=%async_computation.2 | async-start | bytes 1048576 | tf_op jit(solution)/shard_map/all_to_all | solution.py:1349
  347.9 128.1 %reduce-scatter.8.cloned.1.call-start = ((), (), s32[]{:S(2)}) async-start(), calls=%async_computation.7 | async-start | bytes 3133440 | tf_op jit(solution)/shard_map/reduce_scatter | solution.py:1377
  354.2 7.1 %collective-permute-start.41 = (bf16[2,64,1024]{2,1,0:T(8,128)(2,1)}, bf16[2,64,1024]{2,1,0:T(8,128)(2,1)S(1)}, u32[]{:S(2)}, u32[]{:S(2)}) collective-permute-start(bf16[2,64,1024]{2,1,0:T(8,128)(2,1)} %get-tuple-element.176), channel_id=1, source_target_pairs={{0,4},{4,0},{8,12},{12,8},{1,5},{5,1},{9,13},{13,9},{2,6},{6,2},{1... | collective-permute-start | bytes 786440 | tf_op jit(solution)/shard_map/ppermute | solution.py:381
  356.8 56.5 %collective-permute-start.40 = (bf16[2,64,1024]{2,1,0:T(8,128)(2,1)}, bf16[2,64,1024]{2,1,0:T(8,128)(2,1)S(1)}, u32[]{:S(2)}, u32[]{:S(2)}) collective-permute-start(bf16[2,64,1024]{2,1,0:T(8,128)(2,1)} %get-tuple-element.174), channel_id=1, source_target_pairs={{0,4},{4,0},{8,12},{12,8},{1,5},{5,1},{9,13},{13,9},{2,6},{6,2},{1... | collective-permute-start | bytes 786440 | tf_op jit(solution)/shard_map/ppermute | solution.py:381
  361.4 51.9 %collective-permute-start.42 = (bf16[2,64,1024]{2,1,0:T(8,128)(2,1)S(1)}, bf16[2,64,1024]{2,1,0:T(8,128)(2,1)S(1)}, u32[]{:S(2)}, u32[]{:S(2)}) collective-permute-start(bf16[2,64,1024]{2,1,0:T(8,128)(2,1)S(1)} %add_convert_fusion.10), channel_id=1, source_target_pairs={{0,8},{4,12},{8,0},{12,4},{1,9},{5,13},{9,1},{13,5},{2,10},{6,14},... | collective-permute-start | bytes 786440 | tf_op jit(solution)/shard_map/ppermute | solution.py:381
  366.2 42.8 %collective-permute-start.37 = (bf16[2,272,1088]{2,1,0:T(8,128)(2,1)}, bf16[2,272,1088]{2,1,0:T(8,128)(2,1)S(1)}, u32[]{:S(2)}, u32[]{:S(2)}) collective-permute-start(bf16[2,272,1088]{2,1,0:T(8,128)(2,1)} %bitcast.149), channel_id=1, source_target_pairs={{0,16},{16,0},{1,17},{17,1},{2,18},{18,2},{3,19},{19,3},{4,20},{20... | collective-permute-start | bytes 3551240 | tf_op jit(solution)/shard_map/ppermute | solution.py:678
  409.0 12.2 %collective-permute-start.38 = (bf16[3,64,1024]{2,1,0:T(8,128)(2,1)}, bf16[3,64,1024]{2,1,0:T(8,128)(2,1)S(1)}, u32[]{:S(2)}, u32[]{:S(2)}) collective-permute-start(bf16[3,64,1024]{2,1,0:T(8,128)(2,1)} %get-tuple-element.168), channel_id=1, source_target_pairs={{0,8},{4,12},{8,0},{12,4},{1,9},{5,13},{9,1},{13,5},{2,10},{6,14},... | collective-permute-start | bytes 1179656 | tf_op jit(solution)/shard_map/ppermute | solution.py:381
  409.1 19.6 %collective-permute-start.39 = (bf16[3,64,1024]{2,1,0:T(8,128)(2,1)}, bf16[3,64,1024]{2,1,0:T(8,128)(2,1)S(1)}, u32[]{:S(2)}, u32[]{:S(2)}) collective-permute-start(bf16[3,64,1024]{2,1,0:T(8,128)(2,1)} %get-tuple-element.169), channel_id=1, source_target_pairs={{0,12},{4,8},{8,4},{12,0},{1,13},{5,9},{9,5},{13,1},{2,14},{6,10},... | collective-permute-start | bytes 1179656 | tf_op jit(solution)/shard_map/ppermute | solution.py:381
  434.4 18.2 %collective-permute-start.43 = (bf16[1088,256]{1,0:T(8,128)(2,1)S(1)}, bf16[1088,256]{1,0:T(8,128)(2,1)S(1)}, u32[]{:S(2)}, u32[]{:S(2)}) collective-permute-start(bf16[1088,256]{1,0:T(8,128)(2,1)S(1)} %convolution_convert_fusion.5.refs_4_), channel_id=1, source_target_pairs={{0,1},{3,2},{4,5},{7,6},{8,9},{11,10},{12,13},{15,14},{16,17},{19,... | collective-permute-start | bytes 1671176 | tf_op jit(solution)/shard_map/ppermute | solution.py:682
  449.6 23.8 %collective-permute-start.60 = (bf16[272,960]{1,0:T(8,128)(2,1)}, bf16[272,960]{1,0:T(8,128)(2,1)S(1)}, u32[]{:S(2)}, u32[]{:S(2)}) collective-permute-start(bf16[272,960]{1,0:T(8,128)(2,1)} %get-tuple-element.195), channel_id=1, source_target_pairs={{0,4},{4,0},{8,12},{12,8},{1,5},{5,1},{9,13},{13,9},{2,6},{6,2},{1... | collective-permute-start | bytes 1566728 | tf_op jit(solution)/shard_map/ppermute | solution.py:381
  452.1 21.3 %collective-permute-start.61 = (bf16[272,960]{1,0:T(8,128)(2,1)S(1)}, bf16[272,960]{1,0:T(8,128)(2,1)S(1)}, u32[]{:S(2)}, u32[]{:S(2)}) collective-permute-start(bf16[272,960]{1,0:T(8,128)(2,1)S(1)} %add_convert_fusion.6.refs_4_), channel_id=1, source_target_pairs={{0,8},{4,12},{8,0},{12,4},{1,9},{5,13},{9,1},{13,5},{2,10},{6,14},... | collective-permute-start | bytes 1566728 | tf_op jit(solution)/shard_map/ppermute | solution.py:381
  455.7 16.1 %collective-permute-start.48 = (bf16[1088,256]{1,0:T(8,128)(2,1)}, bf16[1088,256]{1,0:T(8,128)(2,1)S(1)}, u32[]{:S(2)}, u32[]{:S(2)}) collective-permute-start(bf16[1088,256]{1,0:T(8,128)(2,1)} %add_convert_fusion.4), channel_id=1, source_target_pairs={{1,2},{2,1},{5,6},{6,5},{9,10},{10,9},{13,14},{14,13},{17,18},{18,... | collective-permute-start | bytes 1671176 | tf_op jit(solution)/shard_map/ppermute | solution.py:682
  456.4 15.4 %collective-permute-start.49 = (bf16[1088,256]{1,0:T(8,128)(2,1)}, bf16[1088,256]{1,0:T(8,128)(2,1)S(1)}, u32[]{:S(2)}, u32[]{:S(2)}) collective-permute-start(bf16[1088,256]{1,0:T(8,128)(2,1)} %shard_map.309), channel_id=1, source_target_pairs={{0,1},{3,2},{4,5},{7,6},{8,9},{11,10},{12,13},{15,14},{16,17},{19,... | collective-permute-start | bytes 1671176 | tf_op jit(solution)/shard_map/ppermute | solution.py:682
  477.3 13.5 %collective-permute-start.62 = (bf16[136,2048]{1,0:T(8,128)(2,1)S(1)}, bf16[136,2048]{1,0:T(8,128)(2,1)S(1)}, u32[]{:S(2)}, u32[]{:S(2)}) collective-permute-start(bf16[136,2048]{1,0:T(8,128)(2,1)S(1)} %fusion.42), channel_id=1, source_target_pairs={{0,16},{16,0},{1,17},{17,1},{2,18},{18,2},{3,19},{19,3},{4,20},{20... | collective-permute-start | bytes 1671176 | tf_op jit(solution)/shard_map/ppermute | solution.py:678
  477.6 22.1 %collective-permute-start.50 = (bf16[1088,256]{1,0:T(8,128)(2,1)S(1)}, bf16[1088,256]{1,0:T(8,128)(2,1)S(1)}, u32[]{:S(2)}, u32[]{:S(2)}) collective-permute-start(bf16[1088,256]{1,0:T(8,128)(2,1)S(1)} %add_convert_fusion.3), channel_id=1, source_target_pairs={{0,1},{1,0},{2,3},{3,2},{4,5},{5,4},{6,7},{7,6},{8,9},{9,8},{10,11... | collective-permute-start | bytes 1671176 | tf_op jit(solution)/shard_map/ppermute | solution.py:682
  480.2 19.5 %collective-permute-start.51 = (bf16[1088,256]{1,0:T(8,128)(2,1)S(1)}, bf16[1088,256]{1,0:T(8,128)(2,1)S(1)}, u32[]{:S(2)}, u32[]{:S(2)}) collective-permute-start(bf16[1088,256]{1,0:T(8,128)(2,1)S(1)} %add_convert_fusion.2), channel_id=1, source_target_pairs={{1,2},{2,1},{5,6},{6,5},{9,10},{10,9},{13,14},{14,13},{17,18},{18,... | collective-permute-start | bytes 1671176 | tf_op jit(solution)/shard_map/ppermute | solution.py:682
  493.4 20.9 %collective-permute-start.63 = (bf16[136,592]{1,0:T(8,128)(2,1)}, bf16[136,592]{1,0:T(8,128)(2,1)}, u32[]{:S(2)}, u32[]{:S(2)}) collective-permute-start(bf16[136,592]{1,0:T(8,128)(2,1)} %pad_maximum_fusion.11), channel_id=1, source_target_pairs={{0,1},{1,0},{2,3},{3,2},{4,5},{5,4},{6,7},{7,6},{8,9},{9,8},{10,11... | collective-permute-start | bytes 483080 | tf_op jit(solution)/shard_map/ppermute | solution.py:682
  496.5 18.7 %collective-permute-start.64 = (bf16[136,592]{1,0:T(8,128)(2,1)}, bf16[136,592]{1,0:T(8,128)(2,1)S(1)}, u32[]{:S(2)}, u32[]{:S(2)}) collective-permute-start(bf16[136,592]{1,0:T(8,128)(2,1)} %pad_maximum_fusion.12), channel_id=1, source_target_pairs={{0,2},{1,3},{2,0},{3,1},{4,6},{5,7},{6,4},{7,5},{8,10},{9,11},{10,... | collective-permute-start | bytes 483080 | tf_op jit(solution)/shard_map/ppermute | solution.py:682
  498.1 17.7 %collective-permute-start.65 = (bf16[136,592]{1,0:T(8,128)(2,1)}, bf16[136,592]{1,0:T(8,128)(2,1)}, u32[]{:S(2)}, u32[]{:S(2)}) collective-permute-start(bf16[136,592]{1,0:T(8,128)(2,1)} %pad_maximum_fusion.13), channel_id=1, source_target_pairs={{0,3},{1,2},{2,1},{3,0},{4,7},{5,6},{6,5},{7,4},{8,11},{9,10},{10,... | collective-permute-start | bytes 483080 | tf_op jit(solution)/shard_map/ppermute | solution.py:682
  510.9 18.2 %collective-permute-start.47 = (bf16[272,256]{1,0:T(8,128)(2,1)}, bf16[272,256]{1,0:T(8,128)(2,1)S(1)}, u32[]{:S(2)}, u32[]{:S(2)}) collective-permute-start(bf16[272,256]{1,0:T(8,128)(2,1)} %get-tuple-element.271), channel_id=1, source_target_pairs={{0,12},{4,8},{8,4},{12,0},{1,13},{5,9},{9,5},{13,1},{2,14},{6,10},... | collective-permute-start | bytes 417800 | tf_op jit(solution)/shard_map/ppermute | solution.py:381
  513.4 15.8 %collective-permute-start.46 = (bf16[272,256]{1,0:T(8,128)(2,1)}, bf16[272,256]{1,0:T(8,128)(2,1)S(1)}, u32[]{:S(2)}, u32[]{:S(2)}) collective-permute-start(bf16[272,256]{1,0:T(8,128)(2,1)} %get-tuple-element.272), channel_id=1, source_target_pairs={{0,8},{4,12},{8,0},{12,4},{1,9},{5,13},{9,1},{13,5},{2,10},{6,14},... | collective-permute-start | bytes 417800 | tf_op jit(solution)/shard_map/ppermute | solution.py:381
  514.3 15.3 %collective-permute-start.45 = (bf16[272,256]{1,0:T(8,128)(2,1)}, bf16[272,256]{1,0:T(8,128)(2,1)S(1)}, u32[]{:S(2)}, u32[]{:S(2)}) collective-permute-start(bf16[272,256]{1,0:T(8,128)(2,1)} %get-tuple-element.273), channel_id=1, source_target_pairs={{0,4},{4,0},{8,12},{12,8},{1,5},{5,1},{9,13},{13,9},{2,6},{6,2},{1... | collective-permute-start | bytes 417800 | tf_op jit(solution)/shard_map/ppermute | solution.py:381
  515.3 19.7 %collective-permute-start.52 = (bf16[272,256]{1,0:T(8,128)(2,1)}, bf16[272,256]{1,0:T(8,128)(2,1)}, u32[]{:S(2)}, u32[]{:S(2)}) collective-permute-start(bf16[272,256]{1,0:T(8,128)(2,1)} %get-tuple-element.189), channel_id=1, source_target_pairs={{0,4},{4,0},{8,12},{12,8},{1,5},{5,1},{9,13},{13,9},{2,6},{6,2},{1... | collective-permute-start | bytes 417800 | tf_op jit(solution)/shard_map/ppermute | solution.py:381
  528.0 7.0 %collective-permute-start.53 = (bf16[272,256]{1,0:T(8,128)(2,1)}, bf16[272,256]{1,0:T(8,128)(2,1)S(1)}, u32[]{:S(2)}, u32[]{:S(2)}) collective-permute-start(bf16[272,256]{1,0:T(8,128)(2,1)} %get-tuple-element.190), channel_id=1, source_target_pairs={{0,8},{4,12},{8,0},{12,4},{1,9},{5,13},{9,1},{13,5},{2,10},{6,14},... | collective-permute-start | bytes 417800 | tf_op jit(solution)/shard_map/ppermute | solution.py:381
  529.2 13.8 %collective-permute-start.66 = (bf16[136,1088]{1,0:T(8,128)(2,1)}, bf16[136,1088]{1,0:T(8,128)(2,1)}, u32[]{:S(2)}, u32[]{:S(2)}) collective-permute-start(bf16[136,1088]{1,0:T(8,128)(2,1)} %pad_maximum_fusion.9), channel_id=1, source_target_pairs={{0,16},{16,0},{1,17},{17,1},{2,18},{18,2},{3,19},{19,3},{4,20},{20... | collective-permute-start | bytes 887816 | tf_op jit(solution)/shard_map/ppermute | solution.py:678
  529.6 11.3 %collective-permute-start.59 = (f32[8,1768]{1,0:T(8,128)S(1)}, f32[8,1768]{1,0:T(8,128)S(1)}, u32[]{:S(2)}, u32[]{:S(2)}) collective-permute-start(f32[8,1768]{1,0:T(8,128)S(1)} %add.258), channel_id=1, source_target_pairs={{0,16},{16,0},{1,17},{17,1},{2,18},{18,2},{3,19},{19,3},{4,20},{20... | collective-permute-start | bytes 169736 | tf_op jit(solution)/shard_map/ppermute | solution.py:678
  (147 other events, 804.6 us)
Sparse Core Ops, SparseCore 0:
  11.2 50.7 all-gather.6
  67.9 42.4 all-gather.8
  136.3 48.6 all-gather.10
  311.5 54.6 reduce-scatter.5
  368.5 46.1 reduce-scatter.3
  417.3 33.3 reduce-scatter.7

commit v3 on v2

--- a/solution.py
+++ b/solution.py
@@ -1203,7 +1203,7 @@
     tok_a = block_input.shape[1]
     tok_b = tok_a // rows
     feat = block_input.shape[2]
-    block = 2 * tok_b
+    block = 4 * tok_b
     wide = rows * HDIM
     slots = wide + HDIM
     hidden_len = up_weight.shape[1]

time: 561 us -> 557 us (level)
  Pallas kernels: 151 us -> 137 us
  starting transfers between devices: 89.2 us -> 102 us
    ppermute x26, starting transfers between devices: 48.6 us -> 60.1 us  [col_send(): return lax.ppermute(value, 'col', pairs)]
    pallas_call x2, Pallas kernels: 34.7 us -> 25.1 us  [attend(): pl.pallas_call(partial(forward_kernel, len(pieces), own, len(earlier), to...]
  transfers between devices with their start and end apart: 75 -> 75, of which waited for: 28 -> 29; matrix products, arithmetic and copies ran while one was open for 15% -> 15% of each run, Pallas kernels for 26% -> 23%
where the time goes in v3:
time: 557 us; the launch traced here: 555 us
  waiting for transfers between devices  168 us (30%)
  Pallas kernels  137 us (25%)
  starting transfers between devices  102 us (18%)
  local copies, waits for them, and re-layouts  63.7 us (11%)
  other arithmetic  35.9 us (6%)
  matrix products  32.1 us (6%)
  between operations  16.8 us (3%)
    ppermute x26, waiting for transfers between devices, col_send(): return lax.ppermute(value, 'col', pairs)  81.2 us
    pallas_call x16, Pallas kernels, small_kernel(): pl.pallas_call(body, out_shape=out_shape, in_specs=[IN_SMEM] * scalars +...  68.3 us
    ppermute x26, starting transfers between devices, col_send(): return lax.ppermute(value, 'col', pairs)  60.1 us
    ppermute x33, waiting for transfers between devices, swap(): return lax.ppermute(value, 'row', [(i, i ^ step) for i in range(size)])  58.4 us
    pallas_call x2, Pallas kernels, attend_back(): pl.pallas_call(partial(backward_kernel, len(pieces), own, tok_b, block),...  39.1 us
    unnamed x279, local copies, waits for them, and re-layouts  34.3 us
    dot_general x16, matrix products, dot(): lax.dot_general(left, right, (((left_dim,), (right_dim,)), ((), ())), pre...  32.1 us
    pallas_call x2, Pallas kernels, attend(): pl.pallas_call(partial(forward_kernel, len(pieces), own, len(earlier), to...  25.1 us
  transfers between devices with their start and end apart: 75, of which 29 were waited for; matrix products, arithmetic and copies ran while one was open for 15% of the time, Pallas kernels for 23%

profile of v3, /device:TPU:0, one launch (start us, length us, event | category | flops | bytes accessed | tf_op | source)
XLA Modules:
  0.0 555.1 jit_solution(10503759417830104783)
XLA Ops:
  8.4 2.7 pad_maximum_fusion.3
  11.9 2.2 shard_map.272
  17.9 4.7 collective-permute-start.3
  25.1 7.0 %collective-permute-done.3.refs_3_ = bf16[288,592]{1,0:T(8,128)(2,1)S(1)} collective-permute-done((bf16[288,592]{1,0:T(8,128)(2,1)S(1)}, bf16[288,592]{1,0:T(8,128)(2,1)S(1)}, u32[]{:S(2)}, u32[]{:S(2)}) %collective-permute-start.3) | collective-permute-done | bytes 341024 | tf_op jit(solution)/shard_map/ppermute | solution.py:682
  32.1 8.8 %collective-permute-done.1.refs_1_ = bf16[288,592]{1,0:T(8,128)(2,1)S(1)} collective-permute-done((bf16[288,592]{1,0:T(8,128)(2,1)S(1)}, bf16[288,592]{1,0:T(8,128)(2,1)S(1)}, u32[]{:S(2)}, u32[]{:S(2)}) %collective-permute-start.1) | collective-permute-done | bytes 341024 | tf_op jit(solution)/shard_map/ppermute | solution.py:682
  40.8 13.8 %collective-permute-done.2.refs_2_ = bf16[288,592]{1,0:T(8,128)(2,1)S(1)} collective-permute-done((bf16[288,592]{1,0:T(8,128)(2,1)S(1)}, bf16[288,592]{1,0:T(8,128)(2,1)S(1)}, u32[]{:S(2)}, u32[]{:S(2)}) %collective-permute-start.2) | collective-permute-done | bytes 341024 | tf_op jit(solution)/shard_map/ppermute | solution.py:682
  56.2 3.2 shard_map.274
  62.5 2.0 shard_map.276
  71.2 2.2 collective-permute-done.10.refs_4_
  77.5 2.1 fusion.28.refs_0_
  84.5 23.8 %collective-permute-done.14.refs_3_ = bf16[288,960]{1,0:T(8,128)(2,1)S(1)} collective-permute-done((bf16[288,960]{1,0:T(8,128)(2,1)S(1)}, bf16[288,960]{1,0:T(8,128)(2,1)S(1)}, u32[]{:S(2)}, u32[]{:S(2)}) %collective-permute-start.14) | collective-permute-done | bytes 552992 | tf_op jit(solution)/shard_map/ppermute | solution.py:381
  113.8 3.2 shard_map.280
  117.1 3.1 multiply_convert_fusion.1
  123.2 4.3 collective-permute-done.16.refs_0_
  129.4 3.3 multiply_convert_fusion
  136.8 5.0 fusion.64
  141.9 4.2 collective-permute-done.20.refs_5_
  147.0 22.1 %shard_map.282 = (bf16[16,64,256]{2,1,0:T(8,128)(2,1)}, f32[16,64,256]{2,1,0:T(8,128)}, f32[4,1,1024]{2,1,0:T(1,128)}) custom-call(s32[4]{0:T(128)} %add_add_fusion.info, bf16[3,64,512]{2,1,0:T(8,128)(2,1)} %get-tuple-element.261.refs_1_.refs_0_, bf16[3,64,512]{2,1,0:T(8,128)(2,1)} %get-tuple-element.257.refs_1_, ...), custom_call_target="tpu_custom_call" | custom-call | flops 28521267200 | bytes 4194304 | tf_op jit(solution)/shard_map/pallas_call | solution.py:523
  169.1 4.9 all-to-all-start
  176.0 10.1 %collective-permute-done.24.refs_2_ = bf16[2,64,1024]{2,1,0:T(8,128)(2,1)S(1)} collective-permute-done((bf16[2,64,1024]{2,1,0:T(8,128)(2,1)S(1)}, bf16[2,64,1024]{2,1,0:T(8,128)(2,1)S(1)}, u32[]{:S(2)}, u32[]{:S(2)}) %collective-permute-start.24) | collective-permute-done | bytes 262176 | tf_op jit(solution)/shard_map/ppermute | solution.py:381
  188.3 3.0 shard_map.283
  191.3 3.3 all-to-all-done.heads_ref
  195.4 5.2 shard_map.284
  200.6 13.0 %collective-permute-start.27 = (bf16[1088,256]{1,0:T(8,128)(2,1)}, bf16[1088,256]{1,0:T(8,128)(2,1)S(1)}, u32[]{:S(2)}, u32[]{:S(2)}) collective-permute-start(bf16[1088,256]{1,0:T(8,128)(2,1)} %get-tuple-element.133.n_ref), channel_id=1, source_target_pairs={{1,2},{2,1},{5,6},{6,5},{9,10},{10,9},{13,14},{14,13},{17,18},{18,... | collective-permute-start | bytes 1671176 | tf_op jit(solution)/shard_map/ppermute | solution.py:682
  213.6 4.1 collective-permute-start.26
  218.3 6.8 %shard_map.286 = (bf16[256,1088]{1,0:T(8,128)(2,1)}, bf16[256,1088]{1,0:T(8,128)(2,1)}, bf16[1088,256]{1,0:T(8,128)(2,1)}) custom-call(bf16[1088,256]{1,0:T(8,128)(2,1)} %get-tuple-element.133.n_ref, bf16[1088,256]{1,0:T(8,128)(2,1)} %shard_map.285.cot_ref.refs_4_, bf16[1088,1088]{1,0:T(8,128)(2,1)} %bitcast.140, bf16[1088,1088]{1,0:T(8,128)(2,1)} %bitcast.131, ...), custom_call_target="tpu_custom_call" | custom-call | flops 3030384640 | bytes 7524608 | tf_op jit(solution)/shard_map/pallas_call | solution.py:770
  225.1 5.3 collective-permute-done.26.refs_0_
  233.3 2.6 dynamic-slice_bitcast_fusion
  235.9 6.8 %shard_map.288 = (bf16[256,1088]{1,0:T(8,128)(2,1)}, bf16[256,1088]{1,0:T(8,128)(2,1)}, bf16[1088,256]{1,0:T(8,128)(2,1)}) custom-call(bf16[1088,256]{1,0:T(8,128)(2,1)} %get-tuple-element.136.n_ref, bf16[1088,256]{1,0:T(8,128)(2,1)} %get-tuple-element.253.cot_ref, bf16[1088,1088]{1,0:T(8,128)(2,1)} %bitcast.141, bf16[1088,1088]{1,0:T(8,128)(2,1)} %bitcast.132, ...), custom_call_target="tpu_custom_call" | custom-call | flops 3030384640 | bytes 7524608 | tf_op jit(solution)/shard_map/pallas_call | solution.py:770
  242.7 4.3 collective-permute-done.29.refs_1_
  251.3 6.8 %shard_map.290 = (bf16[256,1088]{1,0:T(8,128)(2,1)}, bf16[256,1088]{1,0:T(8,128)(2,1)}, bf16[1088,256]{1,0:T(8,128)(2,1)}) custom-call(bf16[1088,256]{1,0:T(8,128)(2,1)} %broadcast_select_fusion.1.n_ref, bf16[1088,256]{1,0:T(8,128)(2,1)} %get-tuple-element.252.cot_ref, bf16[1088,1088]{1,0:T(8,128)(2,1)} %bitcast.142, bf16[1088,1088]{1,0:T(8,128)(2,1)} %bitcast.133, ...), custom_call_target="tpu_custom_call" | custom-call | flops 3030384640 | bytes 7524608 | tf_op jit(solution)/shard_map/pallas_call | solution.py:770
  258.1 5.6 %collective-permute-done.30.refs_0_ = bf16[1088,256]{1,0:T(8,128)(2,1)S(1)} collective-permute-done((bf16[1088,256]{1,0:T(8,128)(2,1)}, bf16[1088,256]{1,0:T(8,128)(2,1)S(1)}, u32[]{:S(2)}, u32[]{:S(2)}) %collective-permute-start.30) | collective-permute-done | bytes 557088 | tf_op jit(solution)/shard_map/ppermute | solution.py:682
  266.5 6.8 %shard_map.292 = (bf16[256,1088]{1,0:T(8,128)(2,1)}, bf16[256,1088]{1,0:T(8,128)(2,1)}, bf16[1088,256]{1,0:T(8,128)(2,1)}) custom-call(bf16[1088,256]{1,0:T(8,128)(2,1)} %broadcast_select_fusion.n_ref, bf16[1088,256]{1,0:T(8,128)(2,1)} %get-tuple-element.251.cot_ref, bf16[1088,1088]{1,0:T(8,128)(2,1)} %bitcast.143, bf16[1088,1088]{1,0:T(8,128)(2,1)} %bitcast.134, ...), custom_call_target="tpu_custom_call" | custom-call | flops 3030384640 | bytes 7524608 | tf_op jit(solution)/shard_map/pallas_call | solution.py:770
  274.7 9.9 %collective-permute-done.31.refs_0_ = bf16[1088,256]{1,0:T(8,128)(2,1)S(1)} collective-permute-done((bf16[1088,256]{1,0:T(8,128)(2,1)}, bf16[1088,256]{1,0:T(8,128)(2,1)S(1)}, u32[]{:S(2)}, u32[]{:S(2)}) %collective-permute-start.31) | collective-permute-done | bytes 557088 | tf_op jit(solution)/shard_map/ppermute | solution.py:682
  287.3 7.3 %collective-permute-start.33 = (bf16[1088,256]{1,0:T(8,128)(2,1)}, bf16[1088,256]{1,0:T(8,128)(2,1)S(1)}, u32[]{:S(2)}, u32[]{:S(2)}) collective-permute-start(bf16[1088,256]{1,0:T(8,128)(2,1)} %shard_map.294), channel_id=1, source_target_pairs={{0,1},{3,2},{4,5},{7,6},{8,9},{11,10},{12,13},{15,14},{16,17},{19,... | collective-permute-start | bytes 1671176 | tf_op jit(solution)/shard_map/ppermute | solution.py:682
  297.3 4.3 convolution_convert_fusion.1.refs_2_
  307.8 3.3 convolution_convert_fusion.refs_2_
  311.1 3.0 pad_maximum_fusion
  315.8 2.4 collective-permute-start.34
  319.4 7.4 %collective-permute-done.34.refs_0_ = bf16[1088,256]{1,0:T(8,128)(2,1)S(1)} collective-permute-done((bf16[1088,256]{1,0:T(8,128)(2,1)S(1)}, bf16[1088,256]{1,0:T(8,128)(2,1)S(1)}, u32[]{:S(2)}, u32[]{:S(2)}) %collective-permute-start.34) | collective-permute-done | bytes 557088 | tf_op jit(solution)/shard_map/ppermute | solution.py:682
  328.3 6.7 %shard_map.299 = (f32[1088,256]{1,0:T(8,128)}, bf16[1088,256]{1,0:T(8,128)(2,1)}, f32[1088,3]{1,0:T(8,128)}, bf16[1088,256]{1,0:T(8,128)(2,1)}) custom-call(s32[4]{0:T(128)} %add_add_fusion.info, bf16[1088,256]{1,0:T(8,128)(2,1)} %get-tuple-element.135.refs_2_.refs_1_.refs_0_, bf16[1088,256]{1,0:T(8,128)(2,1)} %get-tuple-element.160.refs_1_, ...), custom_call_target="tpu_custom_call" | custom-call | bytes 7985920 | tf_op jit(solution)/shard_map/pallas_call | solution.py:770
  336.8 2.1 fusion.8
  345.7 5.8 %all-to-all-start.1 = ((bf16[16,64,256]{2,1,0:T(8,128)(2,1)}), bf16[16,64,256]{2,1,0:T(8,128)(2,1)S(1)}, u32[]{:S(2)}, u32[]{:S(2)}) async-start(bf16[16,64,256]{2,1,0:T(8,128)(2,1)} %bitcast.45), calls=%async_computation.2 | async-start | bytes 1048576 | tf_op jit(solution)/shard_map/all_to_all | solution.py:1349
  352.2 4.5 shard_map.303
  359.8 3.7 shard_map.317
  365.2 7.5 %reduce-scatter.6.cloned.1.call-done = bf16[1,2,272,1088]{3,2,1,0:T(8,128)(2,1)} async-done(((bf16[4,2,272,1088]{3,2,1,0:T(8,128)(2,1)}), bf16[1,2,272,1088]{3,2,1,0:T(8,128)(2,1)}) %reduce-scatter.6.cloned.1.call-update) | async-done | bytes 1183760 | tf_op jit(solution)/shard_map/reduce_scatter | solution.py:1368
  374.1 34.6 %shard_map.301 = (bf16[3,64,1024]{2,1,0:T(8,128)(2,1)}, bf16[3,64,1024]{2,1,0:T(8,128)(2,1)}, bf16[3,64,1024]{2,1,0:T(8,128)(2,1)}, bf16[3,64,1024]{2,1,0:T(8,128)(2,1)}) custom-call(s32[4]{0:T(128)} %add_add_fusion.info, bf16[3,64,512]{2,1,0:T(8,128)(2,1)} %get-tuple-element.261.refs_1_.refs_0_, bf16[3,64,512]{2,1,0:T(8,128)(2,1)} %get-tuple-element.257.refs_1_, ...), custom_call_target="tpu_custom_call" | custom-call | flops 36909875200 | bytes 4194304 | tf_op jit(solution)/shard_map/pallas_call | solution.py:643
  413.1 7.8 %collective-permute-done.38.refs_2_ = bf16[3,64,1024]{2,1,0:T(8,128)(2,1)S(1)} collective-permute-done((bf16[3,64,1024]{2,1,0:T(8,128)(2,1)}, bf16[3,64,1024]{2,1,0:T(8,128)(2,1)S(1)}, u32[]{:S(2)}, u32[]{:S(2)}) %collective-permute-start.38) | collective-permute-done | bytes 393248 | tf_op jit(solution)/shard_map/ppermute | solution.py:381
  420.9 7.5 %collective-permute-done.39.refs_3_ = bf16[3,64,1024]{2,1,0:T(8,128)(2,1)S(1)} collective-permute-done((bf16[3,64,1024]{2,1,0:T(8,128)(2,1)}, bf16[3,64,1024]{2,1,0:T(8,128)(2,1)S(1)}, u32[]{:S(2)}, u32[]{:S(2)}) %collective-permute-start.39) | collective-permute-done | bytes 393248 | tf_op jit(solution)/shard_map/ppermute | solution.py:381
  429.2 3.2 shard_map.304.refs_0_
  434.3 3.5 collective-permute-start.43
  442.9 5.6 %shard_map.306 = (bf16[272,960]{1,0:T(8,128)(2,1)}, bf16[272,960]{1,0:T(8,128)(2,1)}, bf16[272,960]{1,0:T(8,128)(2,1)}, bf16[272,960]{1,0:T(8,128)(2,1)}) custom-call(s32[1]{0:T(128)} %bitcast.info, bf16[1088,1024]{1,0:T(8,128)(2,1)} %pad_maximum_fusion.2.left_ref, bf16[960,1024]{1,0:T(8,128)(2,1)} %shard_map.305.right_ref), custom_call_target="tpu_custom_call" | custom-call | bytes 6283264 | tf_op jit(solution)/shard_map/pallas_call | solution.py:770
  453.7 2.0 add_convert_fusion.4
  456.3 3.6 collective-permute-start.49
  460.1 11.8 %collective-permute-done.49.refs_1_ = bf16[1088,256]{1,0:T(8,128)(2,1)S(1)} collective-permute-done((bf16[1088,256]{1,0:T(8,128)(2,1)}, bf16[1088,256]{1,0:T(8,128)(2,1)S(1)}, u32[]{:S(2)}, u32[]{:S(2)}) %collective-permute-start.49) | collective-permute-done | bytes 557088 | tf_op jit(solution)/shard_map/ppermute | solution.py:682
  477.5 3.2 collective-permute-start.62
  480.9 2.4 collective-permute-start.50
  484.4 8.0 %collective-permute-done.62 = bf16[136,2048]{1,0:T(8,128)(2,1)S(1)} collective-permute-done((bf16[136,2048]{1,0:T(8,128)(2,1)S(1)}, bf16[136,2048]{1,0:T(8,128)(2,1)S(1)}, u32[]{:S(2)}, u32[]{:S(2)}) %collective-permute-start.62) | collective-permute-done | bytes 557088 | tf_op jit(solution)/shard_map/ppermute | solution.py:678
  494.9 2.4 collective-permute-start.63
  502.9 4.5 shard_map.314
  520.6 2.0 fusion.29
  526.4 3.2 collective-permute-done.58
  537.2 2.2 shard_map.315
  539.4 3.2 collective-permute-done.59
  (546 shorter events, 153.3 us)
Async XLA Ops:
  7.2 129.6 %all-gather.7.cloned.1.call-start = ((), (), s32[]{:S(2)}) async-start(), calls=%async_computation.8 | async-start | bytes 6266880 | tf_op jit(solution)/shard_map/all_gather | solution.py:1257
  11.1 180.2 %all-gather.9.cloned.1.call-start = ((), (), s32[]{:S(2)}) async-start(), calls=%async_computation.9 | async-start | bytes 4177920 | tf_op jit(solution)/shard_map/all_gather | solution.py:1261
  14.1 10.7 %collective-permute-start = (bf16[272,384]{1,0:T(8,128)(2,1)}, bf16[272,384]{1,0:T(8,128)(2,1)S(1)}, u32[]{:S(2)}, u32[]{:S(2)}) collective-permute-start(bf16[272,384]{1,0:T(8,128)(2,1)} %get-tuple-element.107), channel_id=1, source_target_pairs={{0,4},{4,0},{8,12},{12,8},{1,5},{5,1},{9,13},{13,9},{2,6},{6,2},{1... | collective-permute-start | bytes 626696 | tf_op jit(solution)/shard_map/ppermute | solution.py:381
  17.9 14.2 %collective-permute-start.3 = (bf16[288,592]{1,0:T(8,128)(2,1)S(1)}, bf16[288,592]{1,0:T(8,128)(2,1)S(1)}, u32[]{:S(2)}, u32[]{:S(2)}) collective-permute-start(bf16[288,592]{1,0:T(8,128)(2,1)S(1)} %get-tuple-element.279), channel_id=1, source_target_pairs={{0,3},{1,2},{2,1},{3,0},{4,7},{5,6},{6,5},{7,4},{8,11},{9,10},{10,... | collective-permute-start | bytes 1022984 | tf_op jit(solution)/shard_map/ppermute | solution.py:682
  22.5 18.3 %collective-permute-start.1 = (bf16[288,592]{1,0:T(8,128)(2,1)S(1)}, bf16[288,592]{1,0:T(8,128)(2,1)S(1)}, u32[]{:S(2)}, u32[]{:S(2)}) collective-permute-start(bf16[288,592]{1,0:T(8,128)(2,1)S(1)} %get-tuple-element.280), channel_id=1, source_target_pairs={{0,1},{1,0},{2,3},{3,2},{4,5},{5,4},{6,7},{7,6},{8,9},{9,8},{10,11... | collective-permute-start | bytes 1022984 | tf_op jit(solution)/shard_map/ppermute | solution.py:682
  22.6 32.1 %collective-permute-start.2 = (bf16[288,592]{1,0:T(8,128)(2,1)S(1)}, bf16[288,592]{1,0:T(8,128)(2,1)S(1)}, u32[]{:S(2)}, u32[]{:S(2)}) collective-permute-start(bf16[288,592]{1,0:T(8,128)(2,1)S(1)} %get-tuple-element.281), channel_id=1, source_target_pairs={{0,2},{1,3},{2,0},{3,1},{4,6},{5,7},{6,4},{7,5},{8,10},{9,11},{10,... | collective-permute-start | bytes 1022984 | tf_op jit(solution)/shard_map/ppermute | solution.py:682
  23.2 32.2 %collective-permute-start.4 = (bf16[272,384]{1,0:T(8,128)(2,1)S(1)}, bf16[272,384]{1,0:T(8,128)(2,1)S(1)}, u32[]{:S(2)}, u32[]{:S(2)}) collective-permute-start(bf16[272,384]{1,0:T(8,128)(2,1)S(1)} %copy-done.129), channel_id=1, source_target_pairs={{0,8},{4,12},{8,0},{12,4},{1,9},{5,13},{9,1},{13,5},{2,10},{6,14},... | collective-permute-start | bytes 626696 | tf_op jit(solution)/shard_map/ppermute | solution.py:381
  24.8 30.6 %collective-permute-start.5 = (bf16[272,384]{1,0:T(8,128)(2,1)S(1)}, bf16[272,384]{1,0:T(8,128)(2,1)S(1)}, u32[]{:S(2)}, u32[]{:S(2)}) collective-permute-start(bf16[272,384]{1,0:T(8,128)(2,1)S(1)} %copy-done.128), channel_id=1, source_target_pairs={{0,12},{4,8},{8,4},{12,0},{1,13},{5,9},{9,5},{13,1},{2,14},{6,10},... | collective-permute-start | bytes 626696 | tf_op jit(solution)/shard_map/ppermute | solution.py:381
  59.4 14.1 %collective-permute-start.7 = (bf16[1088,256]{1,0:T(8,128)(2,1)}, bf16[1088,256]{1,0:T(8,128)(2,1)S(1)}, u32[]{:S(2)}, u32[]{:S(2)}) collective-permute-start(bf16[1088,256]{1,0:T(8,128)(2,1)} %get-tuple-element.115.refs_1_), channel_id=1, source_target_pairs={{1,2},{2,1},{5,6},{6,5},{9,10},{10,9},{13,14},{14,13},{17,18},{18,... | collective-permute-start | bytes 1671176 | tf_op jit(solution)/shard_map/ppermute | solution.py:682
  60.1 14.5 %collective-permute-start.6 = (bf16[1088,256]{1,0:T(8,128)(2,1)}, bf16[1088,256]{1,0:T(8,128)(2,1)S(1)}, u32[]{:S(2)}, u32[]{:S(2)}) collective-permute-start(bf16[1088,256]{1,0:T(8,128)(2,1)} %get-tuple-element.115.refs_1_), channel_id=1, source_target_pairs={{0,1},{1,0},{2,3},{3,2},{4,5},{5,4},{6,7},{7,6},{8,9},{9,8},{10,11... | collective-permute-start | bytes 1671176 | tf_op jit(solution)/shard_map/ppermute | solution.py:682
  66.1 7.4 %collective-permute-start.10 = (bf16[272,256]{1,0:T(8,128)(2,1)}, bf16[272,256]{1,0:T(8,128)(2,1)S(1)}, u32[]{:S(2)}, u32[]{:S(2)}) collective-permute-start(bf16[272,256]{1,0:T(8,128)(2,1)} %get-tuple-element.118), channel_id=1, source_target_pairs={{0,12},{4,8},{8,4},{12,0},{1,13},{5,9},{9,5},{13,1},{2,14},{6,10},... | collective-permute-start | bytes 417800 | tf_op jit(solution)/shard_map/ppermute | solution.py:381
  67.7 165.6 %all-gather.11.cloned.1.call-start = ((), (), s32[]{:S(2)}) async-start(), calls=%async_computation.10 | async-start | bytes 2785280 | tf_op jit(solution)/shard_map/all_gather | solution.py:1298
  75.5 32.8 %collective-permute-start.12 = (bf16[1088,256]{1,0:T(8,128)(2,1)}, bf16[1088,256]{1,0:T(8,128)(2,1)S(1)}, u32[]{:S(2)}, u32[]{:S(2)}) collective-permute-start(bf16[1088,256]{1,0:T(8,128)(2,1)} %get-tuple-element.120), channel_id=1, source_target_pairs={{1,0},{2,3},{5,4},{6,7},{9,8},{10,11},{13,12},{14,15},{17,16},{18,... | collective-permute-start | bytes 1671176 | tf_op jit(solution)/shard_map/ppermute | solution.py:682
  76.8 31.5 %collective-permute-start.11 = (bf16[1088,256]{1,0:T(8,128)(2,1)}, bf16[1088,256]{1,0:T(8,128)(2,1)S(1)}, u32[]{:S(2)}, u32[]{:S(2)}) collective-permute-start(bf16[1088,256]{1,0:T(8,128)(2,1)} %get-tuple-element.119), channel_id=1, source_target_pairs={{1,2},{2,1},{5,6},{6,5},{9,10},{10,9},{13,14},{14,13},{17,18},{18,... | collective-permute-start | bytes 1671176 | tf_op jit(solution)/shard_map/ppermute | solution.py:682
  79.6 28.6 %collective-permute-start.14 = (bf16[288,960]{1,0:T(8,128)(2,1)S(1)}, bf16[288,960]{1,0:T(8,128)(2,1)S(1)}, u32[]{:S(2)}, u32[]{:S(2)}) collective-permute-start(bf16[288,960]{1,0:T(8,128)(2,1)S(1)} %fusion.28.refs_0_), channel_id=1, source_target_pairs={{0,8},{4,12},{8,0},{12,4},{1,9},{5,13},{9,1},{13,5},{2,10},{6,14},... | collective-permute-start | bytes 1658888 | tf_op jit(solution)/shard_map/ppermute | solution.py:381
  81.2 27.0 %collective-permute-start.13 = (bf16[288,960]{1,0:T(8,128)(2,1)S(1)}, bf16[288,960]{1,0:T(8,128)(2,1)S(1)}, u32[]{:S(2)}, u32[]{:S(2)}) collective-permute-start(bf16[288,960]{1,0:T(8,128)(2,1)S(1)} %fusion.28.refs_0_), channel_id=1, source_target_pairs={{0,4},{4,0},{8,12},{12,8},{1,5},{5,1},{9,13},{13,9},{2,6},{6,2},{1... | collective-permute-start | bytes 1658888 | tf_op jit(solution)/shard_map/ppermute | solution.py:381
  110.3 17.1 %collective-permute-start.16 = (bf16[1088,256]{1,0:T(8,128)(2,1)}, bf16[1088,256]{1,0:T(8,128)(2,1)S(1)}, u32[]{:S(2)}, u32[]{:S(2)}) collective-permute-start(bf16[1088,256]{1,0:T(8,128)(2,1)} %get-tuple-element.127), channel_id=1, source_target_pairs={{1,0},{2,3},{5,4},{6,7},{9,8},{10,11},{13,12},{14,15},{17,16},{18,... | collective-permute-start | bytes 1671176 | tf_op jit(solution)/shard_map/ppermute | solution.py:682
  121.0 15.2 %collective-permute-start.21 = (bf16[3,64,512]{2,1,0:T(8,128)(2,1)S(1)}, bf16[3,64,512]{2,1,0:T(8,128)(2,1)}, u32[]{:S(2)}, u32[]{:S(2)}) collective-permute-start(bf16[3,64,512]{2,1,0:T(8,128)(2,1)S(1)} %get-tuple-element.258.refs_4_), channel_id=1, source_target_pairs={{0,12},{4,8},{8,4},{12,0},{1,13},{5,9},{9,5},{13,1},{2,14},{6,10},... | collective-permute-start | bytes 589832 | tf_op jit(solution)/shard_map/ppermute | solution.py:381
  122.0 14.8 %collective-permute-start.19 = (bf16[3,64,512]{2,1,0:T(8,128)(2,1)S(1)}, bf16[3,64,512]{2,1,0:T(8,128)(2,1)}, u32[]{:S(2)}, u32[]{:S(2)}) collective-permute-start(bf16[3,64,512]{2,1,0:T(8,128)(2,1)S(1)} %get-tuple-element.259.refs_3_), channel_id=1, source_target_pairs={{0,8},{4,12},{8,0},{12,4},{1,9},{5,13},{9,1},{13,5},{2,10},{6,14},... | collective-permute-start | bytes 589832 | tf_op jit(solution)/shard_map/ppermute | solution.py:381
  123.2 18.7 %collective-permute-start.17 = (bf16[3,64,512]{2,1,0:T(8,128)(2,1)S(1)}, bf16[3,64,512]{2,1,0:T(8,128)(2,1)}, u32[]{:S(2)}, u32[]{:S(2)}) collective-permute-start(bf16[3,64,512]{2,1,0:T(8,128)(2,1)S(1)} %get-tuple-element.260.refs_2_), channel_id=1, source_target_pairs={{0,4},{4,0},{8,12},{12,8},{1,5},{5,1},{9,13},{13,9},{2,6},{6,2},{1... | collective-permute-start | bytes 589832 | tf_op jit(solution)/shard_map/ppermute | solution.py:381
  134.7 7.2 %collective-permute-start.22 = (bf16[3,64,512]{2,1,0:T(8,128)(2,1)S(1)}, bf16[3,64,512]{2,1,0:T(8,128)(2,1)S(1)}, u32[]{:S(2)}, u32[]{:S(2)}) collective-permute-start(bf16[3,64,512]{2,1,0:T(8,128)(2,1)S(1)} %get-tuple-element.254), channel_id=1, source_target_pairs={{0,12},{4,8},{8,4},{12,0},{1,13},{5,9},{9,5},{13,1},{2,14},{6,10},... | collective-permute-start | bytes 589832 | tf_op jit(solution)/shard_map/ppermute | solution.py:381
  135.0 11.1 %collective-permute-start.20 = (bf16[3,64,512]{2,1,0:T(8,128)(2,1)S(1)}, bf16[3,64,512]{2,1,0:T(8,128)(2,1)S(1)}, u32[]{:S(2)}, u32[]{:S(2)}) collective-permute-start(bf16[3,64,512]{2,1,0:T(8,128)(2,1)S(1)} %get-tuple-element.255), channel_id=1, source_target_pairs={{0,8},{4,12},{8,0},{12,4},{1,9},{5,13},{9,1},{13,5},{2,10},{6,14},... | collective-permute-start | bytes 589832 | tf_op jit(solution)/shard_map/ppermute | solution.py:381
  136.3 9.9 %collective-permute-start.18 = (bf16[3,64,512]{2,1,0:T(8,128)(2,1)S(1)}, bf16[3,64,512]{2,1,0:T(8,128)(2,1)S(1)}, u32[]{:S(2)}, u32[]{:S(2)}) collective-permute-start(bf16[3,64,512]{2,1,0:T(8,128)(2,1)S(1)} %get-tuple-element.256), channel_id=1, source_target_pairs={{0,4},{4,0},{8,12},{12,8},{1,5},{5,1},{9,13},{13,9},{2,6},{6,2},{1... | collective-permute-start | bytes 589832 | tf_op jit(solution)/shard_map/ppermute | solution.py:381
  136.7 9.4 %collective-permute-start.23 = (bf16[2,64,1024]{2,1,0:T(8,128)(2,1)S(1)}, bf16[2,64,1024]{2,1,0:T(8,128)(2,1)S(1)}, u32[]{:S(2)}, u32[]{:S(2)}) collective-permute-start(bf16[2,64,1024]{2,1,0:T(8,128)(2,1)S(1)} %pad_maximum_fusion.10.refs_0_), channel_id=1, source_target_pairs={{0,4},{4,0},{8,12},{12,8},{1,5},{5,1},{9,13},{13,9},{2,6},{6,2},{1... | collective-permute-start | bytes 786440 | tf_op jit(solution)/shard_map/ppermute | solution.py:381
  169.1 25.6 %all-to-all-start = ((bf16[16,64,256]{2,1,0:T(8,128)(2,1)}), bf16[16,64,256]{2,1,0:T(8,128)(2,1)S(1)}, u32[]{:S(2)}, u32[]{:S(2)}) async-start(bf16[16,64,256]{2,1,0:T(8,128)(2,1)} %get-tuple-element.129), calls=%async_computation | async-start | bytes 1048576 | tf_op jit(solution)/shard_map/all_to_all | solution.py:1308
  173.9 198.8 %reduce-scatter.6.cloned.1.call-start = ((), (), s32[]{:S(2)}) async-start(), calls=%async_computation.6 | async-start | bytes 6266880 | tf_op jit(solution)/shard_map/reduce_scatter | solution.py:1368
  174.0 12.0 %collective-permute-start.24 = (bf16[2,64,1024]{2,1,0:T(8,128)(2,1)S(1)}, bf16[2,64,1024]{2,1,0:T(8,128)(2,1)S(1)}, u32[]{:S(2)}, u32[]{:S(2)}) collective-permute-start(bf16[2,64,1024]{2,1,0:T(8,128)(2,1)S(1)} %pad_maximum_fusion.10.refs_0_), channel_id=1, source_target_pairs={{0,8},{4,12},{8,0},{12,4},{1,9},{5,13},{9,1},{13,5},{2,10},{6,14},... | collective-permute-start | bytes 786440 | tf_op jit(solution)/shard_map/ppermute | solution.py:381
  200.6 24.5 %collective-permute-start.27 = (bf16[1088,256]{1,0:T(8,128)(2,1)}, bf16[1088,256]{1,0:T(8,128)(2,1)S(1)}, u32[]{:S(2)}, u32[]{:S(2)}) collective-permute-start(bf16[1088,256]{1,0:T(8,128)(2,1)} %get-tuple-element.133.n_ref), channel_id=1, source_target_pairs={{1,2},{2,1},{5,6},{6,5},{9,10},{10,9},{13,14},{14,13},{17,18},{18,... | collective-permute-start | bytes 1671176 | tf_op jit(solution)/shard_map/ppermute | solution.py:682
  213.6 16.9 %collective-permute-start.26 = (bf16[1088,256]{1,0:T(8,128)(2,1)}, bf16[1088,256]{1,0:T(8,128)(2,1)S(1)}, u32[]{:S(2)}, u32[]{:S(2)}) collective-permute-start(bf16[1088,256]{1,0:T(8,128)(2,1)} %get-tuple-element.133.n_ref), channel_id=1, source_target_pairs={{0,1},{1,0},{2,3},{3,2},{4,5},{5,4},{6,7},{7,6},{8,9},{9,8},{10,11... | collective-permute-start | bytes 1671176 | tf_op jit(solution)/shard_map/ppermute | solution.py:682
  231.3 15.8 %collective-permute-start.29 = (bf16[1088,256]{1,0:T(8,128)(2,1)}, bf16[1088,256]{1,0:T(8,128)(2,1)S(1)}, u32[]{:S(2)}, u32[]{:S(2)}) collective-permute-start(bf16[1088,256]{1,0:T(8,128)(2,1)} %get-tuple-element.138), channel_id=1, source_target_pairs={{1,0},{2,3},{5,4},{6,7},{9,8},{10,11},{13,12},{14,15},{17,16},{18,... | collective-permute-start | bytes 1671176 | tf_op jit(solution)/shard_map/ppermute | solution.py:682
  232.6 14.5 %collective-permute-start.28 = (bf16[1088,256]{1,0:T(8,128)(2,1)}, bf16[1088,256]{1,0:T(8,128)(2,1)S(1)}, u32[]{:S(2)}, u32[]{:S(2)}) collective-permute-start(bf16[1088,256]{1,0:T(8,128)(2,1)} %get-tuple-element.136.n_ref), channel_id=1, source_target_pairs={{1,2},{2,1},{5,6},{6,5},{9,10},{10,9},{13,14},{14,13},{17,18},{18,... | collective-permute-start | bytes 1671176 | tf_op jit(solution)/shard_map/ppermute | solution.py:682
  248.1 15.7 %collective-permute-start.30 = (bf16[1088,256]{1,0:T(8,128)(2,1)}, bf16[1088,256]{1,0:T(8,128)(2,1)S(1)}, u32[]{:S(2)}, u32[]{:S(2)}) collective-permute-start(bf16[1088,256]{1,0:T(8,128)(2,1)} %get-tuple-element.140), channel_id=1, source_target_pairs={{1,0},{2,3},{5,4},{6,7},{9,8},{10,11},{13,12},{14,15},{17,16},{18,... | collective-permute-start | bytes 1671176 | tf_op jit(solution)/shard_map/ppermute | solution.py:682
  273.3 11.3 %collective-permute-start.31 = (bf16[1088,256]{1,0:T(8,128)(2,1)}, bf16[1088,256]{1,0:T(8,128)(2,1)S(1)}, u32[]{:S(2)}, u32[]{:S(2)}) collective-permute-start(bf16[1088,256]{1,0:T(8,128)(2,1)} %get-tuple-element.145), channel_id=1, source_target_pairs={{0,1},{3,2},{4,5},{7,6},{8,9},{11,10},{12,13},{15,14},{16,17},{19,... | collective-permute-start | bytes 1671176 | tf_op jit(solution)/shard_map/ppermute | solution.py:682
  286.6 16.9 %collective-permute-start.32 = (bf16[1088,256]{1,0:T(8,128)(2,1)S(1)}, bf16[1088,256]{1,0:T(8,128)(2,1)S(1)}, u32[]{:S(2)}, u32[]{:S(2)}) collective-permute-start(bf16[1088,256]{1,0:T(8,128)(2,1)S(1)} %add_convert_fusion.9), channel_id=1, source_target_pairs={{1,2},{2,1},{5,6},{6,5},{9,10},{10,9},{13,14},{14,13},{17,18},{18,... | collective-permute-start | bytes 1671176 | tf_op jit(solution)/shard_map/ppermute | solution.py:682
  287.3 16.2 %collective-permute-start.33 = (bf16[1088,256]{1,0:T(8,128)(2,1)}, bf16[1088,256]{1,0:T(8,128)(2,1)S(1)}, u32[]{:S(2)}, u32[]{:S(2)}) collective-permute-start(bf16[1088,256]{1,0:T(8,128)(2,1)} %shard_map.294), channel_id=1, source_target_pairs={{0,1},{3,2},{4,5},{7,6},{8,9},{11,10},{12,13},{15,14},{16,17},{19,... | collective-permute-start | bytes 1671176 | tf_op jit(solution)/shard_map/ppermute | solution.py:682
  314.2 146.0 %reduce-scatter.4.cloned.1.call-start = ((), (), s32[]{:S(2)}) async-start(), calls=%async_computation.5 | async-start | bytes 2785280 | tf_op jit(solution)/shard_map/reduce_scatter | solution.py:1376
  315.8 10.9 %collective-permute-start.34 = (bf16[1088,256]{1,0:T(8,128)(2,1)S(1)}, bf16[1088,256]{1,0:T(8,128)(2,1)S(1)}, u32[]{:S(2)}, u32[]{:S(2)}) collective-permute-start(bf16[1088,256]{1,0:T(8,128)(2,1)S(1)} %add_convert_fusion.8), channel_id=1, source_target_pairs={{0,1},{1,0},{2,3},{3,2},{4,5},{5,4},{6,7},{7,6},{8,9},{9,8},{10,11... | collective-permute-start | bytes 1671176 | tf_op jit(solution)/shard_map/ppermute | solution.py:682
  318.3 8.5 %collective-permute-start.35 = (bf16[1088,256]{1,0:T(8,128)(2,1)S(1)}, bf16[1088,256]{1,0:T(8,128)(2,1)S(1)}, u32[]{:S(2)}, u32[]{:S(2)}) collective-permute-start(bf16[1088,256]{1,0:T(8,128)(2,1)S(1)} %add_convert_fusion.7), channel_id=1, source_target_pairs={{1,2},{2,1},{5,6},{6,5},{9,10},{10,9},{13,14},{14,13},{17,18},{18,... | collective-permute-start | bytes 1671176 | tf_op jit(solution)/shard_map/ppermute | solution.py:682
  345.7 27.6 %all-to-all-start.1 = ((bf16[16,64,256]{2,1,0:T(8,128)(2,1)}), bf16[16,64,256]{2,1,0:T(8,128)(2,1)S(1)}, u32[]{:S(2)}, u32[]{:S(2)}) async-start(bf16[16,64,256]{2,1,0:T(8,128)(2,1)} %bitcast.45), calls=%async_computation.2 | async-start | bytes 1048576 | tf_op jit(solution)/shard_map/all_to_all | solution.py:1349
  351.5 124.7 %reduce-scatter.8.cloned.1.call-start = ((), (), s32[]{:S(2)}) async-start(), calls=%async_computation.7 | async-start | bytes 3133440 | tf_op jit(solution)/shard_map/reduce_scatter | solution.py:1377
  356.6 6.9 %collective-permute-start.41 = (bf16[2,64,1024]{2,1,0:T(8,128)(2,1)}, bf16[2,64,1024]{2,1,0:T(8,128)(2,1)S(1)}, u32[]{:S(2)}, u32[]{:S(2)}) collective-permute-start(bf16[2,64,1024]{2,1,0:T(8,128)(2,1)} %get-tuple-element.176), channel_id=1, source_target_pairs={{0,4},{4,0},{8,12},{12,8},{1,5},{5,1},{9,13},{13,9},{2,6},{6,2},{1... | collective-permute-start | bytes 786440 | tf_op jit(solution)/shard_map/ppermute | solution.py:381
  359.2 53.8 %collective-permute-start.40 = (bf16[2,64,1024]{2,1,0:T(8,128)(2,1)}, bf16[2,64,1024]{2,1,0:T(8,128)(2,1)S(1)}, u32[]{:S(2)}, u32[]{:S(2)}) collective-permute-start(bf16[2,64,1024]{2,1,0:T(8,128)(2,1)} %get-tuple-element.174), channel_id=1, source_target_pairs={{0,4},{4,0},{8,12},{12,8},{1,5},{5,1},{9,13},{13,9},{2,6},{6,2},{1... | collective-permute-start | bytes 786440 | tf_op jit(solution)/shard_map/ppermute | solution.py:381
  363.7 49.4 %collective-permute-start.42 = (bf16[2,64,1024]{2,1,0:T(8,128)(2,1)S(1)}, bf16[2,64,1024]{2,1,0:T(8,128)(2,1)S(1)}, u32[]{:S(2)}, u32[]{:S(2)}) collective-permute-start(bf16[2,64,1024]{2,1,0:T(8,128)(2,1)S(1)} %add_convert_fusion.10), channel_id=1, source_target_pairs={{0,8},{4,12},{8,0},{12,4},{1,9},{5,13},{9,1},{13,5},{2,10},{6,14},... | collective-permute-start | bytes 786440 | tf_op jit(solution)/shard_map/ppermute | solution.py:381
  372.7 36.1 %collective-permute-start.37 = (bf16[2,272,1088]{2,1,0:T(8,128)(2,1)}, bf16[2,272,1088]{2,1,0:T(8,128)(2,1)S(1)}, u32[]{:S(2)}, u32[]{:S(2)}) collective-permute-start(bf16[2,272,1088]{2,1,0:T(8,128)(2,1)} %bitcast.149), channel_id=1, source_target_pairs={{0,16},{16,0},{1,17},{17,1},{2,18},{18,2},{3,19},{19,3},{4,20},{20... | collective-permute-start | bytes 3551240 | tf_op jit(solution)/shard_map/ppermute | solution.py:678
  408.7 12.2 %collective-permute-start.38 = (bf16[3,64,1024]{2,1,0:T(8,128)(2,1)}, bf16[3,64,1024]{2,1,0:T(8,128)(2,1)S(1)}, u32[]{:S(2)}, u32[]{:S(2)}) collective-permute-start(bf16[3,64,1024]{2,1,0:T(8,128)(2,1)} %get-tuple-element.168), channel_id=1, source_target_pairs={{0,8},{4,12},{8,0},{12,4},{1,9},{5,13},{9,1},{13,5},{2,10},{6,14},... | collective-permute-start | bytes 1179656 | tf_op jit(solution)/shard_map/ppermute | solution.py:381
  408.8 19.6 %collective-permute-start.39 = (bf16[3,64,1024]{2,1,0:T(8,128)(2,1)}, bf16[3,64,1024]{2,1,0:T(8,128)(2,1)S(1)}, u32[]{:S(2)}, u32[]{:S(2)}) collective-permute-start(bf16[3,64,1024]{2,1,0:T(8,128)(2,1)} %get-tuple-element.169), channel_id=1, source_target_pairs={{0,12},{4,8},{8,4},{12,0},{1,13},{5,9},{9,5},{13,1},{2,14},{6,10},... | collective-permute-start | bytes 1179656 | tf_op jit(solution)/shard_map/ppermute | solution.py:381
  434.3 18.5 %collective-permute-start.43 = (bf16[1088,256]{1,0:T(8,128)(2,1)S(1)}, bf16[1088,256]{1,0:T(8,128)(2,1)S(1)}, u32[]{:S(2)}, u32[]{:S(2)}) collective-permute-start(bf16[1088,256]{1,0:T(8,128)(2,1)S(1)} %convolution_convert_fusion.5.refs_4_), channel_id=1, source_target_pairs={{0,1},{3,2},{4,5},{7,6},{8,9},{11,10},{12,13},{15,14},{16,17},{19,... | collective-permute-start | bytes 1671176 | tf_op jit(solution)/shard_map/ppermute | solution.py:682
  449.5 24.0 %collective-permute-start.60 = (bf16[272,960]{1,0:T(8,128)(2,1)}, bf16[272,960]{1,0:T(8,128)(2,1)S(1)}, u32[]{:S(2)}, u32[]{:S(2)}) collective-permute-start(bf16[272,960]{1,0:T(8,128)(2,1)} %get-tuple-element.195), channel_id=1, source_target_pairs={{0,4},{4,0},{8,12},{12,8},{1,5},{5,1},{9,13},{13,9},{2,6},{6,2},{1... | collective-permute-start | bytes 1566728 | tf_op jit(solution)/shard_map/ppermute | solution.py:381
  452.0 21.6 %collective-permute-start.61 = (bf16[272,960]{1,0:T(8,128)(2,1)S(1)}, bf16[272,960]{1,0:T(8,128)(2,1)S(1)}, u32[]{:S(2)}, u32[]{:S(2)}) collective-permute-start(bf16[272,960]{1,0:T(8,128)(2,1)S(1)} %add_convert_fusion.6.refs_4_), channel_id=1, source_target_pairs={{0,8},{4,12},{8,0},{12,4},{1,9},{5,13},{9,1},{13,5},{2,10},{6,14},... | collective-permute-start | bytes 1566728 | tf_op jit(solution)/shard_map/ppermute | solution.py:381
  455.6 16.3 %collective-permute-start.48 = (bf16[1088,256]{1,0:T(8,128)(2,1)}, bf16[1088,256]{1,0:T(8,128)(2,1)S(1)}, u32[]{:S(2)}, u32[]{:S(2)}) collective-permute-start(bf16[1088,256]{1,0:T(8,128)(2,1)} %add_convert_fusion.4), channel_id=1, source_target_pairs={{1,2},{2,1},{5,6},{6,5},{9,10},{10,9},{13,14},{14,13},{17,18},{18,... | collective-permute-start | bytes 1671176 | tf_op jit(solution)/shard_map/ppermute | solution.py:682
  456.3 15.6 %collective-permute-start.49 = (bf16[1088,256]{1,0:T(8,128)(2,1)}, bf16[1088,256]{1,0:T(8,128)(2,1)S(1)}, u32[]{:S(2)}, u32[]{:S(2)}) collective-permute-start(bf16[1088,256]{1,0:T(8,128)(2,1)} %shard_map.309), channel_id=1, source_target_pairs={{0,1},{3,2},{4,5},{7,6},{8,9},{11,10},{12,13},{15,14},{16,17},{19,... | collective-permute-start | bytes 1671176 | tf_op jit(solution)/shard_map/ppermute | solution.py:682
  477.5 14.9 %collective-permute-start.62 = (bf16[136,2048]{1,0:T(8,128)(2,1)S(1)}, bf16[136,2048]{1,0:T(8,128)(2,1)S(1)}, u32[]{:S(2)}, u32[]{:S(2)}) collective-permute-start(bf16[136,2048]{1,0:T(8,128)(2,1)S(1)} %fusion.42), channel_id=1, source_target_pairs={{0,16},{16,0},{1,17},{17,1},{2,18},{18,2},{3,19},{19,3},{4,20},{20... | collective-permute-start | bytes 1671176 | tf_op jit(solution)/shard_map/ppermute | solution.py:678
  480.9 20.3 %collective-permute-start.50 = (bf16[1088,256]{1,0:T(8,128)(2,1)S(1)}, bf16[1088,256]{1,0:T(8,128)(2,1)S(1)}, u32[]{:S(2)}, u32[]{:S(2)}) collective-permute-start(bf16[1088,256]{1,0:T(8,128)(2,1)S(1)} %add_convert_fusion.3), channel_id=1, source_target_pairs={{0,1},{1,0},{2,3},{3,2},{4,5},{5,4},{6,7},{7,6},{8,9},{9,8},{10,11... | collective-permute-start | bytes 1671176 | tf_op jit(solution)/shard_map/ppermute | solution.py:682
  483.5 17.8 %collective-permute-start.51 = (bf16[1088,256]{1,0:T(8,128)(2,1)S(1)}, bf16[1088,256]{1,0:T(8,128)(2,1)S(1)}, u32[]{:S(2)}, u32[]{:S(2)}) collective-permute-start(bf16[1088,256]{1,0:T(8,128)(2,1)S(1)} %add_convert_fusion.2), channel_id=1, source_target_pairs={{1,2},{2,1},{5,6},{6,5},{9,10},{10,9},{13,14},{14,13},{17,18},{18,... | collective-permute-start | bytes 1671176 | tf_op jit(solution)/shard_map/ppermute | solution.py:682
  494.9 21.0 %collective-permute-start.63 = (bf16[136,592]{1,0:T(8,128)(2,1)}, bf16[136,592]{1,0:T(8,128)(2,1)}, u32[]{:S(2)}, u32[]{:S(2)}) collective-permute-start(bf16[136,592]{1,0:T(8,128)(2,1)} %pad_maximum_fusion.11), channel_id=1, source_target_pairs={{0,1},{1,0},{2,3},{3,2},{4,5},{5,4},{6,7},{7,6},{8,9},{9,8},{10,11... | collective-permute-start | bytes 483080 | tf_op jit(solution)/shard_map/ppermute | solution.py:682
  498.1 18.9 %collective-permute-start.64 = (bf16[136,592]{1,0:T(8,128)(2,1)}, bf16[136,592]{1,0:T(8,128)(2,1)S(1)}, u32[]{:S(2)}, u32[]{:S(2)}) collective-permute-start(bf16[136,592]{1,0:T(8,128)(2,1)} %pad_maximum_fusion.12), channel_id=1, source_target_pairs={{0,2},{1,3},{2,0},{3,1},{4,6},{5,7},{6,4},{7,5},{8,10},{9,11},{10,... | collective-permute-start | bytes 483080 | tf_op jit(solution)/shard_map/ppermute | solution.py:682
  499.6 17.9 %collective-permute-start.65 = (bf16[136,592]{1,0:T(8,128)(2,1)}, bf16[136,592]{1,0:T(8,128)(2,1)}, u32[]{:S(2)}, u32[]{:S(2)}) collective-permute-start(bf16[136,592]{1,0:T(8,128)(2,1)} %pad_maximum_fusion.13), channel_id=1, source_target_pairs={{0,3},{1,2},{2,1},{3,0},{4,7},{5,6},{6,5},{7,4},{8,11},{9,10},{10,... | collective-permute-start | bytes 483080 | tf_op jit(solution)/shard_map/ppermute | solution.py:682
  512.6 18.1 %collective-permute-start.47 = (bf16[272,256]{1,0:T(8,128)(2,1)}, bf16[272,256]{1,0:T(8,128)(2,1)S(1)}, u32[]{:S(2)}, u32[]{:S(2)}) collective-permute-start(bf16[272,256]{1,0:T(8,128)(2,1)} %get-tuple-element.271), channel_id=1, source_target_pairs={{0,12},{4,8},{8,4},{12,0},{1,13},{5,9},{9,5},{13,1},{2,14},{6,10},... | collective-permute-start | bytes 417800 | tf_op jit(solution)/shard_map/ppermute | solution.py:381
  515.0 15.8 %collective-permute-start.46 = (bf16[272,256]{1,0:T(8,128)(2,1)}, bf16[272,256]{1,0:T(8,128)(2,1)S(1)}, u32[]{:S(2)}, u32[]{:S(2)}) collective-permute-start(bf16[272,256]{1,0:T(8,128)(2,1)} %get-tuple-element.272), channel_id=1, source_target_pairs={{0,8},{4,12},{8,0},{12,4},{1,9},{5,13},{9,1},{13,5},{2,10},{6,14},... | collective-permute-start | bytes 417800 | tf_op jit(solution)/shard_map/ppermute | solution.py:381
  516.0 16.6 %collective-permute-start.45 = (bf16[272,256]{1,0:T(8,128)(2,1)}, bf16[272,256]{1,0:T(8,128)(2,1)S(1)}, u32[]{:S(2)}, u32[]{:S(2)}) collective-permute-start(bf16[272,256]{1,0:T(8,128)(2,1)} %get-tuple-element.273), channel_id=1, source_target_pairs={{0,4},{4,0},{8,12},{12,8},{1,5},{5,1},{9,13},{13,9},{2,6},{6,2},{1... | collective-permute-start | bytes 417800 | tf_op jit(solution)/shard_map/ppermute | solution.py:381
  517.0 19.6 %collective-permute-start.52 = (bf16[272,256]{1,0:T(8,128)(2,1)}, bf16[272,256]{1,0:T(8,128)(2,1)}, u32[]{:S(2)}, u32[]{:S(2)}) collective-permute-start(bf16[272,256]{1,0:T(8,128)(2,1)} %get-tuple-element.189), channel_id=1, source_target_pairs={{0,4},{4,0},{8,12},{12,8},{1,5},{5,1},{9,13},{13,9},{2,6},{6,2},{1... | collective-permute-start | bytes 417800 | tf_op jit(solution)/shard_map/ppermute | solution.py:381
  529.6 6.9 %collective-permute-start.53 = (bf16[272,256]{1,0:T(8,128)(2,1)}, bf16[272,256]{1,0:T(8,128)(2,1)S(1)}, u32[]{:S(2)}, u32[]{:S(2)}) collective-permute-start(bf16[272,256]{1,0:T(8,128)(2,1)} %get-tuple-element.190), channel_id=1, source_target_pairs={{0,8},{4,12},{8,0},{12,4},{1,9},{5,13},{9,1},{13,5},{2,10},{6,14},... | collective-permute-start | bytes 417800 | tf_op jit(solution)/shard_map/ppermute | solution.py:381
  530.8 13.9 %collective-permute-start.66 = (bf16[136,1088]{1,0:T(8,128)(2,1)}, bf16[136,1088]{1,0:T(8,128)(2,1)}, u32[]{:S(2)}, u32[]{:S(2)}) collective-permute-start(bf16[136,1088]{1,0:T(8,128)(2,1)} %pad_maximum_fusion.9), channel_id=1, source_target_pairs={{0,16},{16,0},{1,17},{17,1},{2,18},{18,2},{3,19},{19,3},{4,20},{20... | collective-permute-start | bytes 887816 | tf_op jit(solution)/shard_map/ppermute | solution.py:678
  532.6 9.9 %collective-permute-start.59 = (f32[8,1768]{1,0:T(8,128)S(1)}, f32[8,1768]{1,0:T(8,128)S(1)}, u32[]{:S(2)}, u32[]{:S(2)}) collective-permute-start(f32[8,1768]{1,0:T(8,128)S(1)} %add.258), channel_id=1, source_target_pairs={{0,16},{16,0},{1,17},{17,1},{2,18},{18,2},{3,19},{19,3},{4,20},{20... | collective-permute-start | bytes 169736 | tf_op jit(solution)/shard_map/ppermute | solution.py:678
  (147 other events, 801.2 us)
Sparse Core Ops, SparseCore 0:
  11.2 50.7 all-gather.6
  67.9 42.4 all-gather.8
  136.3 57.8 all-gather.10
  314.3 58.4 reduce-scatter.5
  375.0 43.6 reduce-scatter.3
  421.3 33.3 reduce-scatter.7

commit v4 on v3

--- a/solution.py
+++ b/solution.py
@@ -1254,9 +1254,8 @@
     ends = col_send(inner, OUTWARD)
     qkv_strip = assemble(me, [strip, strip_near, strip_far, swap(strip_far, 1)], feat)
 
-    up_down = lax.all_gather(jnp.stack([up_weight, down_weight.T]), "row")
-    up_slice = up_down[:, 0].reshape(rows * feat, hidden_len)
-    down_slice = up_down[:, 1].reshape(rows * feat, hidden_len)
+    up_slice = lax.all_gather(up_weight, "row", axis=0, tiled=True)
+    down_slice = lax.all_gather(down_weight.T, "row", axis=0, tiled=True)
 
     out_full = lax.all_gather(jnp.stack(out_got), "row").reshape((-1,) + out_weight.shape)
 

time: 557 us -> 555 us (level); the launches traced: 555 us -> 547 us
  starting transfers between devices: 102 us -> 88.6 us
  waiting for transfers between devices: 168 us -> 181 us
    ppermute x26, starting transfers between devices: 60.1 us -> 47.7 us  [col_send(): return lax.ppermute(value, 'col', pairs)]
    unnamed x279 -> x277, local copies, waits for them, and re-layouts: 34.3 us -> 35.2 us
  transfers between devices with their start and end apart: 75 -> 76, of which waited for: 29 -> 29; matrix products, arithmetic and copies ran while one was open for 15% -> 14% of each run, Pallas kernels for 23% -> 24%
where the time goes in v4:
time: 555 us; the launch traced here: 547 us
  waiting for transfers between devices  181 us (33%)
  Pallas kernels  137 us (25%)
  starting transfers between devices  88.6 us (16%)
  local copies, waits for them, and re-layouts  58.7 us (11%)
  other arithmetic  33 us (6%)
  matrix products  32 us (6%)
  between operations  17.1 us (3%)
    ppermute x26, waiting for transfers between devices, col_send(): return lax.ppermute(value, 'col', pairs)  86.4 us
    pallas_call x16, Pallas kernels, small_kernel(): pl.pallas_call(body, out_shape=out_shape, in_specs=[IN_SMEM] * scalars +...  68.3 us
    ppermute x33, waiting for transfers between devices, swap(): return lax.ppermute(value, 'row', [(i, i ^ step) for i in range(size)])  63.9 us
    ppermute x26, starting transfers between devices, col_send(): return lax.ppermute(value, 'col', pairs)  47.7 us
    pallas_call x2, Pallas kernels, attend_back(): pl.pallas_call(partial(backward_kernel, len(pieces), own, tok_b, block),...  39.2 us
    unnamed x277, local copies, waits for them, and re-layouts  35.2 us
    dot_general x16, matrix products, dot(): lax.dot_general(left, right, (((left_dim,), (right_dim,)), ((), ())), pre...  32 us
    pallas_call x2, Pallas kernels, attend(): pl.pallas_call(partial(forward_kernel, len(pieces), own, len(earlier), to...  25.1 us
  transfers between devices with their start and end apart: 76, of which 29 were waited for; matrix products, arithmetic and copies ran while one was open for 14% of the time, Pallas kernels for 24%

profile of v4, /device:TPU:0, one launch (start us, length us, event | category | flops | bytes accessed | tf_op | source)
XLA Modules:
  0.0 547.0 jit_solution(9140942041680486398)
XLA Ops:
  10.1 2.2 shard_map.272
  16.0 4.7 collective-permute-start.3
  24.1 6.2 %collective-permute-done.3.refs_3_ = bf16[288,592]{1,0:T(8,128)(2,1)S(1)} collective-permute-done((bf16[288,592]{1,0:T(8,128)(2,1)S(1)}, bf16[288,592]{1,0:T(8,128)(2,1)S(1)}, u32[]{:S(2)}, u32[]{:S(2)}) %collective-permute-start.3) | collective-permute-done | bytes 341024 | tf_op jit(solution)/shard_map/ppermute | solution.py:682
  30.2 8.8 %collective-permute-done.1.refs_1_ = bf16[288,592]{1,0:T(8,128)(2,1)S(1)} collective-permute-done((bf16[288,592]{1,0:T(8,128)(2,1)S(1)}, bf16[288,592]{1,0:T(8,128)(2,1)S(1)}, u32[]{:S(2)}, u32[]{:S(2)}) %collective-permute-start.1) | collective-permute-done | bytes 341024 | tf_op jit(solution)/shard_map/ppermute | solution.py:682
  39.0 13.8 %collective-permute-done.2.refs_2_ = bf16[288,592]{1,0:T(8,128)(2,1)S(1)} collective-permute-done((bf16[288,592]{1,0:T(8,128)(2,1)S(1)}, bf16[288,592]{1,0:T(8,128)(2,1)S(1)}, u32[]{:S(2)}, u32[]{:S(2)}) %collective-permute-start.2) | collective-permute-done | bytes 341024 | tf_op jit(solution)/shard_map/ppermute | solution.py:682
  54.4 3.3 shard_map.274
  66.3 5.0 collective-permute-done.9.refs_3_
  71.3 5.4 collective-permute-done.10.refs_4_
  80.3 2.1 fusion.28.refs_0_
  86.5 19.4 %collective-permute-done.14.refs_3_ = bf16[288,960]{1,0:T(8,128)(2,1)S(1)} collective-permute-done((bf16[288,960]{1,0:T(8,128)(2,1)S(1)}, bf16[288,960]{1,0:T(8,128)(2,1)S(1)}, u32[]{:S(2)}, u32[]{:S(2)}) %collective-permute-start.14) | collective-permute-done | bytes 552992 | tf_op jit(solution)/shard_map/ppermute | solution.py:381
  111.4 3.2 shard_map.280
  114.6 3.1 multiply_convert_fusion.1
  120.8 11.2 %collective-permute-done.16.refs_0_ = bf16[1088,256]{1,0:T(8,128)(2,1)S(1)} collective-permute-done((bf16[1088,256]{1,0:T(8,128)(2,1)}, bf16[1088,256]{1,0:T(8,128)(2,1)S(1)}, u32[]{:S(2)}, u32[]{:S(2)}) %collective-permute-start.16) | collective-permute-done | bytes 557088 | tf_op jit(solution)/shard_map/ppermute | solution.py:682
  134.0 3.3 multiply_convert_fusion
  142.1 3.0 collective-permute-done.22.refs_7_
  145.2 4.4 collective-permute-done.20.refs_5_
  150.4 22.1 %shard_map.282 = (bf16[16,64,256]{2,1,0:T(8,128)(2,1)}, f32[16,64,256]{2,1,0:T(8,128)}, f32[4,1,1024]{2,1,0:T(1,128)}) custom-call(s32[4]{0:T(128)} %add_add_fusion.info, bf16[3,64,512]{2,1,0:T(8,128)(2,1)} %get-tuple-element.259.refs_1_.refs_0_, bf16[3,64,512]{2,1,0:T(8,128)(2,1)} %get-tuple-element.255.refs_1_, ...), custom_call_target="tpu_custom_call" | custom-call | flops 28521267200 | bytes 4194304 | tf_op jit(solution)/shard_map/pallas_call | solution.py:523
  172.5 3.6 all-to-all-start
  176.2 2.2 collective-permute-start.24
  178.3 10.0 %collective-permute-done.24.refs_2_ = bf16[2,64,1024]{2,1,0:T(8,128)(2,1)S(1)} collective-permute-done((bf16[2,64,1024]{2,1,0:T(8,128)(2,1)S(1)}, bf16[2,64,1024]{2,1,0:T(8,128)(2,1)S(1)}, u32[]{:S(2)}, u32[]{:S(2)}) %collective-permute-start.24) | collective-permute-done | bytes 262176 | tf_op jit(solution)/shard_map/ppermute | solution.py:381
  190.5 3.0 shard_map.283
  193.5 4.8 all-to-all-done.heads_ref
  199.2 5.2 shard_map.284
  205.2 4.2 collective-permute-start.26
  210.0 6.8 %shard_map.286 = (bf16[256,1088]{1,0:T(8,128)(2,1)}, bf16[256,1088]{1,0:T(8,128)(2,1)}, bf16[1088,256]{1,0:T(8,128)(2,1)}) custom-call(bf16[1088,256]{1,0:T(8,128)(2,1)} %get-tuple-element.133.n_ref, bf16[1088,256]{1,0:T(8,128)(2,1)} %shard_map.285.cot_ref.refs_4_, bf16[1088,1088]{1,0:T(8,128)(2,1)} %all-gather.7.cloned.1.call-done.refs_8_.up_ref, ...), custom_call_target="tpu_custom_call" | custom-call | flops 3030384640 | bytes 7524608 | tf_op jit(solution)/shard_map/pallas_call | solution.py:770
  216.8 5.4 collective-permute-done.26.refs_0_
  225.1 2.6 dynamic-slice_bitcast_fusion
  227.7 6.8 %shard_map.288 = (bf16[256,1088]{1,0:T(8,128)(2,1)}, bf16[256,1088]{1,0:T(8,128)(2,1)}, bf16[1088,256]{1,0:T(8,128)(2,1)}) custom-call(bf16[1088,256]{1,0:T(8,128)(2,1)} %get-tuple-element.136.n_ref, bf16[1088,256]{1,0:T(8,128)(2,1)} %get-tuple-element.251.cot_ref, bf16[1088,1088]{1,0:T(8,128)(2,1)} %all-gather.7.cloned.1.call-done.refs_8_.up_ref, ...), custom_call_target="tpu_custom_call" | custom-call | flops 3030384640 | bytes 7524608 | tf_op jit(solution)/shard_map/pallas_call | solution.py:770
  234.4 4.4 collective-permute-done.29.refs_1_
  243.5 6.8 %shard_map.290 = (bf16[256,1088]{1,0:T(8,128)(2,1)}, bf16[256,1088]{1,0:T(8,128)(2,1)}, bf16[1088,256]{1,0:T(8,128)(2,1)}) custom-call(bf16[1088,256]{1,0:T(8,128)(2,1)} %broadcast_select_fusion.1.n_ref, bf16[1088,256]{1,0:T(8,128)(2,1)} %get-tuple-element.250.cot_ref, bf16[1088,1088]{1,0:T(8,128)(2,1)} %all-gather.7.cloned.1.call-done.refs_8_.up_ref, ...), custom_call_target="tpu_custom_call" | custom-call | flops 3030384640 | bytes 7524608 | tf_op jit(solution)/shard_map/pallas_call | solution.py:770
  250.3 5.4 collective-permute-done.30.refs_0_
  258.5 6.8 %shard_map.292 = (bf16[256,1088]{1,0:T(8,128)(2,1)}, bf16[256,1088]{1,0:T(8,128)(2,1)}, bf16[1088,256]{1,0:T(8,128)(2,1)}) custom-call(bf16[1088,256]{1,0:T(8,128)(2,1)} %broadcast_select_fusion.n_ref, bf16[1088,256]{1,0:T(8,128)(2,1)} %get-tuple-element.249.cot_ref, bf16[1088,1088]{1,0:T(8,128)(2,1)} %all-gather.7.cloned.1.call-done.refs_8_.up_ref, ...), custom_call_target="tpu_custom_call" | custom-call | flops 3030384640 | bytes 7524608 | tf_op jit(solution)/shard_map/pallas_call | solution.py:770
  266.7 10.0 %collective-permute-done.31.refs_0_ = bf16[1088,256]{1,0:T(8,128)(2,1)S(1)} collective-permute-done((bf16[1088,256]{1,0:T(8,128)(2,1)}, bf16[1088,256]{1,0:T(8,128)(2,1)S(1)}, u32[]{:S(2)}, u32[]{:S(2)}) %collective-permute-start.31) | collective-permute-done | bytes 557088 | tf_op jit(solution)/shard_map/ppermute | solution.py:682
  279.4 6.9 %collective-permute-start.33 = (bf16[1088,256]{1,0:T(8,128)(2,1)}, bf16[1088,256]{1,0:T(8,128)(2,1)S(1)}, u32[]{:S(2)}, u32[]{:S(2)}) collective-permute-start(bf16[1088,256]{1,0:T(8,128)(2,1)} %shard_map.294), channel_id=1, source_target_pairs={{0,1},{3,2},{4,5},{7,6},{8,9},{11,10},{12,13},{15,14},{16,17},{19,... | collective-permute-start | bytes 1671176 | tf_op jit(solution)/shard_map/ppermute | solution.py:682
  289.0 4.3 convolution_convert_fusion.1.refs_2_
  299.4 3.3 convolution_convert_fusion.refs_2_
  302.7 3.0 pad_maximum_fusion
  307.4 2.4 collective-permute-start.34
  310.7 7.5 %collective-permute-done.34.refs_0_ = bf16[1088,256]{1,0:T(8,128)(2,1)S(1)} collective-permute-done((bf16[1088,256]{1,0:T(8,128)(2,1)S(1)}, bf16[1088,256]{1,0:T(8,128)(2,1)S(1)}, u32[]{:S(2)}, u32[]{:S(2)}) %collective-permute-start.34) | collective-permute-done | bytes 557088 | tf_op jit(solution)/shard_map/ppermute | solution.py:682
  319.8 6.7 %shard_map.299 = (f32[1088,256]{1,0:T(8,128)}, bf16[1088,256]{1,0:T(8,128)(2,1)}, f32[1088,3]{1,0:T(8,128)}, bf16[1088,256]{1,0:T(8,128)(2,1)}) custom-call(s32[4]{0:T(128)} %add_add_fusion.info, bf16[1088,256]{1,0:T(8,128)(2,1)} %get-tuple-element.135.refs_2_.refs_1_.refs_0_, bf16[1088,256]{1,0:T(8,128)(2,1)} %get-tuple-element.160.refs_1_, ...), custom_call_target="tpu_custom_call" | custom-call | bytes 7985920 | tf_op jit(solution)/shard_map/pallas_call | solution.py:770
  328.4 2.0 fusion.8
  337.1 6.1 %all-to-all-start.1 = ((bf16[16,64,256]{2,1,0:T(8,128)(2,1)}), bf16[16,64,256]{2,1,0:T(8,128)(2,1)S(1)}, u32[]{:S(2)}, u32[]{:S(2)}) async-start(bf16[16,64,256]{2,1,0:T(8,128)(2,1)} %bitcast.44), calls=%async_computation.2 | async-start | bytes 1048576 | tf_op jit(solution)/shard_map/all_to_all | solution.py:1348
  343.9 4.5 shard_map.303
  351.6 3.7 shard_map.317
  357.0 7.3 %reduce-scatter.6.cloned.1.call-done = bf16[1,2,272,1088]{3,2,1,0:T(8,128)(2,1)} async-done(((bf16[4,2,272,1088]{3,2,1,0:T(8,128)(2,1)}), bf16[1,2,272,1088]{3,2,1,0:T(8,128)(2,1)}) %reduce-scatter.6.cloned.1.call-update) | async-done | bytes 1183760 | tf_op jit(solution)/shard_map/reduce_scatter | solution.py:1367
  365.8 34.7 %shard_map.301 = (bf16[3,64,1024]{2,1,0:T(8,128)(2,1)}, bf16[3,64,1024]{2,1,0:T(8,128)(2,1)}, bf16[3,64,1024]{2,1,0:T(8,128)(2,1)}, bf16[3,64,1024]{2,1,0:T(8,128)(2,1)}) custom-call(s32[4]{0:T(128)} %add_add_fusion.info, bf16[3,64,512]{2,1,0:T(8,128)(2,1)} %get-tuple-element.259.refs_1_.refs_0_, bf16[3,64,512]{2,1,0:T(8,128)(2,1)} %get-tuple-element.255.refs_1_, ...), custom_call_target="tpu_custom_call" | custom-call | flops 36909875200 | bytes 4194304 | tf_op jit(solution)/shard_map/pallas_call | solution.py:643
  404.9 7.8 %collective-permute-done.38.refs_2_ = bf16[3,64,1024]{2,1,0:T(8,128)(2,1)S(1)} collective-permute-done((bf16[3,64,1024]{2,1,0:T(8,128)(2,1)}, bf16[3,64,1024]{2,1,0:T(8,128)(2,1)S(1)}, u32[]{:S(2)}, u32[]{:S(2)}) %collective-permute-start.38) | collective-permute-done | bytes 393248 | tf_op jit(solution)/shard_map/ppermute | solution.py:381
  412.7 7.5 %collective-permute-done.39.refs_3_ = bf16[3,64,1024]{2,1,0:T(8,128)(2,1)S(1)} collective-permute-done((bf16[3,64,1024]{2,1,0:T(8,128)(2,1)}, bf16[3,64,1024]{2,1,0:T(8,128)(2,1)S(1)}, u32[]{:S(2)}, u32[]{:S(2)}) %collective-permute-start.39) | collective-permute-done | bytes 393248 | tf_op jit(solution)/shard_map/ppermute | solution.py:381
  421.0 3.2 shard_map.304.refs_0_
  426.1 3.5 collective-permute-start.43
  434.7 5.6 %shard_map.306 = (bf16[272,960]{1,0:T(8,128)(2,1)}, bf16[272,960]{1,0:T(8,128)(2,1)}, bf16[272,960]{1,0:T(8,128)(2,1)}, bf16[272,960]{1,0:T(8,128)(2,1)}) custom-call(s32[1]{0:T(128)} %bitcast.info, bf16[1088,1024]{1,0:T(8,128)(2,1)} %pad_maximum_fusion.2.left_ref, bf16[960,1024]{1,0:T(8,128)(2,1)} %shard_map.305.right_ref), custom_call_target="tpu_custom_call" | custom-call | bytes 6283264 | tf_op jit(solution)/shard_map/pallas_call | solution.py:770
  445.5 2.0 add_convert_fusion.4
  448.1 3.5 collective-permute-start.49
  451.9 11.9 %collective-permute-done.49.refs_1_ = bf16[1088,256]{1,0:T(8,128)(2,1)S(1)} collective-permute-done((bf16[1088,256]{1,0:T(8,128)(2,1)}, bf16[1088,256]{1,0:T(8,128)(2,1)S(1)}, u32[]{:S(2)}, u32[]{:S(2)}) %collective-permute-start.49) | collective-permute-done | bytes 557088 | tf_op jit(solution)/shard_map/ppermute | solution.py:682
  469.3 3.0 collective-permute-start.62
  472.5 2.4 collective-permute-start.50
  476.1 8.0 %collective-permute-done.62 = bf16[136,2048]{1,0:T(8,128)(2,1)S(1)} collective-permute-done((bf16[136,2048]{1,0:T(8,128)(2,1)S(1)}, bf16[136,2048]{1,0:T(8,128)(2,1)S(1)}, u32[]{:S(2)}, u32[]{:S(2)}) %collective-permute-start.62) | collective-permute-done | bytes 557088 | tf_op jit(solution)/shard_map/ppermute | solution.py:678
  486.6 2.4 collective-permute-start.63
  494.5 4.5 shard_map.314
  512.2 2.0 fusion.29
  518.0 3.2 collective-permute-done.58
  526.2 2.0 shard_map.312
  528.9 2.2 shard_map.315
  531.0 3.2 collective-permute-done.59
  (544 shorter events, 150.5 us)
Async XLA Ops:
  7.3 142.3 %all-gather.7.cloned.1.call-start = ((), (), s32[]{:S(2)}) async-start(), calls=%async_computation.5 | async-start | bytes 3133440 | tf_op jit(solution)/shard_map/all_gather | solution.py:1257
  8.5 141.1 %all-gather.9.cloned.1.call-start = ((), (), s32[]{:S(2)}) async-start(), calls=%async_computation.6 | async-start | bytes 3133440 | tf_op jit(solution)/shard_map/all_gather | solution.py:1258
  9.2 184.3 %all-gather.11.cloned.1.call-start = ((), (), s32[]{:S(2)}) async-start(), calls=%async_computation.10 | async-start | bytes 4177920 | tf_op jit(solution)/shard_map/all_gather | solution.py:1260
  12.3 10.7 %collective-permute-start = (bf16[272,384]{1,0:T(8,128)(2,1)}, bf16[272,384]{1,0:T(8,128)(2,1)S(1)}, u32[]{:S(2)}, u32[]{:S(2)}) collective-permute-start(bf16[272,384]{1,0:T(8,128)(2,1)} %get-tuple-element.107), channel_id=1, source_target_pairs={{0,4},{4,0},{8,12},{12,8},{1,5},{5,1},{9,13},{13,9},{2,6},{6,2},{1... | collective-permute-start | bytes 626696 | tf_op jit(solution)/shard_map/ppermute | solution.py:381
  16.0 14.2 %collective-permute-start.3 = (bf16[288,592]{1,0:T(8,128)(2,1)S(1)}, bf16[288,592]{1,0:T(8,128)(2,1)S(1)}, u32[]{:S(2)}, u32[]{:S(2)}) collective-permute-start(bf16[288,592]{1,0:T(8,128)(2,1)S(1)} %get-tuple-element.277), channel_id=1, source_target_pairs={{0,3},{1,2},{2,1},{3,0},{4,7},{5,6},{6,5},{7,4},{8,11},{9,10},{10,... | collective-permute-start | bytes 1022984 | tf_op jit(solution)/shard_map/ppermute | solution.py:682
  20.7 18.3 %collective-permute-start.1 = (bf16[288,592]{1,0:T(8,128)(2,1)S(1)}, bf16[288,592]{1,0:T(8,128)(2,1)S(1)}, u32[]{:S(2)}, u32[]{:S(2)}) collective-permute-start(bf16[288,592]{1,0:T(8,128)(2,1)S(1)} %get-tuple-element.278), channel_id=1, source_target_pairs={{0,1},{1,0},{2,3},{3,2},{4,5},{5,4},{6,7},{7,6},{8,9},{9,8},{10,11... | collective-permute-start | bytes 1022984 | tf_op jit(solution)/shard_map/ppermute | solution.py:682
  20.7 32.1 %collective-permute-start.2 = (bf16[288,592]{1,0:T(8,128)(2,1)S(1)}, bf16[288,592]{1,0:T(8,128)(2,1)S(1)}, u32[]{:S(2)}, u32[]{:S(2)}) collective-permute-start(bf16[288,592]{1,0:T(8,128)(2,1)S(1)} %get-tuple-element.279), channel_id=1, source_target_pairs={{0,2},{1,3},{2,0},{3,1},{4,6},{5,7},{6,4},{7,5},{8,10},{9,11},{10,... | collective-permute-start | bytes 1022984 | tf_op jit(solution)/shard_map/ppermute | solution.py:682
  21.4 32.2 %collective-permute-start.4 = (bf16[272,384]{1,0:T(8,128)(2,1)S(1)}, bf16[272,384]{1,0:T(8,128)(2,1)S(1)}, u32[]{:S(2)}, u32[]{:S(2)}) collective-permute-start(bf16[272,384]{1,0:T(8,128)(2,1)S(1)} %copy-done.128), channel_id=1, source_target_pairs={{0,8},{4,12},{8,0},{12,4},{1,9},{5,13},{9,1},{13,5},{2,10},{6,14},... | collective-permute-start | bytes 626696 | tf_op jit(solution)/shard_map/ppermute | solution.py:381
  23.0 30.6 %collective-permute-start.5 = (bf16[272,384]{1,0:T(8,128)(2,1)S(1)}, bf16[272,384]{1,0:T(8,128)(2,1)S(1)}, u32[]{:S(2)}, u32[]{:S(2)}) collective-permute-start(bf16[272,384]{1,0:T(8,128)(2,1)S(1)} %copy-done.127), channel_id=1, source_target_pairs={{0,12},{4,8},{8,4},{12,0},{1,13},{5,9},{9,5},{13,1},{2,14},{6,10},... | collective-permute-start | bytes 626696 | tf_op jit(solution)/shard_map/ppermute | solution.py:381
  57.6 19.0 %collective-permute-start.7 = (bf16[1088,256]{1,0:T(8,128)(2,1)}, bf16[1088,256]{1,0:T(8,128)(2,1)S(1)}, u32[]{:S(2)}, u32[]{:S(2)}) collective-permute-start(bf16[1088,256]{1,0:T(8,128)(2,1)} %get-tuple-element.115.refs_1_), channel_id=1, source_target_pairs={{1,2},{2,1},{5,6},{6,5},{9,10},{10,9},{13,14},{14,13},{17,18},{18,... | collective-permute-start | bytes 1671176 | tf_op jit(solution)/shard_map/ppermute | solution.py:682
  58.3 18.3 %collective-permute-start.6 = (bf16[1088,256]{1,0:T(8,128)(2,1)}, bf16[1088,256]{1,0:T(8,128)(2,1)S(1)}, u32[]{:S(2)}, u32[]{:S(2)}) collective-permute-start(bf16[1088,256]{1,0:T(8,128)(2,1)} %get-tuple-element.115.refs_1_), channel_id=1, source_target_pairs={{0,1},{1,0},{2,3},{3,2},{4,5},{5,4},{6,7},{7,6},{8,9},{9,8},{10,11... | collective-permute-start | bytes 1671176 | tf_op jit(solution)/shard_map/ppermute | solution.py:682
  61.6 9.7 %collective-permute-start.9 = (bf16[272,256]{1,0:T(8,128)(2,1)}, bf16[272,256]{1,0:T(8,128)(2,1)S(1)}, u32[]{:S(2)}, u32[]{:S(2)}) collective-permute-start(bf16[272,256]{1,0:T(8,128)(2,1)} %get-tuple-element.117), channel_id=1, source_target_pairs={{0,8},{4,12},{8,0},{12,4},{1,9},{5,13},{9,1},{13,5},{2,10},{6,14},... | collective-permute-start | bytes 417800 | tf_op jit(solution)/shard_map/ppermute | solution.py:381
  63.1 13.6 %collective-permute-start.10 = (bf16[272,256]{1,0:T(8,128)(2,1)}, bf16[272,256]{1,0:T(8,128)(2,1)S(1)}, u32[]{:S(2)}, u32[]{:S(2)}) collective-permute-start(bf16[272,256]{1,0:T(8,128)(2,1)} %get-tuple-element.118), channel_id=1, source_target_pairs={{0,12},{4,8},{8,4},{12,0},{1,13},{5,9},{9,5},{13,1},{2,14},{6,10},... | collective-permute-start | bytes 417800 | tf_op jit(solution)/shard_map/ppermute | solution.py:381
  65.0 160.1 %all-gather.13.cloned.1.call-start = ((), (), s32[]{:S(2)}) async-start(), calls=%async_computation.11 | async-start | bytes 2785280 | tf_op jit(solution)/shard_map/all_gather | solution.py:1297
  78.3 27.6 %collective-permute-start.12 = (bf16[1088,256]{1,0:T(8,128)(2,1)}, bf16[1088,256]{1,0:T(8,128)(2,1)S(1)}, u32[]{:S(2)}, u32[]{:S(2)}) collective-permute-start(bf16[1088,256]{1,0:T(8,128)(2,1)} %get-tuple-element.120), channel_id=1, source_target_pairs={{1,0},{2,3},{5,4},{6,7},{9,8},{10,11},{13,12},{14,15},{17,16},{18,... | collective-permute-start | bytes 1671176 | tf_op jit(solution)/shard_map/ppermute | solution.py:682
  79.6 26.3 %collective-permute-start.11 = (bf16[1088,256]{1,0:T(8,128)(2,1)}, bf16[1088,256]{1,0:T(8,128)(2,1)S(1)}, u32[]{:S(2)}, u32[]{:S(2)}) collective-permute-start(bf16[1088,256]{1,0:T(8,128)(2,1)} %get-tuple-element.119), channel_id=1, source_target_pairs={{1,2},{2,1},{5,6},{6,5},{9,10},{10,9},{13,14},{14,13},{17,18},{18,... | collective-permute-start | bytes 1671176 | tf_op jit(solution)/shard_map/ppermute | solution.py:682
  82.5 23.4 %collective-permute-start.14 = (bf16[288,960]{1,0:T(8,128)(2,1)S(1)}, bf16[288,960]{1,0:T(8,128)(2,1)S(1)}, u32[]{:S(2)}, u32[]{:S(2)}) collective-permute-start(bf16[288,960]{1,0:T(8,128)(2,1)S(1)} %fusion.28.refs_0_), channel_id=1, source_target_pairs={{0,8},{4,12},{8,0},{12,4},{1,9},{5,13},{9,1},{13,5},{2,10},{6,14},... | collective-permute-start | bytes 1658888 | tf_op jit(solution)/shard_map/ppermute | solution.py:381
  83.3 22.6 %collective-permute-start.13 = (bf16[288,960]{1,0:T(8,128)(2,1)S(1)}, bf16[288,960]{1,0:T(8,128)(2,1)S(1)}, u32[]{:S(2)}, u32[]{:S(2)}) collective-permute-start(bf16[288,960]{1,0:T(8,128)(2,1)S(1)} %fusion.28.refs_0_), channel_id=1, source_target_pairs={{0,4},{4,0},{8,12},{12,8},{1,5},{5,1},{9,13},{13,9},{2,6},{6,2},{1... | collective-permute-start | bytes 1658888 | tf_op jit(solution)/shard_map/ppermute | solution.py:381
  108.0 24.1 %collective-permute-start.16 = (bf16[1088,256]{1,0:T(8,128)(2,1)}, bf16[1088,256]{1,0:T(8,128)(2,1)S(1)}, u32[]{:S(2)}, u32[]{:S(2)}) collective-permute-start(bf16[1088,256]{1,0:T(8,128)(2,1)} %get-tuple-element.127), channel_id=1, source_target_pairs={{1,0},{2,3},{5,4},{6,7},{9,8},{10,11},{13,12},{14,15},{17,16},{18,... | collective-permute-start | bytes 1671176 | tf_op jit(solution)/shard_map/ppermute | solution.py:682
  118.6 21.8 %collective-permute-start.21 = (bf16[3,64,512]{2,1,0:T(8,128)(2,1)S(1)}, bf16[3,64,512]{2,1,0:T(8,128)(2,1)}, u32[]{:S(2)}, u32[]{:S(2)}) collective-permute-start(bf16[3,64,512]{2,1,0:T(8,128)(2,1)S(1)} %get-tuple-element.256.refs_4_), channel_id=1, source_target_pairs={{0,12},{4,8},{8,4},{12,0},{1,13},{5,9},{9,5},{13,1},{2,14},{6,10},... | collective-permute-start | bytes 589832 | tf_op jit(solution)/shard_map/ppermute | solution.py:381
  119.5 21.1 %collective-permute-start.19 = (bf16[3,64,512]{2,1,0:T(8,128)(2,1)S(1)}, bf16[3,64,512]{2,1,0:T(8,128)(2,1)}, u32[]{:S(2)}, u32[]{:S(2)}) collective-permute-start(bf16[3,64,512]{2,1,0:T(8,128)(2,1)S(1)} %get-tuple-element.257.refs_3_), channel_id=1, source_target_pairs={{0,8},{4,12},{8,0},{12,4},{1,9},{5,13},{9,1},{13,5},{2,10},{6,14},... | collective-permute-start | bytes 589832 | tf_op jit(solution)/shard_map/ppermute | solution.py:381
  120.8 21.3 %collective-permute-start.17 = (bf16[3,64,512]{2,1,0:T(8,128)(2,1)S(1)}, bf16[3,64,512]{2,1,0:T(8,128)(2,1)}, u32[]{:S(2)}, u32[]{:S(2)}) collective-permute-start(bf16[3,64,512]{2,1,0:T(8,128)(2,1)S(1)} %get-tuple-element.258.refs_2_), channel_id=1, source_target_pairs={{0,4},{4,0},{8,12},{12,8},{1,5},{5,1},{9,13},{13,9},{2,6},{6,2},{1... | collective-permute-start | bytes 589832 | tf_op jit(solution)/shard_map/ppermute | solution.py:381
  138.1 7.1 %collective-permute-start.22 = (bf16[3,64,512]{2,1,0:T(8,128)(2,1)S(1)}, bf16[3,64,512]{2,1,0:T(8,128)(2,1)S(1)}, u32[]{:S(2)}, u32[]{:S(2)}) collective-permute-start(bf16[3,64,512]{2,1,0:T(8,128)(2,1)S(1)} %get-tuple-element.252), channel_id=1, source_target_pairs={{0,12},{4,8},{8,4},{12,0},{1,13},{5,9},{9,5},{13,1},{2,14},{6,10},... | collective-permute-start | bytes 589832 | tf_op jit(solution)/shard_map/ppermute | solution.py:381
  139.9 9.7 %collective-permute-start.20 = (bf16[3,64,512]{2,1,0:T(8,128)(2,1)S(1)}, bf16[3,64,512]{2,1,0:T(8,128)(2,1)S(1)}, u32[]{:S(2)}, u32[]{:S(2)}) collective-permute-start(bf16[3,64,512]{2,1,0:T(8,128)(2,1)S(1)} %get-tuple-element.253), channel_id=1, source_target_pairs={{0,8},{4,12},{8,0},{12,4},{1,9},{5,13},{9,1},{13,5},{2,10},{6,14},... | collective-permute-start | bytes 589832 | tf_op jit(solution)/shard_map/ppermute | solution.py:381
  140.4 9.1 %collective-permute-start.18 = (bf16[3,64,512]{2,1,0:T(8,128)(2,1)S(1)}, bf16[3,64,512]{2,1,0:T(8,128)(2,1)S(1)}, u32[]{:S(2)}, u32[]{:S(2)}) collective-permute-start(bf16[3,64,512]{2,1,0:T(8,128)(2,1)S(1)} %get-tuple-element.254), channel_id=1, source_target_pairs={{0,4},{4,0},{8,12},{12,8},{1,5},{5,1},{9,13},{13,9},{2,6},{6,2},{1... | collective-permute-start | bytes 589832 | tf_op jit(solution)/shard_map/ppermute | solution.py:381
  140.6 9.0 %collective-permute-start.23 = (bf16[2,64,1024]{2,1,0:T(8,128)(2,1)S(1)}, bf16[2,64,1024]{2,1,0:T(8,128)(2,1)S(1)}, u32[]{:S(2)}, u32[]{:S(2)}) collective-permute-start(bf16[2,64,1024]{2,1,0:T(8,128)(2,1)S(1)} %pad_maximum_fusion.9.refs_0_), channel_id=1, source_target_pairs={{0,4},{4,0},{8,12},{12,8},{1,5},{5,1},{9,13},{13,9},{2,6},{6,2},{1... | collective-permute-start | bytes 786440 | tf_op jit(solution)/shard_map/ppermute | solution.py:381
  172.5 25.9 %all-to-all-start = ((bf16[16,64,256]{2,1,0:T(8,128)(2,1)}), bf16[16,64,256]{2,1,0:T(8,128)(2,1)S(1)}, u32[]{:S(2)}, u32[]{:S(2)}) async-start(bf16[16,64,256]{2,1,0:T(8,128)(2,1)} %get-tuple-element.129), calls=%async_computation | async-start | bytes 1048576 | tf_op jit(solution)/shard_map/all_to_all | solution.py:1307
  176.1 188.2 %reduce-scatter.6.cloned.1.call-start = ((), (), s32[]{:S(2)}) async-start(), calls=%async_computation.8 | async-start | bytes 6266880 | tf_op jit(solution)/shard_map/reduce_scatter | solution.py:1367
  176.2 12.1 %collective-permute-start.24 = (bf16[2,64,1024]{2,1,0:T(8,128)(2,1)S(1)}, bf16[2,64,1024]{2,1,0:T(8,128)(2,1)S(1)}, u32[]{:S(2)}, u32[]{:S(2)}) collective-permute-start(bf16[2,64,1024]{2,1,0:T(8,128)(2,1)S(1)} %pad_maximum_fusion.9.refs_0_), channel_id=1, source_target_pairs={{0,8},{4,12},{8,0},{12,4},{1,9},{5,13},{9,1},{13,5},{2,10},{6,14},... | collective-permute-start | bytes 786440 | tf_op jit(solution)/shard_map/ppermute | solution.py:381
  204.3 12.5 %collective-permute-start.27 = (bf16[1088,256]{1,0:T(8,128)(2,1)}, bf16[1088,256]{1,0:T(8,128)(2,1)S(1)}, u32[]{:S(2)}, u32[]{:S(2)}) collective-permute-start(bf16[1088,256]{1,0:T(8,128)(2,1)} %get-tuple-element.133.n_ref), channel_id=1, source_target_pairs={{1,2},{2,1},{5,6},{6,5},{9,10},{10,9},{13,14},{14,13},{17,18},{18,... | collective-permute-start | bytes 1671176 | tf_op jit(solution)/shard_map/ppermute | solution.py:682
  205.2 17.0 %collective-permute-start.26 = (bf16[1088,256]{1,0:T(8,128)(2,1)}, bf16[1088,256]{1,0:T(8,128)(2,1)S(1)}, u32[]{:S(2)}, u32[]{:S(2)}) collective-permute-start(bf16[1088,256]{1,0:T(8,128)(2,1)} %get-tuple-element.133.n_ref), channel_id=1, source_target_pairs={{0,1},{1,0},{2,3},{3,2},{4,5},{5,4},{6,7},{7,6},{8,9},{9,8},{10,11... | collective-permute-start | bytes 1671176 | tf_op jit(solution)/shard_map/ppermute | solution.py:682
  223.0 15.8 %collective-permute-start.29 = (bf16[1088,256]{1,0:T(8,128)(2,1)}, bf16[1088,256]{1,0:T(8,128)(2,1)S(1)}, u32[]{:S(2)}, u32[]{:S(2)}) collective-permute-start(bf16[1088,256]{1,0:T(8,128)(2,1)} %get-tuple-element.138), channel_id=1, source_target_pairs={{1,0},{2,3},{5,4},{6,7},{9,8},{10,11},{13,12},{14,15},{17,16},{18,... | collective-permute-start | bytes 1671176 | tf_op jit(solution)/shard_map/ppermute | solution.py:682
  224.3 14.6 %collective-permute-start.28 = (bf16[1088,256]{1,0:T(8,128)(2,1)}, bf16[1088,256]{1,0:T(8,128)(2,1)S(1)}, u32[]{:S(2)}, u32[]{:S(2)}) collective-permute-start(bf16[1088,256]{1,0:T(8,128)(2,1)} %get-tuple-element.136.n_ref), channel_id=1, source_target_pairs={{1,2},{2,1},{5,6},{6,5},{9,10},{10,9},{13,14},{14,13},{17,18},{18,... | collective-permute-start | bytes 1671176 | tf_op jit(solution)/shard_map/ppermute | solution.py:682
  239.9 15.8 %collective-permute-start.30 = (bf16[1088,256]{1,0:T(8,128)(2,1)}, bf16[1088,256]{1,0:T(8,128)(2,1)S(1)}, u32[]{:S(2)}, u32[]{:S(2)}) collective-permute-start(bf16[1088,256]{1,0:T(8,128)(2,1)} %get-tuple-element.140), channel_id=1, source_target_pairs={{1,0},{2,3},{5,4},{6,7},{9,8},{10,11},{13,12},{14,15},{17,16},{18,... | collective-permute-start | bytes 1671176 | tf_op jit(solution)/shard_map/ppermute | solution.py:682
  265.3 11.4 %collective-permute-start.31 = (bf16[1088,256]{1,0:T(8,128)(2,1)}, bf16[1088,256]{1,0:T(8,128)(2,1)S(1)}, u32[]{:S(2)}, u32[]{:S(2)}) collective-permute-start(bf16[1088,256]{1,0:T(8,128)(2,1)} %get-tuple-element.145), channel_id=1, source_target_pairs={{0,1},{3,2},{4,5},{7,6},{8,9},{11,10},{12,13},{15,14},{16,17},{19,... | collective-permute-start | bytes 1671176 | tf_op jit(solution)/shard_map/ppermute | solution.py:682
  278.7 16.4 %collective-permute-start.32 = (bf16[1088,256]{1,0:T(8,128)(2,1)S(1)}, bf16[1088,256]{1,0:T(8,128)(2,1)S(1)}, u32[]{:S(2)}, u32[]{:S(2)}) collective-permute-start(bf16[1088,256]{1,0:T(8,128)(2,1)S(1)} %add_convert_fusion.9), channel_id=1, source_target_pairs={{1,2},{2,1},{5,6},{6,5},{9,10},{10,9},{13,14},{14,13},{17,18},{18,... | collective-permute-start | bytes 1671176 | tf_op jit(solution)/shard_map/ppermute | solution.py:682
  279.4 15.7 %collective-permute-start.33 = (bf16[1088,256]{1,0:T(8,128)(2,1)}, bf16[1088,256]{1,0:T(8,128)(2,1)S(1)}, u32[]{:S(2)}, u32[]{:S(2)}) collective-permute-start(bf16[1088,256]{1,0:T(8,128)(2,1)} %shard_map.294), channel_id=1, source_target_pairs={{0,1},{3,2},{4,5},{7,6},{8,9},{11,10},{12,13},{15,14},{16,17},{19,... | collective-permute-start | bytes 1671176 | tf_op jit(solution)/shard_map/ppermute | solution.py:682
  305.7 146.2 %reduce-scatter.4.cloned.1.call-start = ((), (), s32[]{:S(2)}) async-start(), calls=%async_computation.7 | async-start | bytes 2785280 | tf_op jit(solution)/shard_map/reduce_scatter | solution.py:1375
  307.4 10.8 %collective-permute-start.34 = (bf16[1088,256]{1,0:T(8,128)(2,1)S(1)}, bf16[1088,256]{1,0:T(8,128)(2,1)S(1)}, u32[]{:S(2)}, u32[]{:S(2)}) collective-permute-start(bf16[1088,256]{1,0:T(8,128)(2,1)S(1)} %add_convert_fusion.8), channel_id=1, source_target_pairs={{0,1},{1,0},{2,3},{3,2},{4,5},{5,4},{6,7},{7,6},{8,9},{9,8},{10,11... | collective-permute-start | bytes 1671176 | tf_op jit(solution)/shard_map/ppermute | solution.py:682
  309.8 8.4 %collective-permute-start.35 = (bf16[1088,256]{1,0:T(8,128)(2,1)S(1)}, bf16[1088,256]{1,0:T(8,128)(2,1)S(1)}, u32[]{:S(2)}, u32[]{:S(2)}) collective-permute-start(bf16[1088,256]{1,0:T(8,128)(2,1)S(1)} %add_convert_fusion.7), channel_id=1, source_target_pairs={{1,2},{2,1},{5,6},{6,5},{9,10},{10,9},{13,14},{14,13},{17,18},{18,... | collective-permute-start | bytes 1671176 | tf_op jit(solution)/shard_map/ppermute | solution.py:682
  337.1 27.9 %all-to-all-start.1 = ((bf16[16,64,256]{2,1,0:T(8,128)(2,1)}), bf16[16,64,256]{2,1,0:T(8,128)(2,1)S(1)}, u32[]{:S(2)}, u32[]{:S(2)}) async-start(bf16[16,64,256]{2,1,0:T(8,128)(2,1)} %bitcast.44), calls=%async_computation.2 | async-start | bytes 1048576 | tf_op jit(solution)/shard_map/all_to_all | solution.py:1348
  343.2 124.8 %reduce-scatter.8.cloned.1.call-start = ((), (), s32[]{:S(2)}) async-start(), calls=%async_computation.9 | async-start | bytes 3133440 | tf_op jit(solution)/shard_map/reduce_scatter | solution.py:1376
  351.0 53.8 %collective-permute-start.40 = (bf16[2,64,1024]{2,1,0:T(8,128)(2,1)}, bf16[2,64,1024]{2,1,0:T(8,128)(2,1)S(1)}, u32[]{:S(2)}, u32[]{:S(2)}) collective-permute-start(bf16[2,64,1024]{2,1,0:T(8,128)(2,1)} %get-tuple-element.174), channel_id=1, source_target_pairs={{0,4},{4,0},{8,12},{12,8},{1,5},{5,1},{9,13},{13,9},{2,6},{6,2},{1... | collective-permute-start | bytes 786440 | tf_op jit(solution)/shard_map/ppermute | solution.py:381
  355.4 49.4 %collective-permute-start.42 = (bf16[2,64,1024]{2,1,0:T(8,128)(2,1)S(1)}, bf16[2,64,1024]{2,1,0:T(8,128)(2,1)S(1)}, u32[]{:S(2)}, u32[]{:S(2)}) collective-permute-start(bf16[2,64,1024]{2,1,0:T(8,128)(2,1)S(1)} %add_convert_fusion.10), channel_id=1, source_target_pairs={{0,8},{4,12},{8,0},{12,4},{1,9},{5,13},{9,1},{13,5},{2,10},{6,14},... | collective-permute-start | bytes 786440 | tf_op jit(solution)/shard_map/ppermute | solution.py:381
  364.3 36.3 %collective-permute-start.37 = (bf16[2,272,1088]{2,1,0:T(8,128)(2,1)}, bf16[2,272,1088]{2,1,0:T(8,128)(2,1)S(1)}, u32[]{:S(2)}, u32[]{:S(2)}) collective-permute-start(bf16[2,272,1088]{2,1,0:T(8,128)(2,1)} %bitcast.132), channel_id=1, source_target_pairs={{0,16},{16,0},{1,17},{17,1},{2,18},{18,2},{3,19},{19,3},{4,20},{20... | collective-permute-start | bytes 3551240 | tf_op jit(solution)/shard_map/ppermute | solution.py:678
  400.5 12.2 %collective-permute-start.38 = (bf16[3,64,1024]{2,1,0:T(8,128)(2,1)}, bf16[3,64,1024]{2,1,0:T(8,128)(2,1)S(1)}, u32[]{:S(2)}, u32[]{:S(2)}) collective-permute-start(bf16[3,64,1024]{2,1,0:T(8,128)(2,1)} %get-tuple-element.168), channel_id=1, source_target_pairs={{0,8},{4,12},{8,0},{12,4},{1,9},{5,13},{9,1},{13,5},{2,10},{6,14},... | collective-permute-start | bytes 1179656 | tf_op jit(solution)/shard_map/ppermute | solution.py:381
  400.6 19.6 %collective-permute-start.39 = (bf16[3,64,1024]{2,1,0:T(8,128)(2,1)}, bf16[3,64,1024]{2,1,0:T(8,128)(2,1)S(1)}, u32[]{:S(2)}, u32[]{:S(2)}) collective-permute-start(bf16[3,64,1024]{2,1,0:T(8,128)(2,1)} %get-tuple-element.169), channel_id=1, source_target_pairs={{0,12},{4,8},{8,4},{12,0},{1,13},{5,9},{9,5},{13,1},{2,14},{6,10},... | collective-permute-start | bytes 1179656 | tf_op jit(solution)/shard_map/ppermute | solution.py:381
  426.1 18.6 %collective-permute-start.43 = (bf16[1088,256]{1,0:T(8,128)(2,1)S(1)}, bf16[1088,256]{1,0:T(8,128)(2,1)S(1)}, u32[]{:S(2)}, u32[]{:S(2)}) collective-permute-start(bf16[1088,256]{1,0:T(8,128)(2,1)S(1)} %convolution_convert_fusion.5.refs_4_), channel_id=1, source_target_pairs={{0,1},{3,2},{4,5},{7,6},{8,9},{11,10},{12,13},{15,14},{16,17},{19,... | collective-permute-start | bytes 1671176 | tf_op jit(solution)/shard_map/ppermute | solution.py:682
  441.4 24.0 %collective-permute-start.60 = (bf16[272,960]{1,0:T(8,128)(2,1)}, bf16[272,960]{1,0:T(8,128)(2,1)S(1)}, u32[]{:S(2)}, u32[]{:S(2)}) collective-permute-start(bf16[272,960]{1,0:T(8,128)(2,1)} %get-tuple-element.195), channel_id=1, source_target_pairs={{0,4},{4,0},{8,12},{12,8},{1,5},{5,1},{9,13},{13,9},{2,6},{6,2},{1... | collective-permute-start | bytes 1566728 | tf_op jit(solution)/shard_map/ppermute | solution.py:381
  443.8 21.6 %collective-permute-start.61 = (bf16[272,960]{1,0:T(8,128)(2,1)S(1)}, bf16[272,960]{1,0:T(8,128)(2,1)S(1)}, u32[]{:S(2)}, u32[]{:S(2)}) collective-permute-start(bf16[272,960]{1,0:T(8,128)(2,1)S(1)} %add_convert_fusion.6.refs_4_), channel_id=1, source_target_pairs={{0,8},{4,12},{8,0},{12,4},{1,9},{5,13},{9,1},{13,5},{2,10},{6,14},... | collective-permute-start | bytes 1566728 | tf_op jit(solution)/shard_map/ppermute | solution.py:381
  447.4 16.3 %collective-permute-start.48 = (bf16[1088,256]{1,0:T(8,128)(2,1)}, bf16[1088,256]{1,0:T(8,128)(2,1)S(1)}, u32[]{:S(2)}, u32[]{:S(2)}) collective-permute-start(bf16[1088,256]{1,0:T(8,128)(2,1)} %add_convert_fusion.4), channel_id=1, source_target_pairs={{1,2},{2,1},{5,6},{6,5},{9,10},{10,9},{13,14},{14,13},{17,18},{18,... | collective-permute-start | bytes 1671176 | tf_op jit(solution)/shard_map/ppermute | solution.py:682
  448.1 15.6 %collective-permute-start.49 = (bf16[1088,256]{1,0:T(8,128)(2,1)}, bf16[1088,256]{1,0:T(8,128)(2,1)S(1)}, u32[]{:S(2)}, u32[]{:S(2)}) collective-permute-start(bf16[1088,256]{1,0:T(8,128)(2,1)} %shard_map.309), channel_id=1, source_target_pairs={{0,1},{3,2},{4,5},{7,6},{8,9},{11,10},{12,13},{15,14},{16,17},{19,... | collective-permute-start | bytes 1671176 | tf_op jit(solution)/shard_map/ppermute | solution.py:682
  469.3 14.7 %collective-permute-start.62 = (bf16[136,2048]{1,0:T(8,128)(2,1)S(1)}, bf16[136,2048]{1,0:T(8,128)(2,1)S(1)}, u32[]{:S(2)}, u32[]{:S(2)}) collective-permute-start(bf16[136,2048]{1,0:T(8,128)(2,1)S(1)} %fusion.42), channel_id=1, source_target_pairs={{0,16},{16,0},{1,17},{17,1},{2,18},{18,2},{3,19},{19,3},{4,20},{20... | collective-permute-start | bytes 1671176 | tf_op jit(solution)/shard_map/ppermute | solution.py:678
  472.5 20.4 %collective-permute-start.50 = (bf16[1088,256]{1,0:T(8,128)(2,1)S(1)}, bf16[1088,256]{1,0:T(8,128)(2,1)S(1)}, u32[]{:S(2)}, u32[]{:S(2)}) collective-permute-start(bf16[1088,256]{1,0:T(8,128)(2,1)S(1)} %add_convert_fusion.3), channel_id=1, source_target_pairs={{0,1},{1,0},{2,3},{3,2},{4,5},{5,4},{6,7},{7,6},{8,9},{9,8},{10,11... | collective-permute-start | bytes 1671176 | tf_op jit(solution)/shard_map/ppermute | solution.py:682
  475.1 17.8 %collective-permute-start.51 = (bf16[1088,256]{1,0:T(8,128)(2,1)S(1)}, bf16[1088,256]{1,0:T(8,128)(2,1)S(1)}, u32[]{:S(2)}, u32[]{:S(2)}) collective-permute-start(bf16[1088,256]{1,0:T(8,128)(2,1)S(1)} %add_convert_fusion.2), channel_id=1, source_target_pairs={{1,2},{2,1},{5,6},{6,5},{9,10},{10,9},{13,14},{14,13},{17,18},{18,... | collective-permute-start | bytes 1671176 | tf_op jit(solution)/shard_map/ppermute | solution.py:682
  486.6 21.0 %collective-permute-start.63 = (bf16[136,592]{1,0:T(8,128)(2,1)}, bf16[136,592]{1,0:T(8,128)(2,1)}, u32[]{:S(2)}, u32[]{:S(2)}) collective-permute-start(bf16[136,592]{1,0:T(8,128)(2,1)} %pad_maximum_fusion.10), channel_id=1, source_target_pairs={{0,1},{1,0},{2,3},{3,2},{4,5},{5,4},{6,7},{7,6},{8,9},{9,8},{10,11... | collective-permute-start | bytes 483080 | tf_op jit(solution)/shard_map/ppermute | solution.py:682
  489.8 18.8 %collective-permute-start.64 = (bf16[136,592]{1,0:T(8,128)(2,1)}, bf16[136,592]{1,0:T(8,128)(2,1)S(1)}, u32[]{:S(2)}, u32[]{:S(2)}) collective-permute-start(bf16[136,592]{1,0:T(8,128)(2,1)} %pad_maximum_fusion.11), channel_id=1, source_target_pairs={{0,2},{1,3},{2,0},{3,1},{4,6},{5,7},{6,4},{7,5},{8,10},{9,11},{10,... | collective-permute-start | bytes 483080 | tf_op jit(solution)/shard_map/ppermute | solution.py:682
  491.3 17.9 %collective-permute-start.65 = (bf16[136,592]{1,0:T(8,128)(2,1)}, bf16[136,592]{1,0:T(8,128)(2,1)}, u32[]{:S(2)}, u32[]{:S(2)}) collective-permute-start(bf16[136,592]{1,0:T(8,128)(2,1)} %pad_maximum_fusion.12), channel_id=1, source_target_pairs={{0,3},{1,2},{2,1},{3,0},{4,7},{5,6},{6,5},{7,4},{8,11},{9,10},{10,... | collective-permute-start | bytes 483080 | tf_op jit(solution)/shard_map/ppermute | solution.py:682
  504.2 18.1 %collective-permute-start.47 = (bf16[272,256]{1,0:T(8,128)(2,1)}, bf16[272,256]{1,0:T(8,128)(2,1)S(1)}, u32[]{:S(2)}, u32[]{:S(2)}) collective-permute-start(bf16[272,256]{1,0:T(8,128)(2,1)} %get-tuple-element.269), channel_id=1, source_target_pairs={{0,12},{4,8},{8,4},{12,0},{1,13},{5,9},{9,5},{13,1},{2,14},{6,10},... | collective-permute-start | bytes 417800 | tf_op jit(solution)/shard_map/ppermute | solution.py:381
  506.6 15.8 %collective-permute-start.46 = (bf16[272,256]{1,0:T(8,128)(2,1)}, bf16[272,256]{1,0:T(8,128)(2,1)S(1)}, u32[]{:S(2)}, u32[]{:S(2)}) collective-permute-start(bf16[272,256]{1,0:T(8,128)(2,1)} %get-tuple-element.270), channel_id=1, source_target_pairs={{0,8},{4,12},{8,0},{12,4},{1,9},{5,13},{9,1},{13,5},{2,10},{6,14},... | collective-permute-start | bytes 417800 | tf_op jit(solution)/shard_map/ppermute | solution.py:381
  507.6 16.7 %collective-permute-start.45 = (bf16[272,256]{1,0:T(8,128)(2,1)}, bf16[272,256]{1,0:T(8,128)(2,1)S(1)}, u32[]{:S(2)}, u32[]{:S(2)}) collective-permute-start(bf16[272,256]{1,0:T(8,128)(2,1)} %get-tuple-element.271), channel_id=1, source_target_pairs={{0,4},{4,0},{8,12},{12,8},{1,5},{5,1},{9,13},{13,9},{2,6},{6,2},{1... | collective-permute-start | bytes 417800 | tf_op jit(solution)/shard_map/ppermute | solution.py:381
  508.6 19.6 %collective-permute-start.52 = (bf16[272,256]{1,0:T(8,128)(2,1)}, bf16[272,256]{1,0:T(8,128)(2,1)}, u32[]{:S(2)}, u32[]{:S(2)}) collective-permute-start(bf16[272,256]{1,0:T(8,128)(2,1)} %get-tuple-element.189), channel_id=1, source_target_pairs={{0,4},{4,0},{8,12},{12,8},{1,5},{5,1},{9,13},{13,9},{2,6},{6,2},{1... | collective-permute-start | bytes 417800 | tf_op jit(solution)/shard_map/ppermute | solution.py:381
  522.5 13.9 %collective-permute-start.66 = (bf16[136,1088]{1,0:T(8,128)(2,1)}, bf16[136,1088]{1,0:T(8,128)(2,1)}, u32[]{:S(2)}, u32[]{:S(2)}) collective-permute-start(bf16[136,1088]{1,0:T(8,128)(2,1)} %pad_maximum_fusion.8), channel_id=1, source_target_pairs={{0,16},{16,0},{1,17},{17,1},{2,18},{18,2},{3,19},{19,3},{4,20},{20... | collective-permute-start | bytes 887816 | tf_op jit(solution)/shard_map/ppermute | solution.py:678
  524.3 10.0 %collective-permute-start.59 = (f32[8,1768]{1,0:T(8,128)S(1)}, f32[8,1768]{1,0:T(8,128)S(1)}, u32[]{:S(2)}, u32[]{:S(2)}) collective-permute-start(f32[8,1768]{1,0:T(8,128)S(1)} %add.258), channel_id=1, source_target_pairs={{0,16},{16,0},{1,17},{17,1},{2,18},{18,2},{3,19},{19,3},{4,20},{20... | collective-permute-start | bytes 169736 | tf_op jit(solution)/shard_map/ppermute | solution.py:678
  (146 other events, 866.2 us)
Sparse Core Ops, SparseCore 0:
  9.7 36.5 all-gather.6
  47.8 30.8 all-gather.8
  80.9 36.9 all-gather.10
  142.2 56.2 all-gather.12
  305.8 58.4 reduce-scatter.5
  366.6 43.7 reduce-scatter.3
  413.1 33.3 reduce-scatter.7
